TPU v7x, 32 devices: a whole 2x2x4 slice. The times are simulated.
32 devices in a mesh: comp: 2 (over core), tile: 16 (over z, y, x).
Axes of the slice: x: 2, y: 2, z: 4, core: 2. Of those that a mesh axis runs over, the one named last changes fastest.
Arguments:
- fields: float32 [2, 8, 131072], P('comp', None, 'tile'), may hold values from -6 to 6
- level_rate: float32 [2, 8], P('comp'), may hold values from 0.1 to 0.9
- edge_weight: float32 [2, 3, 131072], P('comp', None, 'tile'), may hold values from 0.5 to 2
- fine_diagonal: float32 [2, 131072], P('comp', 'tile'), may hold values from 0.1 to 1
- fine_table: int32 [2, 3, 131072], P('comp', None, 'tile'), may hold values from 0 to 8447, as said below
- old_height: float32 [2, 131072], P('comp', 'tile'), may hold values from -6 to 6
- level_weight: float32 [2, 8], P('comp'), may hold values from 0.1 to 0.6
- flux_weight: float32 [2, 4], P('comp'), may hold values from 0.2 to 1
- fine_owner: int32 [2, 131072], P('comp', 'tile'), may hold values from 0 to 1023, as said below
- coarse_table: int32 [2, 3, 16384], P('comp', None, 'tile'), may hold values from 0 to 1055, as said below
- coarse_edge: float32 [2, 3, 16384], P('comp', None, 'tile'), may hold values from 2 to 8
- coarse_diagonal: float32 [2, 16384], P('comp', 'tile'), may hold values from 0.5 to 5
- coarse_owner: int32 [2, 16384], P('comp', 'tile'), may hold values from 0 to 15, as said below
- coarse_inverse: float32 [2, 256, 256], P('comp', 'tile'), may hold values from -0.05 to 0.05, as said below
- surface_out: bfloat16 [2, 4, 131072], P('comp', None, 'tile'), may hold values from -6 to 6
- send_blocks: int32 [2, 16, 160], P('comp', 'tile'), may hold values from 0 to 64, as said below
- entry_slot: int32 [2, 16, 160], P('comp', 'tile'), may hold values from 0 to 159, as said below
- entry_block: int32 [2, 16, 160], P('comp', 'tile'), may hold values from 0 to 63, as said below
- remap_tiles: bfloat16 [2, 16, 160, 128, 128], P('comp', 'tile'), may hold values from 0 to 0.17675781
Outputs:
- new_fields: float32 [2, 8, 131072], P('comp', None, 'tile')
- received: float32 [2, 4, 131072], P('comp', None, 'tile')
- height: float32 [2, 131072], P('comp', 'tile')
Inputs may be any that keep to these rules, and one draw needn't show every extreme that they name: A position in the cells of the cell's own device, extended by 128 cells on each side (the loop of tiles closes), lying within 128 cells of the cell itself: fine_table[g, k, c] - 128 - (c mod 8192) is between -128 and 128. A position in the first-level cells of the cell's own device, extended by 16 cells on each side (the loop of tiles closes), lying within 16 cells of the cell itself: coarse_table[g, k, a] - 16 - (a mod 1024) is between -16 and 16. `fine_owner`: nondecreasing within each device's cells; every aggregate of a device owns at least one cell. `coarse_owner`: nondecreasing within each device's first-level cells; every aggregate owns at least one cell. `coarse_inverse`: exactly symmetric. `send_blocks`: for each offset j, the used slots come first and at least one is used; 64 marks an unused slot; on some offset of every device all 32 slots are used. `entry_slot`: names a used slot of the receiving device; every used slot is named by some entry. `entry_block`: nondecreasing along the entries of a device; every block is named.
All inputs are finite; a program needn't handle non-finite values.
Results may differ from a plain program's by a relative error of at most 0.0003.
Values may be sent and summed in bfloat16 or wider, within the bound.
No kernel may reach another device: no remote copies, remote signals or barrier semaphores. Data moves between devices by JAX's collectives and lax.ppermute only.
A program may use at most 128 MiB of HBM per device.

v0:
```python
import math

import jax
import jax.numpy as jnp
from jax import lax
from jax.sharding import PartitionSpec as P

HALO = 128
AGG0 = 8


RELAXATION = 0.8


def extended(cells, sides, width):
    for axis, dim in sides:
        count = lax.axis_size(axis)
        head = lax.slice_in_dim(cells, 0, width, axis=dim)
        tail = lax.slice_in_dim(cells, cells.shape[dim] - width, cells.shape[dim], axis=dim)
        cells = jnp.concatenate(
            [
                lax.ppermute(tail, axis, [(i, (i + 1) % count) for i in range(count)]),
                cells,
                lax.ppermute(head, axis, [((i + 1) % count, i) for i in range(count)]),
            ],
            axis=dim,
        )
    return cells


def window_blocks(padded, reach):
    length = padded.shape[-1] - 2 * reach
    leading = padded.shape[:-1]
    parts = [
        padded[..., step * reach : step * reach + length].reshape(
            leading + (length // reach, reach)
        )
        for step in range(3)
    ]
    return jnp.concatenate(parts, axis=-1)


def coupling_matrix(index_table, weights, reach):
    length = index_table.shape[-1]
    block_start = jnp.arange(length, dtype=jnp.int32) // reach * reach
    relative = (index_table - block_start[None, :]).reshape(3, length // reach, reach)
    scaled = weights.reshape(3, length // reach, reach)
    columns = jnp.arange(3 * reach, dtype=jnp.int32)
    matrix = jnp.zeros((length // reach, reach, 3 * reach), jnp.float32)
    for link in range(3):
        matrix = matrix + jnp.where(
            relative[link][:, :, None] == columns, scaled[link][:, :, None], 0.0
        )
    return matrix


def neighbour_sum(padded, matrix, reach):
    windows = window_blocks(padded, reach)
    result = jnp.einsum(
        "...bj,bij->...bi",
        windows,
        matrix,
        precision=lax.Precision.HIGHEST,
        preferred_element_type=jnp.float32,
    )
    return result.reshape(result.shape[:-2] + (result.shape[-2] * result.shape[-1],))


def owner_sum(values, owner, count):
    block = math.gcd(values.shape[0], 1024)
    identity = jnp.arange(count, dtype=jnp.int32)

    def part(pair):
        piece, owner_piece = pair
        onehot = (owner_piece[:, None] == identity[None, :]).astype(jnp.float32)
        return jnp.dot(piece, onehot, precision=lax.Precision.HIGHEST)

    return jnp.sum(lax.map(part, (values.reshape(-1, block), owner.reshape(-1, block))), axis=0)


def owner_expand(values, owner):
    block = math.gcd(owner.shape[0], 1024)
    identity = jnp.arange(values.shape[0], dtype=jnp.int32)

    def part(owner_piece):
        onehot = (owner_piece[:, None] == identity[None, :]).astype(jnp.float32)
        return jnp.dot(onehot, values, precision=lax.Precision.HIGHEST)

    return lax.map(part, owner.reshape(-1, block)).reshape(-1)


def fine_apply(values, matrix, diagonal):
    padded = extended(values, (("tile", 0),), HALO)
    return diagonal * values - neighbour_sum(padded, matrix, HALO)


def coarse_apply(values, matrix, diagonal):
    padded = extended(values, (("tile", 0),), HALO // AGG0)
    return diagonal * values - neighbour_sum(padded, matrix, HALO // AGG0)


def per_device(
    fields,
    level_rate,
    edge_weight,
    fine_diagonal,
    fine_table,
    old_height,
    level_weight,
    flux_weight,
    fine_owner,
    coarse_table,
    coarse_edge,
    coarse_diagonal,
    coarse_owner,
    coarse_inverse,
    surface_out,
    send_blocks,
    entry_slot,
    entry_block,
    remap_tiles,
):
    group_index = lax.axis_index("comp")
    tile_index = lax.axis_index("tile")
    tile_count = lax.axis_size("tile")
    link_weights = edge_weight[0]
    weight_sum = jnp.sum(link_weights, axis=0)
    fine_total = fine_diagonal[0] + weight_sum
    fine_matrix = coupling_matrix(fine_table[0], link_weights, HALO)
    levels = fields.shape[1]
    current = fields[0]
    stacked = jnp.concatenate([current, old_height], axis=0)
    padded = extended(stacked, (("tile", 1),), HALO)
    beside_all = neighbour_sum(padded, fine_matrix, HALO)
    advanced = (
        current + level_rate[0][:, None] * (beside_all[:levels] - weight_sum * current) / weight_sum
    )
    channels = surface_out.shape[1]
    cell_count = surface_out.shape[2]
    block_width = remap_tiles.shape[-1]
    block_count = cell_count // block_width
    source_blocks = (
        surface_out[0]
        .reshape(channels, block_count, block_width)
        .transpose(1, 0, 2)
        .reshape(block_count, channels * block_width)
    )
    send_hot = (
        send_blocks[0, 0][:, None] == jnp.arange(block_count, dtype=jnp.int32)[None, :]
    ).astype(jnp.bfloat16)
    outgoing = jnp.dot(send_hot, source_blocks, preferred_element_type=jnp.float32).astype(
        jnp.bfloat16
    )
    outgoing = outgoing.reshape(5, -1, channels, block_width)
    slot_count = outgoing.shape[1]
    target_offset = (tile_index + 2 - jnp.arange(tile_count, dtype=jnp.int32)) % tile_count
    usable = (target_offset < 5).astype(outgoing.dtype)
    chosen = outgoing[jnp.minimum(target_offset, 4)] * usable[:, None, None, None]
    blank_rows = jnp.zeros_like(chosen)
    dense_buffer = jnp.where(
        group_index == 0,
        jnp.concatenate([blank_rows, chosen], axis=0),
        jnp.concatenate([chosen, blank_rows], axis=0),
    )
    arrived = lax.all_to_all(
        dense_buffer, ("comp", "tile"), split_axis=0, concat_axis=0, tiled=True
    )
    source_rows = (1 - group_index) * tile_count + (
        tile_index + jnp.arange(5, dtype=jnp.int32) - 2
    ) % tile_count
    incoming = arrived[source_rows]
    incoming = incoming.reshape(5 * slot_count, channels * block_width)
    slot_hot = (
        entry_slot[0, 0][:, None] == jnp.arange(5 * slot_count, dtype=jnp.int32)[None, :]
    ).astype(jnp.bfloat16)
    picked = jnp.dot(slot_hot, incoming, preferred_element_type=jnp.float32).astype(jnp.bfloat16)
    picked = picked.reshape(-1, channels, block_width)
    products = jnp.einsum(
        "efs,eds->efd", picked, remap_tiles[0, 0], preferred_element_type=jnp.float32
    )
    membership = (
        entry_block[0, 0][None, :] == jnp.arange(block_count, dtype=jnp.int32)[:, None]
    ).astype(jnp.float32)
    summed = jnp.dot(
        membership,
        products.reshape(products.shape[0], channels * block_width),
        precision=lax.Precision.HIGHEST,
    )
    received = (
        summed.reshape(block_count, channels, block_width)
        .transpose(1, 0, 2)
        .reshape(channels, cell_count)
    )
    forcing = jnp.sum(level_weight[0][:, None] * advanced, axis=0) + jnp.sum(
        flux_weight[0][:, None] * received, axis=0
    )
    previous = old_height[0]
    smoothed = (
        previous
        + RELAXATION * (forcing - (fine_total * previous - beside_all[levels])) / fine_total
    )
    fine_residual = forcing - fine_apply(smoothed, fine_matrix, fine_total)
    first_level = coarse_diagonal.shape[1]
    coarse_source = owner_sum(fine_residual, fine_owner[0], first_level)
    coarse_weights = coarse_edge[0]
    coarse_matrix = coupling_matrix(coarse_table[0], coarse_weights, HALO // AGG0)
    coarse_total = coarse_diagonal[0] + jnp.sum(coarse_weights, axis=0)
    coarse_first = RELAXATION * coarse_source / coarse_total
    coarse_residual = coarse_source - coarse_apply(coarse_first, coarse_matrix, coarse_total)
    bottom_count = coarse_inverse.shape[1]
    bottom_source = owner_sum(coarse_residual, coarse_owner[0], bottom_count)
    inverse_rows = coarse_inverse[0]
    bottom_value = lax.psum_scatter(
        jnp.dot(bottom_source, inverse_rows, precision=lax.Precision.HIGHEST),
        "tile",
        scatter_dimension=0,
        tiled=True,
    )
    coarse_second = coarse_first + owner_expand(bottom_value, coarse_owner[0])
    coarse_third = (
        coarse_second
        + RELAXATION
        * (coarse_source - coarse_apply(coarse_second, coarse_matrix, coarse_total))
        / coarse_total
    )
    corrected = smoothed + owner_expand(coarse_third, fine_owner[0])
    height = (
        corrected
        + RELAXATION * (forcing - fine_apply(corrected, fine_matrix, fine_total)) / fine_total
    )
    return (advanced[None], received[None], height[None])


def solution(mesh):
    in_specs = (
        P("comp", None, "tile"),
        P("comp", None),
        P("comp", None, "tile"),
        P("comp", "tile"),
        P("comp", None, "tile"),
        P("comp", "tile"),
        P("comp", None),
        P("comp", None),
        P("comp", "tile"),
        P("comp", None, "tile"),
        P("comp", None, "tile"),
        P("comp", "tile"),
        P("comp", "tile"),
        P("comp", "tile", None),
        P("comp", None, "tile"),
        P("comp", "tile", None),
        P("comp", "tile", None),
        P("comp", "tile", None),
        P("comp", "tile", None, None, None),
    )
    out_specs = (P("comp", None, "tile"), P("comp", None, "tile"), P("comp", "tile"))
    return jax.shard_map(
        per_device, mesh=mesh, in_specs=in_specs, out_specs=out_specs, check_vma=False
    )
```

profile of v0, /device:TPU:0, one launch (start us, length us, event | category | flops | bytes accessed | tf_op | source)
XLA Modules:
  0.0 214.3 jit_solution(2129237051377071559)
XLA Ops:
  0.6 0.7 pad_maximum_fusion.11
  1.4 2.9 %collective-permute-start = (f32[9,128]{1,0:T(8,128)S(1)}, f32[9,128]{1,0:T(8,128)S(1)}, u32[]{:S(2)}, u32[]{:S(2)}) collective-permute-start(f32[9,128]{1,0:T(8,128)S(1)} %get-tuple-element.137), channel_id=1, source_target_pairs={{0,1},{1,2},{2,3},{3,4},{4,5},{5,6},{6,7},{7,8},{8,9},{9,10},{10,1... | collective-permute-start | bytes 13832 | tf_op jit(solution)/shard_map/ppermute | solution.py:22
  4.3 4.0 %collective-permute-start.1 = (f32[9,128]{1,0:T(8,128)S(1)}, f32[9,128]{1,0:T(8,128)S(1)}, u32[]{:S(2)}, u32[]{:S(2)}) collective-permute-start(f32[9,128]{1,0:T(8,128)S(1)} %get-tuple-element.138), channel_id=1, source_target_pairs={{1,0},{2,1},{3,2},{4,3},{5,4},{6,5},{7,6},{8,7},{9,8},{10,9},{11,1... | collective-permute-start | bytes 13832 | tf_op jit(solution)/shard_map/ppermute | solution.py:24
  8.4 1.1 convolution_convert_fusion.1
  9.6 1.0 gather_fusion
  10.9 1.7 pad_select_fusion
  12.6 2.6 %all-to-all-start = ((bf16[32,32,4,128]{3,2,1,0:T(4,128)(2,1)}), bf16[32,32,4,128]{3,2,1,0:T(4,128)(2,1)S(1)}, u32[]{:S(2)}, u32[]{:S(2)}) async-start(bf16[32,32,4,128]{3,2,1,0:T(4,128)(2,1)} %pad_select_fusion), calls=%async_computation | async-start | bytes 2097152 | tf_op jit(solution)/shard_map/all_to_all | solution.py:165
  15.3 1.0 bitcast_subtract_fusion.2
  16.4 0.8 fusion.134
  17.3 8.9 %select_add_fusion.28 = f32[64,128,384]{2,1,0:T(8,128)} fusion(f32[64,128]{1,0:T(8,128)S(1)} %bitcast.258, s32[64,128]{1,0:T(8,128)S(1)} %bitcast.246, f32[64,128]{1,0:T(8,128)S(1)} %bitcast.255, s32[64,128]{1,0:T(8,128)S(1)} %bitcast.249, f32[64,128]{1,0:T(8,128)S(1)} %bitcast.252, s32[64,128]{1,0:T(8,128)S(1)} %bitcast.243), kind=kLoop, calls=%fused_computation.15.clone.1.clone.1 | loop fusion | flops 25165824 | bytes 12779520 | tf_op jit(solution)/shard_map/...bj,bij->...bi/dot_general | solution.py:59
  26.1 8.7 %select_add_fusion.29 = f32[64,128,384]{2,1,0:T(8,128)} fusion(f32[64,128]{1,0:T(8,128)S(1)} %bitcast.259, s32[64,128]{1,0:T(8,128)S(1)} %bitcast.247, f32[64,128]{1,0:T(8,128)S(1)} %bitcast.256, s32[64,128]{1,0:T(8,128)S(1)} %bitcast.250, f32[64,128]{1,0:T(8,128)S(1)} %bitcast.253, ...), kind=kLoop, calls=%fused_computation.15.clone.clone.clone.clone.clone.clone.clone.clone.clone.clone... | loop fusion | flops 25165824 | bytes 12779520 | tf_op jit(solution)/shard_map/...bj,bij->...bi/dot_general | solution.py:59
  35.7 0.7 reduce.44
  36.4 0.7 reduce.45
  37.8 0.8 reduce.43
  42.1 24.2 %fusion.50 = f32[9,64,128]{2,0,1:T(8,128)S(1)} fusion(f32[64,128]{1,0:T(8,128)S(1)} %bitcast.260, s32[64,128]{1,0:T(8,128)S(1)} %bitcast.248, f32[64,128]{1,0:T(8,128)S(1)} %bitcast.257, s32[64,128]{1,0:T(8,128)S(1)} %bitcast.251, f32[64,128]{1,0:T(8,128)S(1)} %bitcast.254, s32[64,128]{1,0:T(8,128)S(1)} %bitcast.245, f32[9,64,384]{2,0,1:T(8,128)S(1)} %fusion.152), kind=kOutput, calls=%fused_computation.58 | convolution fusion | flops 364904448 | bytes 1376256 | tf_op jit(solution)/shard_map/...bj,bij->...bi/dot_general | solution.py:59
  67.7 5.3 %fusion.41 = f32[160,4,128]{2,1,0:T(4,128)S(1)} fusion(bf16[160,4,128]{2,1,0:T(4,128)(2,1)S(1)} %reshape.428, bf16[1,1,160,128,128]{4,3,2,1,0:T(8,128)(2,1)} %param.41), kind=kOutput, calls=%fused_computation.49 | convolution fusion | flops 20971520 | bytes 5734400 | tf_op jit(solution)/shard_map/efs,eds->efd/dot_general | solution.py:178
  73.3 1.7 collective-permute-start.2
  75.0 4.1 %collective-permute-start.3 = (f32[128]{0:T(128)S(1)}, f32[128]{0:T(128)S(1)}, u32[]{:S(2)}, u32[]{:S(2)}) collective-permute-start(f32[128]{0:T(128)S(1)} %get-tuple-element.152), channel_id=1, source_target_pairs={{1,0},{2,1},{3,2},{4,3},{5,4},{6,5},{7,6},{8,7},{9,8},{10,9},{11,1... | collective-permute-start | bytes 1544 | tf_op jit(solution)/shard_map/ppermute | solution.py:24
  79.1 1.4 collective-permute-done.2
  80.5 16.2 %fusion.12 = f32[64,1,128]{2,1,0:T(1,128)S(1)} fusion(f32[64,384,1]{1,0,2:T(8,128)S(1)} %maximum_bitcast_fusion, f32[64,128,384]{2,1,0:T(8,128)} %select_add_fusion.28), kind=kOutput, calls=%fused_computation.20 | convolution fusion | flops 37748736 | bytes 12713984 | tf_op jit(solution)/shard_map/...bj,bij->...bi/dot_general | solution.py:59
  96.8 12.7 %while.6 = (s32[]{:T(128)}, f32[8,1024]{1,0:T(8,128)S(1)}, f32[8,1024]{1,0:T(8,128)S(1)}, s32[8,1024]{1,0:T(8,128)S(1)}, s32[]{:T(128)}, /*index=5*/s32[]{:T(128)}) while((s32[]{:T(128)}, f32[8,1024]{1,0:T(8,128)S(1)}, f32[8,1024]{1,0:T(8,128)S(1)}, s32[8,1024]{1,0:T(8,128)S(1)}, s32[]{:T(128)}, /*index=5*/s32[]{:T(128)}) %tuple.67), condition=%wide.region_4.5_spmd.clone, body=%wide.region_3.4_spmd.clone.sunk | while | flops 13631490 | bytes 28753 | solution.py:78
  96.8 1.5 fusion.159
  98.4 1.5 fusion.159
  100.0 1.5 fusion.159
  101.6 1.5 fusion.159
  103.2 1.5 fusion.159
  104.7 1.5 fusion.159
  106.3 1.5 fusion.159
  107.9 1.5 fusion.159
  110.1 5.3 %collective-permute-start.5 = (f32[16]{0:T(128)S(1)}, f32[16]{0:T(128)S(1)}, u32[]{:S(2)}, u32[]{:S(2)}) collective-permute-start(f32[16]{0:T(128)S(1)} %get-tuple-element.160), channel_id=1, source_target_pairs={{1,0},{2,1},{3,2},{4,3},{5,4},{6,5},{7,6},{8,7},{9,8},{10,9},{11,1... | collective-permute-start | bytes 200 | tf_op jit(solution)/shard_map/ppermute | solution.py:24
  115.4 1.4 collective-permute-done.4
  117.2 2.3 %fusion.55 = f32[64,1,16]{2,1,0:T(1,128)S(1)} fusion(f32[64,48,1]{1,2,0:T(1,128)S(1)} %bitcast.274, f32[64,16]{1,0:T(8,128)S(1)} %broadcast_in_dim.117, s32[64,16]{1,0:T(8,128)S(1)} %eq.245, f32[64,16]{1,0:T(8,128)S(1)} %broadcast_in_dim.115, s32[64,16]{1,0:T(8,128)S(1)} %eq.241, f32[64,16]{1,0:T(8,128)S(1)} %broadcast_in_dim.112, s32[64,16]{1,0:T(8,128)S(1)} %eq.237), kind=kOutput, calls=%fused_computation.75 | convolution fusion | flops 983040 | bytes 40960 | tf_op jit(solution)/shard_map/...bj,bij->...bi/dot_general | solution.py:59
  120.1 42.2 %all-reduce.2 = f32[256]{0:T(256)S(1)} all-reduce(f32[256]{0:T(256)S(1)} %bitcast.277), channel_id=2, replica_groups=mesh['comp'=2,'tile'=16] {'tile'}, use_global_device_ids=true, to_apply=%region_7.8.clone | all-reduce | flops 256 | bytes 2048
  163.0 5.6 %collective-permute-start.7 = (f32[16]{0:T(128)S(1)}, f32[16]{0:T(128)S(1)}, u32[]{:S(2)}, u32[]{:S(2)}) collective-permute-start(f32[16]{0:T(128)S(1)} %get-tuple-element.156), channel_id=1, source_target_pairs={{1,0},{2,1},{3,2},{4,3},{5,4},{6,5},{7,6},{8,7},{9,8},{10,9},{11,1... | collective-permute-start | bytes 200 | tf_op jit(solution)/shard_map/ppermute | solution.py:24
  168.6 1.5 collective-permute-done.6
  170.4 2.3 %fusion.54 = f32[64,1,16]{2,1,0:T(1,128)S(1)} fusion(f32[64,48,1]{1,2,0:T(1,128)S(1)} %bitcast.273, f32[64,16]{1,0:T(8,128)S(1)} %broadcast_in_dim.117, s32[64,16]{1,0:T(8,128)S(1)} %eq.245, f32[64,16]{1,0:T(8,128)S(1)} %broadcast_in_dim.115, s32[64,16]{1,0:T(8,128)S(1)} %eq.241, f32[64,16]{1,0:T(8,128)S(1)} %broadcast_in_dim.112, s32[64,16]{1,0:T(8,128)S(1)} %eq.237), kind=kOutput, calls=%fused_computation.74 | convolution fusion | flops 983040 | bytes 40960 | tf_op jit(solution)/shard_map/...bj,bij->...bi/dot_general | solution.py:59
  172.8 17.0 %while.7 = (s32[]{:T(128)}, f32[8,1024]{1,0:T(8,128)S(1)}, s32[8,1024]{1,0:T(8,128)S(1)}, f32[1024]{0:T(1024)S(1)}, s32[]{:T(128)}, /*index=5*/s32[]{:T(128)}) while((s32[]{:T(128)}, f32[8,1024]{1,0:T(8,128)S(1)}, s32[8,1024]{1,0:T(8,128)S(1)}, f32[1024]{0:T(1024)S(1)}, s32[]{:T(128)}, /*index=5*/s32[]{:T(128)}) %tuple.73), condition=%wide.region_9.10_spmd.clone, body=%wide.region_8.9_spmd.clone.sunk | while | flops 13631490 | bytes 28749 | solution.py:89
  172.8 2.0 fusion.161
  175.0 2.0 fusion.161
  177.1 2.0 fusion.161
  179.2 2.0 fusion.161
  181.3 2.0 fusion.161
  183.5 2.0 fusion.161
  185.6 2.0 fusion.161
  187.7 2.0 fusion.161
  189.9 5.9 %collective-permute-start.9 = (f32[128]{0:T(128)S(1)}, f32[128]{0:T(128)S(1)}, u32[]{:S(2)}, u32[]{:S(2)}) collective-permute-start(f32[128]{0:T(128)S(1)} %get-tuple-element.148), channel_id=1, source_target_pairs={{1,0},{2,1},{3,2},{4,3},{5,4},{6,5},{7,6},{8,7},{9,8},{10,9},{11,1... | collective-permute-start | bytes 1544 | tf_op jit(solution)/shard_map/ppermute | solution.py:24
  195.8 0.8 fusion.64
  197.5 16.8 %fusion.19 = f32[1,8192]{1,0:T(1,128)} fusion(f32[64,384,1]{1,0,2:T(8,128)S(1)} %maximum_bitcast_fusion.1, f32[1,8192]{1,0:T(1,128)S(1)} %bitcast.263, f32[1,8192]{1,0:T(1,128)S(1)} %copy-done.2, f32[1,8192]{1,0:T(1,128)S(1)} %copy-done.3, f32[1,8192]{1,0:T(1,128)S(1)} %bitcast.232, f32[1,8192]{1,0:T(1,128)S(1)} %bitcast.236, f32[1,8192]{1,0:T(1,128)S(1)} %bitcast.237, ...), kind=kOutput, calls=%fused_computation.27 | convolution fusion | flops 37871616 | bytes 12943360 | tf_op jit(solution)/shard_map/...bj,bij->...bi/dot_general | solution.py:59
  (164 shorter events, 11.3 us)
Async XLA Ops:
  0.6 119.3 %copy-start = (f32[1,16,256]{2,1,0:T(8,128)S(1)}, f32[1,16,256]{2,1,0:T(8,128)}, u32[]{:S(2)}) copy-start(f32[1,16,256]{2,1,0:T(8,128)} %param.36) | copy-start | bytes 49156
  1.4 39.7 %collective-permute-start = (f32[9,128]{1,0:T(8,128)S(1)}, f32[9,128]{1,0:T(8,128)S(1)}, u32[]{:S(2)}, u32[]{:S(2)}) collective-permute-start(f32[9,128]{1,0:T(8,128)S(1)} %get-tuple-element.137), channel_id=1, source_target_pairs={{0,1},{1,2},{2,3},{3,4},{4,5},{5,6},{6,7},{7,8},{8,9},{9,10},{10,1... | collective-permute-start | bytes 13832 | tf_op jit(solution)/shard_map/ppermute | solution.py:22
  4.3 36.8 %collective-permute-start.1 = (f32[9,128]{1,0:T(8,128)S(1)}, f32[9,128]{1,0:T(8,128)S(1)}, u32[]{:S(2)}, u32[]{:S(2)}) collective-permute-start(f32[9,128]{1,0:T(8,128)S(1)} %get-tuple-element.138), channel_id=1, source_target_pairs={{1,0},{2,1},{3,2},{4,3},{5,4},{6,5},{7,6},{8,7},{9,8},{10,9},{11,1... | collective-permute-start | bytes 13832 | tf_op jit(solution)/shard_map/ppermute | solution.py:24
  12.6 54.1 %all-to-all-start = ((bf16[32,32,4,128]{3,2,1,0:T(4,128)(2,1)}), bf16[32,32,4,128]{3,2,1,0:T(4,128)(2,1)S(1)}, u32[]{:S(2)}, u32[]{:S(2)}) async-start(bf16[32,32,4,128]{3,2,1,0:T(4,128)(2,1)} %pad_select_fusion), calls=%async_computation | async-start | bytes 2097152 | tf_op jit(solution)/shard_map/all_to_all | solution.py:165
  17.2 17.7 %copy-start.8 = (s32[1,3,1024]{2,0,1:T(1,128)S(1)}, s32[1,3,1024]{2,0,1:T(1,128)}, u32[]{:S(2)}) copy-start(s32[1,3,1024]{2,0,1:T(1,128)} %param.32) | copy-start | bytes 36868
  17.2 17.8 %copy-start.5 = (f32[1,3,1024]{2,0,1:T(1,128)S(1)}, f32[1,3,1024]{2,0,1:T(1,128)}, u32[]{:S(2)}) copy-start(f32[1,3,1024]{2,0,1:T(1,128)} %param.33) | copy-start | bytes 36868
  17.2 17.8 %copy-start.4 = (f32[1,3,8192]{2,0,1:T(1,128)S(1)}, f32[1,3,8192]{2,0,1:T(1,128)}, u32[]{:S(2)}) copy-start(f32[1,3,8192]{2,0,1:T(1,128)} %param.25) | copy-start | bytes 294916
  17.2 18.5 %copy-start.2 = (f32[1,8192]{1,0:T(1,128)S(1)}, f32[1,8192]{1,0:T(1,128)}, u32[]{:S(2)}) copy-start(f32[1,8192]{1,0:T(1,128)} %param.28) | copy-start | bytes 98308
  17.2 19.2 %copy-start.3 = (f32[1,8192]{1,0:T(1,128)S(1)}, f32[1,8192]{1,0:T(1,128)}, u32[]{:S(2)}) copy-start(f32[1,8192]{1,0:T(1,128)} %param.26) | copy-start | bytes 98308
  17.2 20.6 %copy-start.6 = (s32[1,8192]{1,0:T(1,128)S(1)}, s32[1,8192]{1,0:T(1,128)}, u32[]{:S(2)}) copy-start(s32[1,8192]{1,0:T(1,128)} %param.31) | copy-start | bytes 98308
  17.2 21.4 %copy-start.7 = (f32[1,1024]{1,0:T(1,128)S(1)}, f32[1,1024]{1,0:T(1,128)}, u32[]{:S(2)}) copy-start(f32[1,1024]{1,0:T(1,128)} %param.34) | copy-start | bytes 12292
  17.2 22.6 %copy-start.15 = (u32[32]{0:T(128)S(1)}, u32[32]{0:T(128)}, u32[]{:S(2)}) copy-start(u32[32]{0:T(128)} %constant.151) | copy-start | bytes 388
  17.3 23.9 %copy-start.1 = (f32[1,8,8192]{2,1,0:T(8,128)S(1)}, f32[1,8,8192]{2,1,0:T(8,128)}, u32[]{:S(2)}) copy-start(f32[1,8,8192]{2,1,0:T(8,128)} %param.23) | copy-start | bytes 786436
  42.0 24.3 %copy-start.9 = (f32[1,8]{1,0:T(1,128)S(1)}, f32[1,8]{1,0:T(1,128)}, u32[]{:S(2)}) copy-start(f32[1,8]{1,0:T(1,128)} %param.24) | copy-start | bytes 100
  42.0 24.3 %copy-start.12 = (f32[1,8]{1,0:T(1,128)S(1)}, f32[1,8]{1,0:T(1,128)}, u32[]{:S(2)}) copy-start(f32[1,8]{1,0:T(1,128)} %param.29) | copy-start | bytes 100
  42.1 25.4 %copy-start.10 = (s32[1,1,160]{2,1,0:T(1,128)S(1)}, s32[1,1,160]{2,1,0:T(1,128)}, u32[]{:S(2)}) copy-start(s32[1,1,160]{2,1,0:T(1,128)} %param.39) | copy-start | bytes 1924
  42.1 30.9 %copy-start.11 = (s32[1,1,160]{2,1,0:T(1,128)S(1)}, s32[1,1,160]{2,1,0:T(1,128)}, u32[]{:S(2)}) copy-start(s32[1,1,160]{2,1,0:T(1,128)} %param.40) | copy-start | bytes 1924
  42.1 30.9 %copy-start.13 = (f32[1,4]{1,0:T(1,128)S(1)}, f32[1,4]{1,0:T(1,128)}, u32[]{:S(2)}) copy-start(f32[1,4]{1,0:T(1,128)} %param.30) | copy-start | bytes 52
  73.0 46.6 %copy-start.14 = (s32[1,1024]{1,0:T(1,128)S(1)}, s32[1,1024]{1,0:T(1,128)}, u32[]{:S(2)}) copy-start(s32[1,1024]{1,0:T(1,128)} %param.35) | copy-start | bytes 12292
  73.3 7.2 %collective-permute-start.2 = (f32[128]{0:T(128)S(1)}, f32[128]{0:T(128)S(1)}, u32[]{:S(2)}, u32[]{:S(2)}) collective-permute-start(f32[128]{0:T(128)S(1)} %get-tuple-element.151), channel_id=1, source_target_pairs={{0,1},{1,2},{2,3},{3,4},{4,5},{5,6},{6,7},{7,8},{8,9},{9,10},{10,1... | collective-permute-start | bytes 1544 | tf_op jit(solution)/shard_map/ppermute | solution.py:22
  75.0 5.5 %collective-permute-start.3 = (f32[128]{0:T(128)S(1)}, f32[128]{0:T(128)S(1)}, u32[]{:S(2)}, u32[]{:S(2)}) collective-permute-start(f32[128]{0:T(128)S(1)} %get-tuple-element.152), channel_id=1, source_target_pairs={{1,0},{2,1},{3,2},{4,3},{5,4},{6,5},{7,6},{8,7},{9,8},{10,9},{11,1... | collective-permute-start | bytes 1544 | tf_op jit(solution)/shard_map/ppermute | solution.py:24
  109.7 7.2 %collective-permute-start.4 = (f32[16]{0:T(128)S(1)}, f32[16]{0:T(128)S(1)}, u32[]{:S(2)}, u32[]{:S(2)}) collective-permute-start(f32[16]{0:T(128)S(1)} %get-tuple-element.159), channel_id=1, source_target_pairs={{0,1},{1,2},{2,3},{3,4},{4,5},{5,6},{6,7},{7,8},{8,9},{9,10},{10,1... | collective-permute-start | bytes 200 | tf_op jit(solution)/shard_map/ppermute | solution.py:22
  110.1 6.8 %collective-permute-start.5 = (f32[16]{0:T(128)S(1)}, f32[16]{0:T(128)S(1)}, u32[]{:S(2)}, u32[]{:S(2)}) collective-permute-start(f32[16]{0:T(128)S(1)} %get-tuple-element.160), channel_id=1, source_target_pairs={{1,0},{2,1},{3,2},{4,3},{5,4},{6,5},{7,6},{8,7},{9,8},{10,9},{11,1... | collective-permute-start | bytes 200 | tf_op jit(solution)/shard_map/ppermute | solution.py:24
  163.0 7.1 %collective-permute-start.6 = (f32[16]{0:T(128)S(1)}, f32[16]{0:T(128)S(1)}, u32[]{:S(2)}, u32[]{:S(2)}) collective-permute-start(f32[16]{0:T(128)S(1)} %get-tuple-element.155), channel_id=1, source_target_pairs={{0,1},{1,2},{2,3},{3,4},{4,5},{5,6},{6,7},{7,8},{8,9},{9,10},{10,1... | collective-permute-start | bytes 200 | tf_op jit(solution)/shard_map/ppermute | solution.py:22
  163.0 7.1 %collective-permute-start.7 = (f32[16]{0:T(128)S(1)}, f32[16]{0:T(128)S(1)}, u32[]{:S(2)}, u32[]{:S(2)}) collective-permute-start(f32[16]{0:T(128)S(1)} %get-tuple-element.156), channel_id=1, source_target_pairs={{1,0},{2,1},{3,2},{4,3},{5,4},{6,5},{7,6},{8,7},{9,8},{10,9},{11,1... | collective-permute-start | bytes 200 | tf_op jit(solution)/shard_map/ppermute | solution.py:24
  189.9 7.6 %collective-permute-start.8 = (f32[128]{0:T(128)S(1)}, f32[128]{0:T(128)S(1)}, u32[]{:S(2)}, u32[]{:S(2)}) collective-permute-start(f32[128]{0:T(128)S(1)} %get-tuple-element.147), channel_id=1, source_target_pairs={{0,1},{1,2},{2,3},{3,4},{4,5},{5,6},{6,7},{7,8},{8,9},{9,10},{10,1... | collective-permute-start | bytes 1544 | tf_op jit(solution)/shard_map/ppermute | solution.py:22
  189.9 7.5 %collective-permute-start.9 = (f32[128]{0:T(128)S(1)}, f32[128]{0:T(128)S(1)}, u32[]{:S(2)}, u32[]{:S(2)}) collective-permute-start(f32[128]{0:T(128)S(1)} %get-tuple-element.148), channel_id=1, source_target_pairs={{1,0},{2,1},{3,2},{4,3},{5,4},{6,5},{7,6},{8,7},{9,8},{10,9},{11,1... | collective-permute-start | bytes 1544 | tf_op jit(solution)/shard_map/ppermute | solution.py:24
where the time goes:
time: 215 us; the launch traced here: 214 us
  matrix products  97.2 us (45%)
  blocking collectives  42.2 us (20%)
  starting transfers between devices  32.7 us (15%)
  other arithmetic  26.2 us (12%)
  local copies, waits for them, and re-layouts  8.97 us (4%)
  waiting for transfers between devices  4.36 us (2%)
    dot_general x5, matrix products, neighbour_sum(): jnp.einsum('...bj,bij->...bi', windows, matrix, precision=lax.Precision.H...  61.8 us
    unnamed x1, blocking collectives  42.2 us
    ppermute x5, starting transfers between devices, extended(): lax.ppermute(head, axis, [((i + 1) % count, i) for i in range(count)])  25 us
    dot_general x3, other arithmetic, neighbour_sum(): jnp.einsum('...bj,bij->...bi', windows, matrix, precision=lax.Precision.H...  17.7 us
    dot_general x9, matrix products, part(): return jnp.dot(onehot, values, precision=lax.Precision.HIGHEST)  16.4 us
    dot_general x9, matrix products, part(): return jnp.dot(piece, onehot, precision=lax.Precision.HIGHEST)  12 us
    dot_general x1, matrix products, per_device(): jnp.einsum('efs,eds->efd', picked, remap_tiles[0, 0], preferred_element_t...  5.27 us
    ppermute x5, starting transfers between devices, extended(): lax.ppermute(tail, axis, [(i, (i + 1) % count) for i in range(count)])  5.11 us
  transfers between devices with their start and end apart: 11, of which 3 were waited for; matrix products, arithmetic and copies ran while one was open for 26% of the time, Pallas kernels for 0%

commit v1 on v0

v1 whole, which is shorter than its diff:
```python
import functools

import jax
import jax.numpy as jnp
from jax import lax
from jax.experimental import pallas as pl
from jax.experimental.pallas import tpu as pltpu
from jax.sharding import PartitionSpec as P

LANES = 128
RELAXATION = 0.8
F32 = jnp.float32
BF16 = jnp.bfloat16
I32 = jnp.int32

FIELD_HI, FIELD_LO = 0, 8
EDGE_HI, EDGE_LO, OLD_HI, OLD_LO = 16, 19, 22, 23
OFFSET, OWNER = 24, 27
CEDGE_HI, CEDGE_LO, CDIAG_HI, CDIAG_LO = 32, 38, 44, 46
COFFSET, COWNER = 48, 54
INVERSE = 56

FRAME, OWN = 32, 8


def gather_lanes(table, index):
    return jnp.take_along_axis(table, index, axis=1)


def wide(row, count=8):
    return jnp.broadcast_to(row, (count, row.shape[1]))


def split3(x):
    high = x.astype(BF16)
    rest = x - high.astype(F32)
    middle = rest.astype(BF16)
    low = (rest - middle.astype(F32)).astype(BF16)
    return high, middle, low


def dot_nt(a, b):
    return lax.dot_general(a, b, (((1,), (1,)), ((), ())), preferred_element_type=F32)


def dot_tn(a, b):
    return lax.dot_general(a, b, (((0,), (0,)), ((), ())), preferred_element_type=F32)


def column_of(scalars, offset, count):
    sublane = lax.broadcasted_iota(I32, (8, LANES), 0)
    value = jnp.zeros((8, LANES), F32)
    for level in range(count):
        value = jnp.where(sublane == level, scalars[0, level], value)
    return value


def pick_base(inverse_blocks):
    return -(-(INVERSE + 32 * inverse_blocks) // 16) * 16


def pack_kernel(
    surface, sends, fields, old, edge, table, owner, ctable, cedge, cdiag, cowner, cinverse,
    near1, far1, near2, far2, here, chunks, left_rows, right_rows,
):
    tile = lax.axis_index("tile")
    even = lax.rem(tile, 2) == 0
    low = lax.rem(tile, 4) < 2
    cells = fields.shape[1]
    blocks = cells // LANES
    firsts = ctable.shape[1]
    frows = firsts // LANES
    base = pick_base(cinverse.shape[1] // LANES)
    lane = lax.broadcasted_iota(I32, (1, LANES), 1)

    for rows, at_left in ((right_rows, False), (left_rows, True)):
        start = 0 if at_left else cells - LANES
        part = pl.ds(start, LANES)

        def both(high, low_row, value):
            count = value.shape[0]
            rows[pl.ds(high, count), :] = value
            rows[pl.ds(low_row, count), :] = value - value.astype(BF16).astype(F32)

        rows[pl.ds(24, 8), :] = jnp.zeros((8, LANES), F32)
        both(FIELD_HI, FIELD_LO, fields[:, part])
        both(EDGE_HI, EDGE_LO, edge[:, part])
        block = 0 if at_left else blocks - 1
        both(OLD_HI, OLD_LO, old[pl.ds(block, 1), :])
        rows[pl.ds(OFFSET, 3), :] = (table[:, part] - (LANES + start) - lane).astype(F32)
        shift = 0 if at_left else firsts - LANES
        rows[pl.ds(OWNER, 1), :] = (owner[pl.ds(block, 1), :] - shift).astype(F32)
        first = 0 if at_left else frows - 2
        reach = LANES // 8
        for step in range(2):
            cpart = pl.ds((first + step) * LANES, LANES)
            both(CEDGE_HI + 3 * step, CEDGE_LO + 3 * step, cedge[:, cpart])
            rows[pl.ds(COFFSET + 3 * step, 3), :] = (
                ctable[:, cpart] - (reach + (first + step) * LANES) - lane
            ).astype(F32)
            both(CDIAG_HI + step, CDIAG_LO + step, cdiag[pl.ds(first + step, 1), :])
            rows[pl.ds(COWNER + step, 1), :] = cowner[pl.ds(first + step, 1), :].astype(F32)
        halves = cinverse.shape[1] // LANES
        for half in range(halves):
            both(
                INVERSE + 16 * half,
                INVERSE + 16 * (halves + half),
                cinverse[:, pl.ds(half * LANES, LANES)],
            )
        end = INVERSE + 32 * halves
        if base > end:
            rows[pl.ds(end, base - end), :] = jnp.zeros((base - end, LANES), F32)

    for block in range(blocks):
        chunks[pl.ds(4 * block, 4), :] = surface[:, pl.ds(block * LANES, LANES)].astype(F32)
    slots = sends.shape[1]
    hot = jnp.where(
        lax.broadcasted_iota(I32, (blocks, slots), 0) == sends[...], 1.0, 0.0
    ).astype(BF16)
    picks = []
    for channel in range(4):
        source = chunks[pl.ds(channel, blocks, stride=4), :].astype(BF16)
        picks.append(dot_tn(hot, source).astype(BF16))
    count = slots // 5

    def chosen(j):
        return jnp.concatenate([p[j * count : (j + 1) * count] for p in picks], axis=0)

    to_right, to_left = chosen(1), chosen(3)
    far_right, far_left = chosen(0), chosen(4)
    here[...] = chosen(2)
    rim_right = right_rows[...].astype(BF16)
    rim_left = left_rows[...].astype(BF16)
    near1[pl.ds(0, base), :] = jnp.where(even, rim_right, rim_left)
    far1[pl.ds(0, base), :] = jnp.where(even, rim_left, rim_right)
    near1[pl.ds(base, 4 * count), :] = jnp.where(even, to_right, to_left)
    far1[pl.ds(base, 4 * count), :] = jnp.where(even, to_left, to_right)
    near2[...] = jnp.where(low, far_right, far_left)
    far2[...] = jnp.where(low, far_left, far_right)


def stencil_kernel(
    rate, level_weight, fields, edge, table, old, owner,
    fresh, force, beside_old, edges, window, ends_row, ends_lane, oldpad,
):
    blocks = old.shape[0]
    speed = column_of(rate, 0, fields.shape[0])
    share = column_of(level_weight, 0, fields.shape[0])

    def one(block, before, here, after):
        part = pl.ds(pl.multiple_of(block * LANES, LANES), LANES)
        weights = edge[:, part]
        place = table[:, part] - block * LANES
        for link in range(3):
            edges[link, pl.ds(block, 1), :] = weights[link : link + 1]
            window[link, pl.ds(block, 1), :] = place[link : link + 1]
        total = weights[0:1] + weights[1:2] + weights[2:3]
        inverse = 1.0 / total
        lanes = lax.bitwise_and(place, LANES - 1)
        which = lax.shift_right_logical(place, 7)
        beside = jnp.zeros((8, LANES), F32)
        for link in range(3):
            index = wide(lanes[link : link + 1])
            row = wide(which[link : link + 1])
            value = jnp.where(
                row == 1,
                gather_lanes(here, index),
                jnp.where(row == 0, gather_lanes(before, index), gather_lanes(after, index)),
            )
            beside = beside + wide(weights[link : link + 1]) * value
        result = here + speed * (beside - wide(total) * here) * wide(inverse)
        fresh[:, part] = result
        force[pl.ds(block, 1), :] = jnp.sum(result * share, axis=0, keepdims=True)

    blank = jnp.zeros((8, LANES), F32)

    def chunk(block):
        return fields[:, pl.ds(pl.multiple_of(block * LANES, LANES), LANES)]

    one(0, blank, chunk(0), chunk(1))

    def step(block, carry):
        one(block, chunk(block - 1), chunk(block), chunk(block + 1))
        return carry

    lax.fori_loop(1, blocks - 1, step, 0, unroll=2)
    one(blocks - 1, chunk(blocks - 2), chunk(blocks - 1), blank)

    oldpad[pl.ds(0, 8), :] = blank
    oldpad[pl.ds(8 + blocks, 8), :] = blank
    oldpad[pl.ds(8, blocks), :] = old[...]
    beside_old[...] = neighbour_sum(oldpad, edges, window, blocks)

    firsts = ends_row.shape[0] * LANES
    ident = lax.broadcasted_iota(I32, ends_row.shape, 0) * LANES + lax.broadcasted_iota(
        I32, ends_row.shape, 1
    )
    count = ends_row.shape[0]
    rows = jnp.zeros(ends_row.shape, I32)
    for block in range(blocks):
        last = jnp.broadcast_to(owner[pl.ds(block, 1), LANES - 1 : LANES], ends_row.shape)
        rows = rows + jnp.where(last <= ident, 1, 0)
    lanes = jnp.zeros(ends_row.shape, I32)
    for bit in (64, 32, 16, 8, 4, 2, 1):
        probe = lanes + (bit - 1)
        value = jnp.full(ends_row.shape, firsts, I32)
        for block in range(blocks):
            value = jnp.where(
                rows == block, gather_lanes(wide(owner[pl.ds(block, 1), :], count), probe), value
            )
        lanes = jnp.where(value <= ident, lanes + bit, lanes)
    ends_row[...] = rows
    ends_lane[...] = lanes


def neighbour_sum(padded, edges, window, blocks):
    before = padded[pl.ds(7, blocks), :]
    here = padded[pl.ds(8, blocks), :]
    after = padded[pl.ds(9, blocks), :]
    result = jnp.zeros((blocks, LANES), F32)
    for link in range(3):
        place = window[link]
        index = lax.bitwise_and(place, LANES - 1)
        row = lax.shift_right_logical(place, 7)
        value = jnp.where(
            row == 1,
            gather_lanes(here, index),
            jnp.where(row == 0, gather_lanes(before, index), gather_lanes(after, index)),
        )
        result = result + edges[link] * value
    return result


def first_level_sum(values, frame):
    before = pltpu.roll(values, 1, axis=0)
    after = pltpu.roll(values, FRAME - 1, axis=0)
    lane = lax.broadcasted_iota(I32, (FRAME, LANES), 1)
    result = jnp.zeros((FRAME, LANES), F32)
    for link in range(3):
        place = lane + frame[pl.ds(link * FRAME, FRAME), :].astype(I32)
        index = lax.bitwise_and(place, LANES - 1)
        value = jnp.where(
            place < 0,
            gather_lanes(before, index),
            jnp.where(place >= LANES, gather_lanes(after, index), gather_lanes(values, index)),
        )
        result = result + frame[pl.ds((3 + link) * FRAME, FRAME), :] * value
    return result


def previous_one(values):
    rolled = pltpu.roll(values, 1, axis=1)
    above = pltpu.roll(rolled, 1, axis=0)
    lane = lax.broadcasted_iota(I32, values.shape, 1)
    row = lax.broadcasted_iota(I32, values.shape, 0)
    return jnp.where(lane > 0, rolled, jnp.where(row > 0, above, 0.0))


def triangle():
    return jnp.where(
        lax.broadcasted_iota(I32, (LANES, LANES), 0) < lax.broadcasted_iota(I32, (LANES, LANES), 1),
        1.0,
        0.0,
    ).astype(BF16)


def prefix(values):
    ones = jnp.ones((LANES, LANES), BF16)
    right = jnp.concatenate([triangle(), ones], axis=1)
    count = values.shape[0]
    out = jnp.dot(
        jnp.concatenate(split3(values), axis=0), right, preferred_element_type=F32
    )
    out = out[:count] + out[count : 2 * count] + out[2 * count :]
    return out[:, :LANES], out[:, LANES:]


def forward_kernel(
    entry_block, rate, level_weight, flux_weight,
    tiles, near1, far1, near2, far2, here, slots, fields, edges, window, old, diagonal,
    force_part, beside_old, ends_row, ends_lane, fresh_ends,
    ctable, cedge, cdiag, cowner,
    summed, force_out, smooth_out, source_out, frame, ends_out, message,
    tile_buffer, picked, padded, prefixed, totals, arrivals, sems,
):
    tile = lax.axis_index("tile")
    tile_count = lax.axis_size("tile")
    even = lax.rem(tile, 2) == 0
    low = lax.rem(tile, 4) < 2
    entries = tiles.shape[0]
    blocks = old.shape[0]
    parts = sems.shape[0]
    step = entries // parts

    def load(part):
        return pltpu.make_async_copy(
            tiles.at[pl.ds(part * step, step)],
            tile_buffer.at[pl.ds(part * step, step)],
            sems.at[part],
        )

    for part in range(parts):
        load(part).start()

    base = near1.shape[0] - near2.shape[0]
    near, far = near1[...], far1[...]
    from_left = jnp.where(even, far, near)
    from_right = jnp.where(even, near, far)
    two_near, two_far = near2[...], far2[...]
    j0 = jnp.where(low, two_far, two_near)
    j4 = jnp.where(low, two_near, two_far)
    j1, j3, j2 = from_left[base:], from_right[base:], here[...]
    slot_count = slots.shape[1]
    each = j0.shape[0] // 4
    hot = jnp.where(
        lax.broadcasted_iota(I32, (slot_count, entries), 0) == slots[...], 1.0, 0.0
    ).astype(BF16)
    for channel in range(4):
        span = slice(channel * each, (channel + 1) * each)
        source = jnp.concatenate([j[span] for j in (j0, j1, j2, j3, j4)], axis=0)
        picked[pl.ds(channel, entries, stride=4), :] = dot_tn(hot, source)

    arrivals[0] = from_left[:base].astype(F32)
    arrivals[1] = from_right[:base].astype(F32)

    summed[...] = jnp.zeros(summed.shape, F32)
    for part in range(parts):
        load(part).wait()

        def pair(number, carry):
            entry = part * step + 2 * number
            rows = picked[pl.ds(pl.multiple_of(4 * entry, 8), 8), :].astype(BF16)
            first = dot_nt(rows, tile_buffer[entry])
            second = dot_nt(rows, tile_buffer[entry + 1])
            at = entry_block[0, entry]
            summed[at, pl.ds(0, 4), :] += first[0:4]
            at = entry_block[0, entry + 1]
            summed[at, pl.ds(4, 4), :] += second[4:8]
            return carry

        lax.fori_loop(0, step // 2, pair, 0, unroll=8)

    speed = column_of(rate, 0, fields.shape[0])
    share = column_of(level_weight, 0, fields.shape[0])
    force_out[...] = force_part[...]
    padded[pl.ds(0, 8), :] = jnp.zeros((8, LANES), F32)
    padded[pl.ds(8 + blocks, 8), :] = jnp.zeros((8, LANES), F32)
    beside_extra = []
    for side, block, target in ((0, 0, 0), (1, blocks - 1, 2)):
        halo = arrivals[side, pl.ds(FIELD_HI, 8), :] + arrivals[side, pl.ds(FIELD_LO, 8), :]
        halo_old = arrivals[side, pl.ds(OLD_HI, 1), :] + arrivals[side, pl.ds(OLD_LO, 1), :]
        total = edges[0, pl.ds(block, 1), :] + edges[1, pl.ds(block, 1), :] + edges[2, pl.ds(block, 1), :]
        extra = jnp.zeros((8, LANES), F32)
        extra_old = jnp.zeros((8, LANES), F32)
        for link in range(3):
            place = wide(window[link, pl.ds(block, 1), :])
            index = lax.bitwise_and(place, LANES - 1)
            weight = jnp.where(
                lax.shift_right_logical(place, 7) == target, wide(edges[link, pl.ds(block, 1), :]), 0.0
            )
            extra = extra + weight * gather_lanes(halo, index)
            extra_old = extra_old + weight * gather_lanes(wide(halo_old), index)
        change = speed * extra / wide(total)
        ends_out[:, pl.ds(side * LANES, LANES)] = fresh_ends[:, pl.ds(side * LANES, LANES)] + change
        force_out[pl.ds(block, 1), :] += jnp.sum(change * share, axis=0, keepdims=True)
        beside_extra.append(extra_old[0:1])

    force = force_out[...]
    for channel in range(4):
        value = summed[:, channel, :] + summed[:, channel + 4, :]
        force = force + flux_weight[0, channel] * value
    force_out[...] = force
    total = diagonal[...] + edges[0] + edges[1] + edges[2]
    smooth_out[...] = beside_old[...]
    smooth_out[pl.ds(0, 1), :] += beside_extra[0]
    smooth_out[pl.ds(blocks - 1, 1), :] += beside_extra[1]
    previous = old[...]
    smooth = previous + RELAXATION * (force - (total * previous - smooth_out[...])) / total
    smooth_out[...] = smooth
    padded[pl.ds(8, blocks), :] = smooth
    residual = force - total * smooth + neighbour_sum(padded, edges, window, blocks)

    inner, whole = prefix(residual)
    prefixed[...] = inner
    totals[...] = whole
    rows, lanes = ends_row[...], ends_lane[...]
    count = rows.shape[0]
    run = jnp.zeros((count, LANES), F32)
    ends = jnp.zeros((count, LANES), F32)
    for block in range(blocks):
        value = gather_lanes(wide(prefixed[pl.ds(block, 1), :], count), lanes) + run
        ends = jnp.where(rows == block, value, ends)
        run = run + wide(totals[pl.ds(block, 1), :], count)
    ends = jnp.where(rows == blocks, run, ends)
    own_source = ends - previous_one(ends)

    lane = lax.broadcasted_iota(I32, (1, LANES), 1)
    rim_rows, rim_counts = [], []
    for side in range(2):
        inside = padded[pl.ds(8 if side == 0 else 7 + blocks, 1), :]
        value = jnp.zeros((1, LANES), F32)
        for link in range(3):
            place = lane + arrivals[side, pl.ds(OFFSET + link, 1), :].astype(I32)
            index = lax.bitwise_and(place, LANES - 1)
            reached = (place >= LANES) if side == 0 else (place < 0)
            weight = arrivals[side, pl.ds(EDGE_HI + link, 1), :] + arrivals[side, pl.ds(EDGE_LO + link, 1), :]
            value = value + jnp.where(
                wide(reached.astype(I32)) > 0,
                wide(weight) * gather_lanes(wide(inside), wide(index)),
                0.0,
            )[0:1]
        rim_rows.append(value)
        owners = arrivals[side, pl.ds(OWNER, 1), :].astype(I32)
        below = jnp.where(
            lax.broadcasted_iota(I32, (LANES, LANES), 0) >= owners, 1.0, 0.0
        ).astype(BF16)
        rim_counts.append(dot_nt(jnp.ones((8, LANES), BF16), below))
    rim_inner, rim_whole = prefix(jnp.concatenate([wide(r) for r in rim_rows], axis=0))
    rim_source = []
    for side in range(2):
        place = rim_counts[side].astype(I32)
        index = lax.bitwise_and(place, LANES - 1)
        value = gather_lanes(rim_inner[8 * side : 8 * side + 8], index)
        value = jnp.where(place >= LANES, rim_whole[8 * side : 8 * side + 8], value)
        shifted = pltpu.roll(value, 1, axis=1)
        first = lax.broadcasted_iota(I32, (8, LANES), 1) == 0
        rim_source.append((value - jnp.where(first, 0.0, shifted))[0:1])

    frows = own_source.shape[0]
    source_out[...] = jnp.zeros((FRAME, LANES), F32)
    source_out[pl.ds(OWN, frows), :] = own_source
    source_out[pl.ds(OWN - 1, 1), :] = rim_source[0]
    source_out[pl.ds(OWN + frows, 1), :] = rim_source[1]
    reach = LANES // 8
    frame[...] = jnp.zeros(frame.shape, F32)
    frame[pl.ds(6 * FRAME, FRAME), :] = jnp.ones((FRAME, LANES), F32)
    frame[pl.ds(7 * FRAME, FRAME), :] = jnp.full((FRAME, LANES), 127.0, F32)
    bottoms = 16
    for row in range(frows):
        part = pl.ds(row * LANES, LANES)
        offsets = (ctable[:, part] - (reach + row * LANES) - lane).astype(F32)
        weights = cedge[:, part]
        for link in range(3):
            frame[pl.ds(link * FRAME + OWN + row, 1), :] = offsets[link : link + 1]
            frame[pl.ds((3 + link) * FRAME + OWN + row, 1), :] = weights[link : link + 1]
    frame[pl.ds(6 * FRAME + OWN, frows), :] = cdiag[...]
    frame[pl.ds(7 * FRAME + OWN, frows), :] = (cowner[...] + bottoms).astype(F32)
    for side in range(2):
        for row in range(2):
            at = (OWN - 2 + row) if side == 0 else (OWN + frows + row)
            for link in range(3):
                put = 3 * row + link
                frame[pl.ds(link * FRAME + at, 1), :] = arrivals[side, pl.ds(COFFSET + put, 1), :]
                frame[pl.ds((3 + link) * FRAME + at, 1), :] = (
                    arrivals[side, pl.ds(CEDGE_HI + put, 1), :] + arrivals[side, pl.ds(CEDGE_LO + put, 1), :]
                )
            frame[pl.ds(6 * FRAME + at, 1), :] = (
                arrivals[side, pl.ds(CDIAG_HI + row, 1), :] + arrivals[side, pl.ds(CDIAG_LO + row, 1), :]
            )
            frame[pl.ds(7 * FRAME + at, 1), :] = arrivals[side, pl.ds(COWNER + row, 1), :] + (
                2.0 * bottoms * side
            )
    for link in range(3):
        frame[pl.ds(6 * FRAME, FRAME), :] += frame[pl.ds((3 + link) * FRAME, FRAME), :]
    source = source_out[...]
    first = RELAXATION * source / frame[pl.ds(6 * FRAME, FRAME), :]
    residual = (1.0 - RELAXATION) * source + first_level_sum(first, frame)
    codes = frame[pl.ds(7 * FRAME, FRAME), :].astype(I32)
    pieces = split3(residual)
    left_side, right_side = [], []
    bins = lax.broadcasted_iota(I32, (LANES, LANES), 0)
    for row in range(OWN - 2, OWN + frows + 2):
        left_side.append(jnp.concatenate([p[row : row + 1] for p in pieces], axis=0))
        right_side.append(
            jnp.where(bins == codes[row : row + 1], 1.0, 0.0).astype(BF16)
        )
    bottom = dot_nt(jnp.concatenate(left_side, axis=1), jnp.concatenate(right_side, axis=1))
    bottom = bottom[0:1] + bottom[1:2] + bottom[2:3]
    bottom = jnp.where(lane < 3 * bottoms, bottom, 0.0)

    to_left = jnp.concatenate(
        [bottom, padded[pl.ds(8, 1), :], own_source[0:2], rim_source[0], jnp.zeros((3, LANES), F32)], axis=0
    )
    to_right = jnp.concatenate(
        [bottom, padded[pl.ds(7 + blocks, 1), :], own_source[frows - 2 : frows], rim_source[1], jnp.zeros((3, LANES), F32)],
        axis=0,
    )
    for other in range(message.shape[0]):
        message[other] = to_right
    message[lax.rem(tile + tile_count - 1, tile_count)] = to_left


def prepare_kernel(
    fresh, ends_new, summed, near1, far1, cinverse, fresh_out, received, weights, sem, extended
):
    del fresh
    tile = lax.axis_index("tile")
    even = lax.rem(tile, 2) == 0
    cells = fresh_out.shape[1]
    copies = [
        pltpu.make_async_copy(
            ends_new.at[:, pl.ds(side * LANES, LANES)],
            fresh_out.at[:, pl.ds(side * (cells - LANES), LANES)],
            sem.at[side],
        )
        for side in range(2)
    ]
    for copy in copies:
        copy.start()
    blocks = summed.shape[0]
    for block in range(blocks):
        received[:, pl.ds(block * LANES, LANES)] = summed[block, pl.ds(0, 4), :] + summed[block, pl.ds(4, 4), :]
    bottoms, size = cinverse.shape
    halves = size // LANES
    near = near1[pl.ds(INVERSE, 32 * halves), :].astype(F32)
    far = far1[pl.ds(INVERSE, 32 * halves), :].astype(F32)
    left = jnp.where(even, far, near)
    right = jnp.where(even, near, far)
    for half in range(halves):
        part = pl.ds(half * LANES, LANES)
        for at, block in ((0, left), (2, right)):
            extended[pl.ds(at * bottoms, bottoms), part] = (
                block[16 * half : 16 * half + 16]
                + block[16 * (halves + half) : 16 * (halves + half) + 16]
            )
        extended[pl.ds(bottoms, bottoms), part] = cinverse[:, part]
    table = extended[...]
    lane = lax.broadcasted_iota(I32, (3 * bottoms, LANES), 1)
    for other in range(weights.shape[0]):
        shift = (size - (other - 1) * bottoms) % size
        turned = pltpu.roll(table, shift, axis=1) if shift else table
        weights[other] = jnp.where(lane < 3 * bottoms, turned[:, :LANES], 0.0)
    for copy in copies:
        copy.wait()


def backward_kernel(
    frame_rows, arrived, weights, source, frame, force, smooth, edges, window, diagonal, owner, near1, far1,
    height, frame_source, padded, third_rows,
):
    tile = lax.axis_index("tile")
    tile_count = lax.axis_size("tile")
    even = lax.rem(tile, 2) == 0
    blocks = force.shape[0]
    left = arrived[lax.rem(tile + tile_count - 1, tile_count)]
    right = arrived[lax.rem(tile + 1, tile_count)]
    count = weights.shape[1]
    partial = jnp.zeros((count, LANES), F32)
    for other in range(weights.shape[0]):
        partial = partial + weights[other] * wide(arrived[other, pl.ds(0, 1), :], count)
    partial = jnp.concatenate([partial, jnp.zeros((LANES - count, LANES), F32)], axis=0)
    ones = jnp.ones((8, LANES), BF16)
    pieces = split3(partial)
    bottom = dot_nt(ones, pieces[0]) + dot_nt(ones, pieces[1]) + dot_nt(ones, pieces[2])

    frows = frame_rows
    frame_source[...] = source[...]
    frame_source[pl.ds(OWN - 2, 2), :] += left[2:4]
    frame_source[pl.ds(OWN, 1), :] += left[4:5]
    frame_source[pl.ds(OWN + frows - 1, 1), :] += right[4:5]
    frame_source[pl.ds(OWN + frows, 2), :] += right[2:4]
    total_source = frame_source[...]
    total = frame[pl.ds(6 * FRAME, FRAME), :]
    codes = frame[pl.ds(7 * FRAME, FRAME), :].astype(I32)
    second = RELAXATION * total_source / total + gather_lanes(wide(bottom[0:1], FRAME), codes)
    third = second + RELAXATION * (
        total_source - total * second + first_level_sum(second, frame)
    ) / total
    third_rows[...] = third

    owners = owner[...]
    index = lax.bitwise_and(owners, LANES - 1)
    which = lax.shift_right_logical(owners, 7)
    corrected = jnp.zeros((blocks, LANES), F32)
    for row in range(frows):
        corrected = jnp.where(
            which == row, gather_lanes(wide(third_rows[pl.ds(OWN + row, 1), :], blocks), index), corrected
        )
    corrected = smooth[...] + corrected
    padded[pl.ds(8, blocks), :] = corrected
    near = near1[pl.ds(16, 16), :].astype(F32)
    far = far1[pl.ds(16, 16), :].astype(F32)
    left_owner = jnp.where(even, far, near)[OWNER - 16 : OWNER - 15].astype(I32)
    right_owner = jnp.where(even, near, far)[OWNER - 16 : OWNER - 15].astype(I32)
    left_rim = left[1:2] + gather_lanes(wide(third_rows[pl.ds(OWN - 1, 1), :]), wide(left_owner))[0:1]
    right_rim = right[1:2] + gather_lanes(wide(third_rows[pl.ds(OWN + frows, 1), :]), wide(right_owner))[0:1]
    padded[pl.ds(7, 1), :] = left_rim
    padded[pl.ds(8 + blocks, 1), :] = right_rim
    fine_total = diagonal[...] + edges[0] + edges[1] + edges[2]
    beside = neighbour_sum(padded, edges, window, blocks)
    height[...] = corrected + RELAXATION * (force[...] - (fine_total * corrected - beside)) / fine_total


def struct(shape, dtype=F32):
    return jax.ShapeDtypeStruct(shape, dtype)


VMEM = pl.BlockSpec(memory_space=pltpu.VMEM)
SMEM = pl.BlockSpec(memory_space=pltpu.SMEM)
ANY = pl.BlockSpec(memory_space=pl.ANY)
PARAMS = pltpu.CompilerParams(vmem_limit_bytes=48 * 1024 * 1024)


def pair_up(count, distance):
    period = 2 * distance
    result = []
    for start in (0, distance):
        pairs = []
        for i in range(count):
            if (i - start) % period < distance:
                pairs += [(i, (i + distance) % count), ((i + distance) % count, i)]
        result.append(pairs)
    return result


def per_device(
    fields, level_rate, edge_weight, fine_diagonal, fine_table, old_height, level_weight,
    flux_weight, fine_owner, coarse_table, coarse_edge, coarse_diagonal, coarse_owner,
    coarse_inverse, surface_out, send_blocks, entry_slot, entry_block, remap_tiles,
):
    tile_count = lax.axis_size("tile")
    cells = fields.shape[2]
    blocks = cells // LANES
    firsts = coarse_diagonal.shape[1]
    frows = firsts // LANES
    entries = entry_slot.shape[2]
    channels = surface_out.shape[1]
    slots = send_blocks.shape[2]
    each = slots // 5
    halves = coarse_inverse.shape[2] // LANES
    bottoms = coarse_inverse.shape[1]
    base = pick_base(halves)
    swap = [(0, 1), (1, 0)]
    surface = lax.ppermute(surface_out[0], "comp", swap)
    sends = lax.ppermute(send_blocks[0], "comp", swap)
    old = old_height.reshape(blocks, LANES)
    owner = fine_owner.reshape(blocks, LANES)
    diagonal = fine_diagonal.reshape(blocks, LANES)
    cdiag = coarse_diagonal.reshape(frows, LANES)
    cowner = coarse_owner.reshape(frows, LANES)

    near1, far1, near2, far2, here = pl.pallas_call(
        pack_kernel,
        out_shape=[
            struct((base + 4 * each, LANES), BF16),
            struct((base + 4 * each, LANES), BF16),
            struct((4 * each, LANES), BF16),
            struct((4 * each, LANES), BF16),
            struct((4 * each, LANES), BF16),
        ],
        in_specs=[VMEM] * 12,
        out_specs=[VMEM] * 5,
        scratch_shapes=[
            pltpu.VMEM((channels * blocks, LANES), F32),
            pltpu.VMEM((base, LANES), F32),
            pltpu.VMEM((base, LANES), F32),
        ],
        compiler_params=PARAMS,
        name="pack",
    )(
        surface, sends, fields[0], old, edge_weight[0], fine_table[0], owner,
        coarse_table[0], coarse_edge[0], cdiag, cowner, coarse_inverse[0],
    )
    one_a, one_b = pair_up(tile_count, 1)
    two_a, two_b = pair_up(tile_count, 2)
    far1 = lax.ppermute(far1, "tile", one_b)
    far2 = lax.ppermute(far2, "tile", two_b)
    near1 = lax.ppermute(near1, "tile", one_a)
    near2 = lax.ppermute(near2, "tile", two_a)

    fresh, force_part, beside_old, edges, window, ends_row, ends_lane = pl.pallas_call(
        stencil_kernel,
        out_shape=[
            struct((fields.shape[1], cells)),
            struct((blocks, LANES)),
            struct((blocks, LANES)),
            struct((3, blocks, LANES)),
            struct((3, blocks, LANES), I32),
            struct((frows, LANES), I32),
            struct((frows, LANES), I32),
        ],
        in_specs=[SMEM, SMEM] + [VMEM] * 5,
        out_specs=[VMEM] * 7,
        scratch_shapes=[pltpu.VMEM((blocks + 16, LANES), F32)],
        compiler_params=PARAMS,
        name="stencil",
    )(level_rate, level_weight, fields[0], edge_weight[0], fine_table[0], old, owner)
    fresh_ends = jnp.concatenate([fresh[:, :LANES], fresh[:, cells - LANES :]], axis=1)

    parts = 5
    summed, force, smooth, source, frame, ends_new, message = pl.pallas_call(
        forward_kernel,
        out_shape=[
            struct((blocks, 8, LANES)),
            struct((blocks, LANES)),
            struct((blocks, LANES)),
            struct((FRAME, LANES)),
            struct((8 * FRAME, LANES)),
            struct((fields.shape[1], 2 * LANES)),
            struct((tile_count, 8, LANES)),
        ],
        in_specs=[SMEM] * 4 + [ANY] + [VMEM] * 20,
        out_specs=[VMEM] * 7,
        scratch_shapes=[
            pltpu.VMEM((entries, LANES, LANES), BF16),
            pltpu.VMEM((4 * entries, LANES), F32),
            pltpu.VMEM((blocks + 16, LANES), F32),
            pltpu.VMEM((blocks, LANES), F32),
            pltpu.VMEM((blocks, LANES), F32),
            pltpu.VMEM((2, base, LANES), F32),
            pltpu.SemaphoreType.DMA((parts,)),
        ],
        compiler_params=PARAMS,
        name="forward",
    )(
        entry_block[0], level_rate, level_weight, flux_weight,
        remap_tiles[0, 0], near1, far1, near2, far2, here, entry_slot[0], fields[0], edges, window,
        old, diagonal, force_part, beside_old, ends_row, ends_lane, fresh_ends,
        coarse_table[0], coarse_edge[0], cdiag, cowner,
    )
    arrived = lax.all_to_all(message, "tile", split_axis=0, concat_axis=0, tiled=True)
    advanced, received, weights = pl.pallas_call(
        prepare_kernel,
        out_shape=[
            struct((fields.shape[1], cells)),
            struct((channels, cells)),
            struct((tile_count, 3 * bottoms, LANES)),
        ],
        in_specs=[ANY] + [VMEM] * 5,
        out_specs=[ANY, VMEM, VMEM],
        scratch_shapes=[
            pltpu.SemaphoreType.DMA((2,)),
            pltpu.VMEM((3 * bottoms, bottoms * tile_count), F32),
        ],
        input_output_aliases={0: 0},
        compiler_params=PARAMS,
        name="prepare",
    )(fresh, ends_new, summed, near1, far1, coarse_inverse[0])
    height = pl.pallas_call(
        functools.partial(backward_kernel, frows),
        out_shape=struct((blocks, LANES)),
        in_specs=[VMEM] * 12,
        out_specs=VMEM,
        scratch_shapes=[
            pltpu.VMEM((FRAME, LANES), F32),
            pltpu.VMEM((blocks + 16, LANES), F32),
            pltpu.VMEM((FRAME, LANES), F32),
        ],
        compiler_params=PARAMS,
        name="backward",
    )(arrived, weights, source, frame, force, smooth, edges, window, diagonal, owner, near1, far1)
    return advanced[None], received[None], height.reshape(1, cells)


def solution(mesh):
    in_specs = (
        P("comp", None, "tile"),
        P("comp", None),
        P("comp", None, "tile"),
        P("comp", "tile"),
        P("comp", None, "tile"),
        P("comp", "tile"),
        P("comp", None),
        P("comp", None),
        P("comp", "tile"),
        P("comp", None, "tile"),
        P("comp", None, "tile"),
        P("comp", "tile"),
        P("comp", "tile"),
        P("comp", "tile", None),
        P("comp", None, "tile"),
        P("comp", "tile", None),
        P("comp", "tile", None),
        P("comp", "tile", None),
        P("comp", "tile", None, None, None),
    )
    out_specs = (P("comp", None, "tile"), P("comp", None, "tile"), P("comp", "tile"))
    return jax.shard_map(
        per_device, mesh=mesh, in_specs=in_specs, out_specs=out_specs, check_vma=False
    )
```

time: 215 us -> 64.6 us (0.30)
  matrix products: 97.2 us -> 0 us
  blocking collectives: 42.2 us -> 0 us
  other arithmetic: 26.2 us -> 0.01 us
  starting transfers between devices: 32.7 us -> 13.3 us
  Pallas kernels: 0 us -> 16.9 us
  local copies, waits for them, and re-layouts: 8.97 us -> 19.5 us
  waiting for transfers between devices: 4.36 us -> 12.9 us
    dot_general x28 -> x0, matrix products: 97.2 us -> none  [the longest x5 61.8 us: neighbour_sum(): jnp.einsum('...bj,bij->...bi', windows, matrix, precision=lax.Precision.H...]
    unnamed x1 -> x0, blocking collectives: 42.2 us -> none
    ppermute x10 -> x6, starting transfers between devices: 30.1 us -> 9.79 us  [the longest x1 3.55 us: per_device(): far2 = lax.ppermute(far2, 'tile', two_b)]
    dot_general x3 -> x0, other arithmetic: 17.7 us -> none  [neighbour_sum(): jnp.einsum('...bj,bij->...bi', windows, matrix, precision=lax.Precision.H...]
    pallas_call x0 -> x5, Pallas kernels: none -> 16.9 us  [the longest x1 7.62 us: per_device(): pl.pallas_call(forward_kernel, out_shape=[struct((blocks, 8, LANES)), str...]
    unnamed x38 -> x52, local copies, waits for them, and re-layouts: 2.04 us -> 18.8 us
    all_to_all x1, waiting for transfers between devices: 0.01 us -> 6.2 us  [per_device(): lax.all_to_all(message, 'tile', split_axis=0, concat_axis=0, tiled=True)]
    unnamed x4 -> x0, other arithmetic: 2.87 us -> none
  transfers between devices with their start and end apart: 11 -> 7, of which waited for: 3 -> 4; matrix products, arithmetic and copies ran while one was open for 26% -> 6% of each run, Pallas kernels for 0% -> 12%
where the time goes in v1:
time: 64.6 us; the launch traced here: 63.5 us
  local copies, waits for them, and re-layouts  19.5 us (30%)
  Pallas kernels  16.9 us (26%)
  starting transfers between devices  13.3 us (21%)
  waiting for transfers between devices  12.9 us (20%)
  between operations  0.75 us (1%)
    unnamed x52, local copies, waits for them, and re-layouts  18.8 us
    pallas_call x1, Pallas kernels, per_device(): pl.pallas_call(forward_kernel, out_shape=[struct((blocks, 8, LANES)), str...  7.62 us
    pallas_call x1, Pallas kernels, per_device(): pl.pallas_call(stencil_kernel, out_shape=[struct((fields.shape[1], cells)...  6.24 us
    all_to_all x1, waiting for transfers between devices, per_device(): lax.all_to_all(message, 'tile', split_axis=0, concat_axis=0, tiled=True)  6.2 us
    ppermute x1, waiting for transfers between devices, per_device(): far1 = lax.ppermute(far1, 'tile', one_b)  5.09 us
    ppermute x1, starting transfers between devices, per_device(): far2 = lax.ppermute(far2, 'tile', two_b)  3.55 us
    all_to_all x1, starting transfers between devices, per_device(): lax.all_to_all(message, 'tile', split_axis=0, concat_axis=0, tiled=True)  3.5 us
    ppermute x1, starting transfers between devices, per_device(): near2 = lax.ppermute(near2, 'tile', two_a)  3.01 us
  transfers between devices with their start and end apart: 7, of which 4 were waited for; matrix products, arithmetic and copies ran while one was open for 6% of the time, Pallas kernels for 12%

profile of v1, /device:TPU:0, one launch (start us, length us, event | category | flops | bytes accessed | tf_op | source)
XLA Modules:
  0.0 63.5 jit_solution(8078273757972721518)
XLA Ops:
  0.6 0.0 copy-start.8
  0.6 0.0 copy-start.12
  0.7 0.0 copy-start.10
  0.7 0.5 collective-permute-start.1
  1.2 0.1 collective-permute-start
  1.3 1.0 %copy.32 = f32[1,3,8192]{2,1,0:T(4,128)S(1)} copy(f32[1,3,8192]{2,0,1:T(1,128)} %param.21) | data formatting | bytes 196608
  2.2 1.0 %copy.31 = s32[1,3,8192]{2,1,0:T(4,128)S(1)} copy(s32[1,3,8192]{2,0,1:T(1,128)} %param.23) | data formatting | bytes 196608
  3.2 0.0 copy-start
  3.2 0.9 %copy-done = f32[1,8,8192]{2,1,0:T(8,128)S(1)} copy-done((f32[1,8,8192]{2,1,0:T(8,128)S(1)}, f32[1,8,8192]{2,1,0:T(8,128)}, u32[]{:S(2)}) %copy-start) | copy-done | bytes 262168
  4.2 0.8 %copy-done.3 = f32[1,8192]{1,0:T(1,128)S(1)} copy-done((f32[1,8192]{1,0:T(1,128)S(1)}, f32[1,8192]{1,0:T(1,128)}, u32[]{:S(2)}) %copy-start.3) | copy-done | bytes 32792
  4.9 0.8 %copy-done.6 = s32[1,8192]{1,0:T(1,128)S(1)} copy-done((s32[1,8192]{1,0:T(1,128)S(1)}, s32[1,8192]{1,0:T(1,128)}, u32[]{:S(2)}) %copy-start.6) | copy-done | bytes 32792
  5.7 0.7 %copy-done.17 = f32[1,8]{1,0:T(1,128)S(1)} copy-done((f32[1,8]{1,0:T(1,128)S(1)}, f32[1,8]{1,0:T(1,128)}, u32[]{:S(2)}) %copy-start.17) | copy-done | bytes 56
  6.3 0.7 %copy-done.19 = f32[1,8]{1,0:T(1,128)S(1)} copy-done((f32[1,8]{1,0:T(1,128)S(1)}, f32[1,8]{1,0:T(1,128)}, u32[]{:S(2)}) %copy-start.19) | copy-done | bytes 56
  7.0 6.2 %stencil.1 = (f32[8,8192]{1,0:T(8,128)}, f32[64,128]{1,0:T(8,128)S(1)}, f32[64,128]{1,0:T(8,128)S(1)}, f32[3,64,128]{2,1,0:T(8,128)S(1)}, s32[3,64,128]{2,1,0:T(...) custom-call(f32[1,8]{1,0:T(1,128)S(1)} %copy-done.17, f32[1,8]{1,0:T(1,128)S(1)} %copy-done.19, ...), custom_call_target="tpu_custom_call" | custom-call | tf_op jit(solution)/shard_map/stencil/pallas_call | solution.py:671
  13.2 0.7 %fusion = (f32[8,128]{1,0:T(8,128)S(1)}, f32[8,128]{1,0:T(8,128)S(1)}) fusion(f32[8,8192]{1,0:T(8,128)} %get-tuple-element.25.fresh), kind=kLoop, calls=%fused_computation.5 | loop fusion | bytes 16384 | tf_op jit(solution)/shard_map/slice | solution.py:688
  13.9 0.7 %copy.34 = s32[1,3,1024]{2,1,0:T(4,128)S(1)} copy(s32[1,3,1024]{2,0,1:T(1,128)} %param.28) | data formatting | bytes 24576
  14.6 0.7 %copy.33 = f32[1,3,1024]{2,1,0:T(4,128)S(1)} copy(f32[1,3,1024]{2,0,1:T(1,128)} %param.29) | data formatting | bytes 24576
  15.3 0.0 collective-permute-done.1.sends
  15.4 0.0 copy-start.1
  15.4 0.9 %copy-done.1 = f32[1,8,8192]{2,1,0:T(8,128)S(1)} copy-done((f32[1,8,8192]{2,1,0:T(8,128)S(1)}, f32[1,8,8192]{2,1,0:T(8,128)}, u32[]{:S(2)}) %copy-start.1) | copy-done | bytes 262168
  16.3 0.8 %copy-done.4 = f32[1,8192]{1,0:T(1,128)S(1)} copy-done((f32[1,8192]{1,0:T(1,128)S(1)}, f32[1,8192]{1,0:T(1,128)}, u32[]{:S(2)}) %copy-start.4) | copy-done | bytes 32792
  17.1 0.8 %copy-done.7 = s32[1,8192]{1,0:T(1,128)S(1)} copy-done((s32[1,8192]{1,0:T(1,128)S(1)}, s32[1,8192]{1,0:T(1,128)}, u32[]{:S(2)}) %copy-start.7) | copy-done | bytes 32792
  17.8 0.7 %copy-done.11 = f32[1,16,256]{2,1,0:T(8,128)S(1)} copy-done((f32[1,16,256]{2,1,0:T(8,128)S(1)}, f32[1,16,256]{2,1,0:T(8,128)}, u32[]{:S(2)}) %copy-start.11) | copy-done | bytes 16408
  18.5 0.7 %copy-done.13 = f32[1,1024]{1,0:T(1,128)S(1)} copy-done((f32[1,1024]{1,0:T(1,128)S(1)}, f32[1,1024]{1,0:T(1,128)}, u32[]{:S(2)}) %copy-start.13) | copy-done | bytes 4120
  19.2 0.7 %copy-done.15 = s32[1,1024]{1,0:T(1,128)S(1)} copy-done((s32[1,1024]{1,0:T(1,128)S(1)}, s32[1,1024]{1,0:T(1,128)}, u32[]{:S(2)}) %copy-start.15) | copy-done | bytes 4120
  19.9 0.2 pack.1
  20.2 3.0 %collective-permute-start.4 = (bf16[128,128]{1,0:T(8,128)(2,1)S(1)}, bf16[128,128]{1,0:T(8,128)(2,1)S(1)}, u32[]{:S(2)}, u32[]{:S(2)}) collective-permute-start(bf16[128,128]{1,0:T(8,128)(2,1)S(1)} %get-tuple-element.28), channel_id=1, source_target_pairs={{0,2},{2,0},{1,3},{3,1},{4,6},{6,4},{5,7},{7,5},{8,10},{10,8},{9,1... | collective-permute-start | bytes 98312 | tf_op jit(solution)/shard_map/ppermute | solution.py:669
  23.2 3.5 %collective-permute-start.5 = (bf16[128,128]{1,0:T(8,128)(2,1)S(1)}, bf16[128,128]{1,0:T(8,128)(2,1)S(1)}, u32[]{:S(2)}, u32[]{:S(2)}) collective-permute-start(bf16[128,128]{1,0:T(8,128)(2,1)S(1)} %get-tuple-element.29), channel_id=1, source_target_pairs={{2,4},{4,2},{3,5},{5,3},{6,8},{8,6},{7,9},{9,7},{10,12},{12,10},{1... | collective-permute-start | bytes 98312 | tf_op jit(solution)/shard_map/ppermute | solution.py:667
  26.7 1.5 %collective-permute-start.2 = (bf16[256,128]{1,0:T(8,128)(2,1)S(1)}, bf16[256,128]{1,0:T(8,128)(2,1)S(1)}, u32[]{:S(2)}, u32[]{:S(2)}) collective-permute-start(bf16[256,128]{1,0:T(8,128)(2,1)S(1)} %get-tuple-element.26), channel_id=1, source_target_pairs={{0,1},{1,0},{2,3},{3,2},{4,5},{5,4},{6,7},{7,6},{8,9},{9,8},{10,11... | collective-permute-start | bytes 196616 | tf_op jit(solution)/shard_map/ppermute | solution.py:668
  28.2 1.1 %collective-permute-start.3 = (bf16[256,128]{1,0:T(8,128)(2,1)S(1)}, bf16[256,128]{1,0:T(8,128)(2,1)S(1)}, u32[]{:S(2)}, u32[]{:S(2)}) collective-permute-start(bf16[256,128]{1,0:T(8,128)(2,1)S(1)} %get-tuple-element.27), channel_id=1, source_target_pairs={{1,2},{2,1},{3,4},{4,3},{5,6},{6,5},{7,8},{8,7},{9,10},{10,9},{11,... | collective-permute-start | bytes 196616 | tf_op jit(solution)/shard_map/ppermute | solution.py:666
  29.4 0.4 collective-permute-done.5.far2
  29.8 1.2 %collective-permute-done.2.near1 = bf16[256,128]{1,0:T(8,128)(2,1)S(1)} collective-permute-done((bf16[256,128]{1,0:T(8,128)(2,1)S(1)}, bf16[256,128]{1,0:T(8,128)(2,1)S(1)}, u32[]{:S(2)}, u32[]{:S(2)}) %collective-permute-start.2) | collective-permute-done | bytes 65568 | tf_op jit(solution)/shard_map/ppermute | solution.py:668
  31.0 5.1 %collective-permute-done.3.far1 = bf16[256,128]{1,0:T(8,128)(2,1)S(1)} collective-permute-done((bf16[256,128]{1,0:T(8,128)(2,1)S(1)}, bf16[256,128]{1,0:T(8,128)(2,1)S(1)}, u32[]{:S(2)}, u32[]{:S(2)}) %collective-permute-start.3) | collective-permute-done | bytes 65568 | tf_op jit(solution)/shard_map/ppermute | solution.py:666
  36.1 0.9 %copy-done.2 = f32[1,8,8192]{2,1,0:T(8,128)S(1)} copy-done((f32[1,8,8192]{2,1,0:T(8,128)S(1)}, f32[1,8,8192]{2,1,0:T(8,128)}, u32[]{:S(2)}) %copy-start.2) | copy-done | bytes 262168
  37.0 0.8 %copy-done.5 = f32[1,8192]{1,0:T(1,128)S(1)} copy-done((f32[1,8192]{1,0:T(1,128)S(1)}, f32[1,8192]{1,0:T(1,128)}, u32[]{:S(2)}) %copy-start.5) | copy-done | bytes 32792
  37.8 0.8 %copy-done.9 = f32[1,8192]{1,0:T(1,128)S(1)} copy-done((f32[1,8192]{1,0:T(1,128)S(1)}, f32[1,8192]{1,0:T(1,128)}, u32[]{:S(2)}) %copy-start.9) | copy-done | bytes 32792
  38.5 0.7 %copy-done.14 = f32[1,1024]{1,0:T(1,128)S(1)} copy-done((f32[1,1024]{1,0:T(1,128)S(1)}, f32[1,1024]{1,0:T(1,128)}, u32[]{:S(2)}) %copy-start.14) | copy-done | bytes 4120
  39.2 0.7 %copy-done.16 = s32[1,1024]{1,0:T(1,128)S(1)} copy-done((s32[1,1024]{1,0:T(1,128)S(1)}, s32[1,1024]{1,0:T(1,128)}, u32[]{:S(2)}) %copy-start.16) | copy-done | bytes 4120
  39.9 0.7 %copy-done.18 = f32[1,8]{1,0:T(1,128)S(1)} copy-done((f32[1,8]{1,0:T(1,128)S(1)}, f32[1,8]{1,0:T(1,128)}, u32[]{:S(2)}) %copy-start.18) | copy-done | bytes 56
  40.6 0.7 %copy-done.20 = f32[1,8]{1,0:T(1,128)S(1)} copy-done((f32[1,8]{1,0:T(1,128)S(1)}, f32[1,8]{1,0:T(1,128)}, u32[]{:S(2)}) %copy-start.20) | copy-done | bytes 56
  41.2 0.7 %copy-done.21 = s32[1,1,160]{2,1,0:T(1,128)S(1)} copy-done((s32[1,1,160]{2,1,0:T(1,128)S(1)}, s32[1,1,160]{2,1,0:T(1,128)}, u32[]{:S(2)}) %copy-start.21) | copy-done | bytes 664
  41.9 0.7 %copy-done.22 = s32[1,1,160]{2,1,0:T(1,128)S(1)} copy-done((s32[1,1,160]{2,1,0:T(1,128)S(1)}, s32[1,1,160]{2,1,0:T(1,128)}, u32[]{:S(2)}) %copy-start.22) | copy-done | bytes 664
  42.6 0.7 %copy-done.23 = f32[1,4]{1,0:T(1,128)S(1)} copy-done((f32[1,4]{1,0:T(1,128)S(1)}, f32[1,4]{1,0:T(1,128)}, u32[]{:S(2)}) %copy-start.23) | copy-done | bytes 40
  43.2 7.6 %forward.1 = (f32[64,8,128]{2,1,0:T(8,128)S(1)}, f32[64,128]{1,0:T(8,128)S(1)}, f32[64,128]{1,0:T(8,128)S(1)}, f32[32,128]{1,0:T(8,128)S(1)}, f32[256,128]{1,0:T...) custom-call(s32[1,160]{1,0:T(1,128)S(1)} %bitcast.52, f32[1,8]{1,0:T(1,128)S(1)} %copy-done.18, ...), custom_call_target="tpu_custom_call" | custom-call | tf_op jit(solution)/shard_map/forward/pallas_call | solution.py:691
  50.9 3.5 %all-to-all-start = ((f32[16,8,128]{2,1,0:T(8,128)}), f32[16,8,128]{2,1,0:T(8,128)S(1)}, u32[]{:S(2)}, u32[]{:S(2)}) async-start(f32[16,8,128]{2,1,0:T(8,128)} %get-tuple-element.41), calls=%async_computation | async-start | bytes 131072 | tf_op jit(solution)/shard_map/all_to_all | solution.py:721
  54.4 1.3 %prepare.1 = (f32[8,8192]{1,0:T(8,128)}, f32[4,8192]{1,0:T(4,128)}, f32[16,48,128]{2,1,0:T(8,128)S(1)}) custom-call(f32[8,8192]{1,0:T(8,128)} %get-tuple-element.25.fresh, f32[8,256]{1,0:T(8,128)S(1)} %get-tuple-element.37.ends_new, f32[64,8,128]{2,1,0:T(8,128)S(1)} %get-tuple-element.38.summed, ...), custom_call_target="tpu_custom_call", output_to_operand_aliasing={{0}: (0, {})} | custom-call | tf_op jit(solution)/shard_map/prepare/pallas_call | solution.py:722
  55.7 6.2 %all-to-all-done.arrived = f32[16,8,128]{2,1,0:T(8,128)S(1)} async-done(((f32[16,8,128]{2,1,0:T(8,128)}), f32[16,8,128]{2,1,0:T(8,128)S(1)}, u32[]{:S(2)}, u32[]{:S(2)}) %all-to-all-start) | async-done | bytes 65568 | tf_op jit(solution)/shard_map/all_to_all | solution.py:721
  61.9 1.6 %backward.1 = f32[64,128]{1,0:T(8,128)} custom-call(f32[16,8,128]{2,1,0:T(8,128)S(1)} %all-to-all-done.arrived, f32[16,48,128]{2,1,0:T(8,128)S(1)} %get-tuple-element.42.weights, f32[32,128]{1,0:T(8,128)S(1)} %get-tuple-element.43.source, f32[256,128]{1,0:T(8,128)S(1)} %get-tuple-element.44.frame, f32[64,128]{1,0:T(8,128)S(1)} %get-tuple-element.45.force, ...), custom_call_target="tpu_custom_call" | custom-call | tf_op jit(solution)/shard_map/backward/pallas_call | solution.py:739
  (25 shorter events, 0.0 us)
Async XLA Ops:
  0.6 61.3 %copy-start.8 = (s32[1,8192]{1,0:T(1,128)S(1)}, s32[1,8192]{1,0:T(1,128)}, u32[]{:S(2)}) copy-start(s32[1,8192]{1,0:T(1,128)} %param.27) | copy-start | bytes 98308
  0.6 53.7 %copy-start.12 = (f32[1,16,256]{2,1,0:T(8,128)S(1)}, f32[1,16,256]{2,1,0:T(8,128)}, u32[]{:S(2)}) copy-start(f32[1,16,256]{2,1,0:T(8,128)} %param.32) | copy-start | bytes 49156
  0.7 61.2 %copy-start.10 = (f32[1,8192]{1,0:T(1,128)S(1)}, f32[1,8192]{1,0:T(1,128)}, u32[]{:S(2)}) copy-start(f32[1,8192]{1,0:T(1,128)} %param.22) | copy-start | bytes 98308
  0.7 14.7 %collective-permute-start.1 = (s32[1,160]{1,0:T(1,128)}, s32[1,160]{1,0:T(1,128)S(1)}, u32[]{:S(2)}, u32[]{:S(2)}) collective-permute-start(s32[1,160]{1,0:T(1,128)} %bitcast.59), channel_id=1, source_target_pairs={{0,16},{16,0},{1,17},{17,1},{2,18},{18,2},{3,19},{19,3},{4,20},{20... | collective-permute-start | bytes 1928 | tf_op jit(solution)/shard_map/ppermute | solution.py:635
  1.2 14.2 %collective-permute-start = (bf16[4,8192]{1,0:T(4,128)(2,1)}, bf16[4,8192]{1,0:T(4,128)(2,1)S(1)}, u32[]{:S(2)}, u32[]{:S(2)}) collective-permute-start(bf16[4,8192]{1,0:T(4,128)(2,1)} %bitcast.58), channel_id=1, source_target_pairs={{0,16},{16,0},{1,17},{17,1},{2,18},{18,2},{3,19},{19,3},{4,20},{20... | collective-permute-start | bytes 196616 | tf_op jit(solution)/shard_map/ppermute | solution.py:634
  3.2 1.0 %copy-start = (f32[1,8,8192]{2,1,0:T(8,128)S(1)}, f32[1,8,8192]{2,1,0:T(8,128)}, u32[]{:S(2)}) copy-start(f32[1,8,8192]{2,1,0:T(8,128)} %param.19) | copy-start | bytes 786436
  4.1 0.8 %copy-start.3 = (f32[1,8192]{1,0:T(1,128)S(1)}, f32[1,8192]{1,0:T(1,128)}, u32[]{:S(2)}) copy-start(f32[1,8192]{1,0:T(1,128)} %param.24) | copy-start | bytes 98308
  4.9 0.8 %copy-start.6 = (s32[1,8192]{1,0:T(1,128)S(1)}, s32[1,8192]{1,0:T(1,128)}, u32[]{:S(2)}) copy-start(s32[1,8192]{1,0:T(1,128)} %param.27) | copy-start | bytes 98308
  5.7 0.7 %copy-start.17 = (f32[1,8]{1,0:T(1,128)S(1)}, f32[1,8]{1,0:T(1,128)}, u32[]{:S(2)}) copy-start(f32[1,8]{1,0:T(1,128)} %rate.3) | copy-start | bytes 100
  6.3 0.7 %copy-start.19 = (f32[1,8]{1,0:T(1,128)S(1)}, f32[1,8]{1,0:T(1,128)}, u32[]{:S(2)}) copy-start(f32[1,8]{1,0:T(1,128)} %level_weight.3) | copy-start | bytes 100
  15.4 1.0 %copy-start.1 = (f32[1,8,8192]{2,1,0:T(8,128)S(1)}, f32[1,8,8192]{2,1,0:T(8,128)}, u32[]{:S(2)}) copy-start(f32[1,8,8192]{2,1,0:T(8,128)} %param.19) | copy-start | bytes 786436
  16.3 0.8 %copy-start.4 = (f32[1,8192]{1,0:T(1,128)S(1)}, f32[1,8192]{1,0:T(1,128)}, u32[]{:S(2)}) copy-start(f32[1,8192]{1,0:T(1,128)} %param.24) | copy-start | bytes 98308
  17.1 0.8 %copy-start.7 = (s32[1,8192]{1,0:T(1,128)S(1)}, s32[1,8192]{1,0:T(1,128)}, u32[]{:S(2)}) copy-start(s32[1,8192]{1,0:T(1,128)} %param.27) | copy-start | bytes 98308
  17.8 0.7 %copy-start.11 = (f32[1,16,256]{2,1,0:T(8,128)S(1)}, f32[1,16,256]{2,1,0:T(8,128)}, u32[]{:S(2)}) copy-start(f32[1,16,256]{2,1,0:T(8,128)} %param.32) | copy-start | bytes 49156
  18.5 0.7 %copy-start.13 = (f32[1,1024]{1,0:T(1,128)S(1)}, f32[1,1024]{1,0:T(1,128)}, u32[]{:S(2)}) copy-start(f32[1,1024]{1,0:T(1,128)} %param.30) | copy-start | bytes 12292
  19.2 0.7 %copy-start.15 = (s32[1,1024]{1,0:T(1,128)S(1)}, s32[1,1024]{1,0:T(1,128)}, u32[]{:S(2)}) copy-start(s32[1,1024]{1,0:T(1,128)} %param.31) | copy-start | bytes 12292
  20.2 9.2 %collective-permute-start.4 = (bf16[128,128]{1,0:T(8,128)(2,1)S(1)}, bf16[128,128]{1,0:T(8,128)(2,1)S(1)}, u32[]{:S(2)}, u32[]{:S(2)}) collective-permute-start(bf16[128,128]{1,0:T(8,128)(2,1)S(1)} %get-tuple-element.28), channel_id=1, source_target_pairs={{0,2},{2,0},{1,3},{3,1},{4,6},{6,4},{5,7},{7,5},{8,10},{10,8},{9,1... | collective-permute-start | bytes 98312 | tf_op jit(solution)/shard_map/ppermute | solution.py:669
  23.2 6.6 %collective-permute-start.5 = (bf16[128,128]{1,0:T(8,128)(2,1)S(1)}, bf16[128,128]{1,0:T(8,128)(2,1)S(1)}, u32[]{:S(2)}, u32[]{:S(2)}) collective-permute-start(bf16[128,128]{1,0:T(8,128)(2,1)S(1)} %get-tuple-element.29), channel_id=1, source_target_pairs={{2,4},{4,2},{3,5},{5,3},{6,8},{8,6},{7,9},{9,7},{10,12},{12,10},{1... | collective-permute-start | bytes 98312 | tf_op jit(solution)/shard_map/ppermute | solution.py:667
  26.7 4.3 %collective-permute-start.2 = (bf16[256,128]{1,0:T(8,128)(2,1)S(1)}, bf16[256,128]{1,0:T(8,128)(2,1)S(1)}, u32[]{:S(2)}, u32[]{:S(2)}) collective-permute-start(bf16[256,128]{1,0:T(8,128)(2,1)S(1)} %get-tuple-element.26), channel_id=1, source_target_pairs={{0,1},{1,0},{2,3},{3,2},{4,5},{5,4},{6,7},{7,6},{8,9},{9,8},{10,11... | collective-permute-start | bytes 196616 | tf_op jit(solution)/shard_map/ppermute | solution.py:668
  28.2 7.9 %collective-permute-start.3 = (bf16[256,128]{1,0:T(8,128)(2,1)S(1)}, bf16[256,128]{1,0:T(8,128)(2,1)S(1)}, u32[]{:S(2)}, u32[]{:S(2)}) collective-permute-start(bf16[256,128]{1,0:T(8,128)(2,1)S(1)} %get-tuple-element.27), channel_id=1, source_target_pairs={{1,2},{2,1},{3,4},{4,3},{5,6},{6,5},{7,8},{8,7},{9,10},{10,9},{11,... | collective-permute-start | bytes 196616 | tf_op jit(solution)/shard_map/ppermute | solution.py:666
  36.1 1.0 %copy-start.2 = (f32[1,8,8192]{2,1,0:T(8,128)S(1)}, f32[1,8,8192]{2,1,0:T(8,128)}, u32[]{:S(2)}) copy-start(f32[1,8,8192]{2,1,0:T(8,128)} %param.19) | copy-start | bytes 786436
  37.0 0.8 %copy-start.5 = (f32[1,8192]{1,0:T(1,128)S(1)}, f32[1,8192]{1,0:T(1,128)}, u32[]{:S(2)}) copy-start(f32[1,8192]{1,0:T(1,128)} %param.24) | copy-start | bytes 98308
  37.8 0.8 %copy-start.9 = (f32[1,8192]{1,0:T(1,128)S(1)}, f32[1,8192]{1,0:T(1,128)}, u32[]{:S(2)}) copy-start(f32[1,8192]{1,0:T(1,128)} %param.22) | copy-start | bytes 98308
  38.5 0.7 %copy-start.14 = (f32[1,1024]{1,0:T(1,128)S(1)}, f32[1,1024]{1,0:T(1,128)}, u32[]{:S(2)}) copy-start(f32[1,1024]{1,0:T(1,128)} %param.30) | copy-start | bytes 12292
  39.2 0.7 %copy-start.16 = (s32[1,1024]{1,0:T(1,128)S(1)}, s32[1,1024]{1,0:T(1,128)}, u32[]{:S(2)}) copy-start(s32[1,1024]{1,0:T(1,128)} %param.31) | copy-start | bytes 12292
  39.9 0.7 %copy-start.18 = (f32[1,8]{1,0:T(1,128)S(1)}, f32[1,8]{1,0:T(1,128)}, u32[]{:S(2)}) copy-start(f32[1,8]{1,0:T(1,128)} %rate.3) | copy-start | bytes 100
  40.6 0.7 %copy-start.20 = (f32[1,8]{1,0:T(1,128)S(1)}, f32[1,8]{1,0:T(1,128)}, u32[]{:S(2)}) copy-start(f32[1,8]{1,0:T(1,128)} %level_weight.3) | copy-start | bytes 100
  41.2 0.7 %copy-start.21 = (s32[1,1,160]{2,1,0:T(1,128)S(1)}, s32[1,1,160]{2,1,0:T(1,128)}, u32[]{:S(2)}) copy-start(s32[1,1,160]{2,1,0:T(1,128)} %param.36) | copy-start | bytes 1924
  41.9 0.7 %copy-start.22 = (s32[1,1,160]{2,1,0:T(1,128)S(1)}, s32[1,1,160]{2,1,0:T(1,128)}, u32[]{:S(2)}) copy-start(s32[1,1,160]{2,1,0:T(1,128)} %param.35) | copy-start | bytes 1924
  42.6 0.7 %copy-start.23 = (f32[1,4]{1,0:T(1,128)S(1)}, f32[1,4]{1,0:T(1,128)}, u32[]{:S(2)}) copy-start(f32[1,4]{1,0:T(1,128)} %flux_weight.1) | copy-start | bytes 52
  50.9 11.0 %all-to-all-start = ((f32[16,8,128]{2,1,0:T(8,128)}), f32[16,8,128]{2,1,0:T(8,128)S(1)}, u32[]{:S(2)}, u32[]{:S(2)}) async-start(f32[16,8,128]{2,1,0:T(8,128)} %get-tuple-element.41), calls=%async_computation | async-start | bytes 131072 | tf_op jit(solution)/shard_map/all_to_all | solution.py:721

commit v2 on v1

--- a/solution.py
+++ b/solution.py
@@ -47,16 +47,27 @@
     return lax.dot_general(a, b, (((0,), (0,)), ((), ())), preferred_element_type=F32)
 
 
-def column_of(scalars, offset, count):
-    sublane = lax.broadcasted_iota(I32, (8, LANES), 0)
-    value = jnp.zeros((8, LANES), F32)
-    for level in range(count):
-        value = jnp.where(sublane == level, scalars[0, level], value)
-    return value
-
-
 def pick_base(inverse_blocks):
     return -(-(INVERSE + 32 * inverse_blocks) // 16) * 16
+
+
+def load_kernel(*refs):
+    count = (len(refs) - 2) // 2
+    sources, targets = refs[:count], refs[count : 2 * count]
+    scalars, sems = refs[2 * count :]
+    copies = [
+        pltpu.make_async_copy(source, target, sems.at[i])
+        for i, (source, target) in enumerate(zip(sources, targets))
+    ]
+    for copy in copies:
+        copy.start()
+    for copy in copies:
+        copy.wait()
+    for i, value in enumerate(targets[-3:]):
+        width = value.shape[1]
+        diagonal = lax.broadcasted_iota(I32, (8, width), 0) == lax.broadcasted_iota(I32, (8, width), 1)
+        column = jnp.sum(jnp.where(diagonal, wide(value[...]), 0.0), axis=1, keepdims=True)
+        scalars[pl.ds(8 * i, 8), :] = jnp.broadcast_to(column, (8, LANES))
 
 
 def pack_kernel(
@@ -68,8 +79,8 @@
     low = lax.rem(tile, 4) < 2
     cells = fields.shape[1]
     blocks = cells // LANES
-    firsts = ctable.shape[1]
-    frows = firsts // LANES
+    frows = ctable.shape[1]
+    firsts = frows * LANES
     base = pick_base(cinverse.shape[1] // LANES)
     lane = lax.broadcasted_iota(I32, (1, LANES), 1)
 
@@ -82,21 +93,23 @@
             rows[pl.ds(high, count), :] = value
             rows[pl.ds(low_row, count), :] = value - value.astype(BF16).astype(F32)
 
+        def three(ref, row):
+            return jnp.concatenate([ref[link, pl.ds(row, 1), :] for link in range(3)], axis=0)
+
         rows[pl.ds(24, 8), :] = jnp.zeros((8, LANES), F32)
         both(FIELD_HI, FIELD_LO, fields[:, part])
-        both(EDGE_HI, EDGE_LO, edge[:, part])
         block = 0 if at_left else blocks - 1
+        both(EDGE_HI, EDGE_LO, three(edge, block))
         both(OLD_HI, OLD_LO, old[pl.ds(block, 1), :])
-        rows[pl.ds(OFFSET, 3), :] = (table[:, part] - (LANES + start) - lane).astype(F32)
+        rows[pl.ds(OFFSET, 3), :] = (three(table, block) - (LANES + start) - lane).astype(F32)
         shift = 0 if at_left else firsts - LANES
         rows[pl.ds(OWNER, 1), :] = (owner[pl.ds(block, 1), :] - shift).astype(F32)
         first = 0 if at_left else frows - 2
         reach = LANES // 8
         for step in range(2):
-            cpart = pl.ds((first + step) * LANES, LANES)
-            both(CEDGE_HI + 3 * step, CEDGE_LO + 3 * step, cedge[:, cpart])
+            both(CEDGE_HI + 3 * step, CEDGE_LO + 3 * step, three(cedge, first + step))
             rows[pl.ds(COFFSET + 3 * step, 3), :] = (
-                ctable[:, cpart] - (reach + (first + step) * LANES) - lane
+                three(ctable, first + step) - (reach + (first + step) * LANES) - lane
             ).astype(F32)
             both(CDIAG_HI + step, CDIAG_LO + step, cdiag[pl.ds(first + step, 1), :])
             rows[pl.ds(COWNER + step, 1), :] = cowner[pl.ds(first + step, 1), :].astype(F32)
@@ -140,56 +153,53 @@
 
 
 def stencil_kernel(
-    rate, level_weight, fields, edge, table, old, owner,
-    fresh, force, beside_old, edges, window, ends_row, ends_lane, oldpad,
+    here, scalars, fields, edge, table, old, owner, slots, tiles,
+    fresh, force, beside_old, window, ends_row, ends_lane, hot, tile_buffer, padded, sem,
 ):
+    del here
+    load = pltpu.make_async_copy(tiles, tile_buffer, sem.at[0])
+    load.start()
     blocks = old.shape[0]
-    speed = column_of(rate, 0, fields.shape[0])
-    share = column_of(level_weight, 0, fields.shape[0])
-
-    def one(block, before, here, after):
-        part = pl.ds(pl.multiple_of(block * LANES, LANES), LANES)
-        weights = edge[:, part]
-        place = table[:, part] - block * LANES
+    levels = fields.shape[0]
+    speed = scalars[pl.ds(0, 8), :]
+    share = scalars[pl.ds(8, 8), :]
+    starts = lax.broadcasted_iota(I32, (blocks, LANES), 0) * LANES
+    total = edge[0] + edge[1] + edge[2]
+    inverse = 1.0 / total
+    for link in range(3):
+        window[link] = table[link] - starts
+    blank = jnp.zeros((levels, LANES), F32)
+
+    def chunk(block):
+        if 0 <= block < blocks:
+            return fields[:, pl.ds(block * LANES, LANES)]
+        return blank
+
+    before, here, after = blank, chunk(0), chunk(1)
+    for block in range(blocks):
+        row = slice(block, block + 1)
+        beside = jnp.zeros((levels, LANES), F32)
         for link in range(3):
-            edges[link, pl.ds(block, 1), :] = weights[link : link + 1]
-            window[link, pl.ds(block, 1), :] = place[link : link + 1]
-        total = weights[0:1] + weights[1:2] + weights[2:3]
-        inverse = 1.0 / total
-        lanes = lax.bitwise_and(place, LANES - 1)
-        which = lax.shift_right_logical(place, 7)
-        beside = jnp.zeros((8, LANES), F32)
-        for link in range(3):
-            index = wide(lanes[link : link + 1])
-            row = wide(which[link : link + 1])
+            place = wide(window[link, pl.ds(block, 1), :])
+            index = lax.bitwise_and(place, LANES - 1)
             value = jnp.where(
-                row == 1,
-                gather_lanes(here, index),
-                jnp.where(row == 0, gather_lanes(before, index), gather_lanes(after, index)),
+                place < LANES,
+                gather_lanes(before, index),
+                jnp.where(place < 2 * LANES, gather_lanes(here, index), gather_lanes(after, index)),
             )
-            beside = beside + wide(weights[link : link + 1]) * value
-        result = here + speed * (beside - wide(total) * here) * wide(inverse)
-        fresh[:, part] = result
+            beside = beside + wide(edge[link, pl.ds(block, 1), :]) * value
+        result = here + speed * ((beside - wide(total[row]) * here) * wide(inverse[row]))
+        fresh[:, pl.ds(block * LANES, LANES)] = result
         force[pl.ds(block, 1), :] = jnp.sum(result * share, axis=0, keepdims=True)
-
-    blank = jnp.zeros((8, LANES), F32)
-
-    def chunk(block):
-        return fields[:, pl.ds(pl.multiple_of(block * LANES, LANES), LANES)]
-
-    one(0, blank, chunk(0), chunk(1))
-
-    def step(block, carry):
-        one(block, chunk(block - 1), chunk(block), chunk(block + 1))
-        return carry
-
-    lax.fori_loop(1, blocks - 1, step, 0, unroll=2)
-    one(blocks - 1, chunk(blocks - 2), chunk(blocks - 1), blank)
-
-    oldpad[pl.ds(0, 8), :] = blank
-    oldpad[pl.ds(8 + blocks, 8), :] = blank
-    oldpad[pl.ds(8, blocks), :] = old[...]
-    beside_old[...] = neighbour_sum(oldpad, edges, window, blocks)
+        before, here, after = here, after, chunk(block + 2)
+
+    padded[pl.ds(0, 8), :] = jnp.zeros((8, LANES), F32)
+    padded[pl.ds(8 + blocks, 8), :] = jnp.zeros((8, LANES), F32)
+    padded[pl.ds(8, blocks), :] = old[...]
+    beside_old[...] = neighbour_sum(padded, edge, window, blocks)
+    hot[...] = jnp.where(
+        lax.broadcasted_iota(I32, hot.shape, 0) == slots[...], 1.0, 0.0
+    ).astype(BF16)
 
     firsts = ends_row.shape[0] * LANES
     ident = lax.broadcasted_iota(I32, ends_row.shape, 0) * LANES + lax.broadcasted_iota(
@@ -211,6 +221,7 @@
         lanes = jnp.where(value <= ident, lanes + bit, lanes)
     ends_row[...] = rows
     ends_lane[...] = lanes
+    load.wait()
 
 
 def neighbour_sum(padded, edges, window, blocks):
@@ -221,11 +232,10 @@
     for link in range(3):
         place = window[link]
         index = lax.bitwise_and(place, LANES - 1)
-        row = lax.shift_right_logical(place, 7)
         value = jnp.where(
-            row == 1,
-            gather_lanes(here, index),
-            jnp.where(row == 0, gather_lanes(before, index), gather_lanes(after, index)),
+            place < LANES,
+            gather_lanes(before, index),
+            jnp.where(place < 2 * LANES, gather_lanes(here, index), gather_lanes(after, index)),
         )
         result = result + edges[link] * value
     return result
@@ -276,31 +286,19 @@
 
 
 def forward_kernel(
-    entry_block, rate, level_weight, flux_weight,
-    tiles, near1, far1, near2, far2, here, slots, fields, edges, window, old, diagonal,
-    force_part, beside_old, ends_row, ends_lane, fresh_ends,
-    ctable, cedge, cdiag, cowner,
+    entry_block_any, tiles, scalars, near1, far1, near2, far2, here, hot, fields, edges, window, old,
+    diagonal, force_part, beside_old, ends_row, ends_lane, fresh, ctable, cedge, cdiag, cowner,
     summed, force_out, smooth_out, source_out, frame, ends_out, message,
-    tile_buffer, picked, padded, prefixed, totals, arrivals, sems,
+    entry_block, picked, padded, prefixed, totals, arrivals, sem,
 ):
+    fetch = pltpu.make_async_copy(entry_block_any, entry_block, sem.at[0])
+    fetch.start()
     tile = lax.axis_index("tile")
     tile_count = lax.axis_size("tile")
     even = lax.rem(tile, 2) == 0
     low = lax.rem(tile, 4) < 2
     entries = tiles.shape[0]
     blocks = old.shape[0]
-    parts = sems.shape[0]
-    step = entries // parts
-
-    def load(part):
-        return pltpu.make_async_copy(
-            tiles.at[pl.ds(part * step, step)],
-            tile_buffer.at[pl.ds(part * step, step)],
-            sems.at[part],
-        )
-
-    for part in range(parts):
-        load(part).start()
 
     base = near1.shape[0] - near2.shape[0]
     near, far = near1[...], far1[...]
@@ -310,38 +308,31 @@
     j0 = jnp.where(low, two_far, two_near)
     j4 = jnp.where(low, two_near, two_far)
     j1, j3, j2 = from_left[base:], from_right[base:], here[...]
-    slot_count = slots.shape[1]
     each = j0.shape[0] // 4
-    hot = jnp.where(
-        lax.broadcasted_iota(I32, (slot_count, entries), 0) == slots[...], 1.0, 0.0
-    ).astype(BF16)
     for channel in range(4):
         span = slice(channel * each, (channel + 1) * each)
         source = jnp.concatenate([j[span] for j in (j0, j1, j2, j3, j4)], axis=0)
-        picked[pl.ds(channel, entries, stride=4), :] = dot_tn(hot, source)
+        picked[pl.ds(channel, entries, stride=4), :] = dot_tn(hot[...], source)
 
     arrivals[0] = from_left[:base].astype(F32)
     arrivals[1] = from_right[:base].astype(F32)
 
     summed[...] = jnp.zeros(summed.shape, F32)
-    for part in range(parts):
-        load(part).wait()
-
-        def pair(number, carry):
-            entry = part * step + 2 * number
-            rows = picked[pl.ds(pl.multiple_of(4 * entry, 8), 8), :].astype(BF16)
-            first = dot_nt(rows, tile_buffer[entry])
-            second = dot_nt(rows, tile_buffer[entry + 1])
-            at = entry_block[0, entry]
-            summed[at, pl.ds(0, 4), :] += first[0:4]
-            at = entry_block[0, entry + 1]
-            summed[at, pl.ds(4, 4), :] += second[4:8]
-            return carry
-
-        lax.fori_loop(0, step // 2, pair, 0, unroll=8)
-
-    speed = column_of(rate, 0, fields.shape[0])
-    share = column_of(level_weight, 0, fields.shape[0])
+    fetch.wait()
+
+    def pair(number, carry):
+        entry = 2 * number
+        rows = picked[pl.ds(pl.multiple_of(4 * entry, 8), 8), :].astype(BF16)
+        first = dot_nt(rows, tiles[entry])
+        second = dot_nt(rows, tiles[entry + 1])
+        summed[entry_block[0, entry], pl.ds(0, 4), :] += first[0:4]
+        summed[entry_block[0, entry + 1], pl.ds(4, 4), :] += second[4:8]
+        return carry
+
+    lax.fori_loop(0, entries // 2, pair, 0, unroll=8)
+
+    speed = scalars[pl.ds(0, 8), :]
+    share = scalars[pl.ds(8, 8), :]
     force_out[...] = force_part[...]
     padded[pl.ds(0, 8), :] = jnp.zeros((8, LANES), F32)
     padded[pl.ds(8 + blocks, 8), :] = jnp.zeros((8, LANES), F32)
@@ -361,14 +352,14 @@
             extra = extra + weight * gather_lanes(halo, index)
             extra_old = extra_old + weight * gather_lanes(wide(halo_old), index)
         change = speed * extra / wide(total)
-        ends_out[:, pl.ds(side * LANES, LANES)] = fresh_ends[:, pl.ds(side * LANES, LANES)] + change
+        ends_out[:, pl.ds(side * LANES, LANES)] = fresh[:, pl.ds(block * LANES, LANES)] + change
         force_out[pl.ds(block, 1), :] += jnp.sum(change * share, axis=0, keepdims=True)
         beside_extra.append(extra_old[0:1])
 
     force = force_out[...]
     for channel in range(4):
         value = summed[:, channel, :] + summed[:, channel + 4, :]
-        force = force + flux_weight[0, channel] * value
+        force = force + scalars[pl.ds(16 + channel, 1), :] * value
     force_out[...] = force
     total = diagonal[...] + edges[0] + edges[1] + edges[2]
     smooth_out[...] = beside_old[...]
@@ -436,13 +427,12 @@
     frame[pl.ds(6 * FRAME, FRAME), :] = jnp.ones((FRAME, LANES), F32)
     frame[pl.ds(7 * FRAME, FRAME), :] = jnp.full((FRAME, LANES), 127.0, F32)
     bottoms = 16
-    for row in range(frows):
-        part = pl.ds(row * LANES, LANES)
-        offsets = (ctable[:, part] - (reach + row * LANES) - lane).astype(F32)
-        weights = cedge[:, part]
-        for link in range(3):
-            frame[pl.ds(link * FRAME + OWN + row, 1), :] = offsets[link : link + 1]
-            frame[pl.ds((3 + link) * FRAME + OWN + row, 1), :] = weights[link : link + 1]
+    at_cell = lax.broadcasted_iota(I32, (frows, LANES), 0) * LANES + lax.broadcasted_iota(
+        I32, (frows, LANES), 1
+    )
+    for link in range(3):
+        frame[pl.ds(link * FRAME + OWN, frows), :] = (ctable[link] - reach - at_cell).astype(F32)
+        frame[pl.ds((3 + link) * FRAME + OWN, frows), :] = cedge[link]
     frame[pl.ds(6 * FRAME + OWN, frows), :] = cdiag[...]
     frame[pl.ds(7 * FRAME + OWN, frows), :] = (cowner[...] + bottoms).astype(F32)
     for side in range(2):
@@ -493,7 +483,6 @@
 def prepare_kernel(
     fresh, ends_new, summed, near1, far1, cinverse, fresh_out, received, weights, sem, extended
 ):
-    del fresh
     tile = lax.axis_index("tile")
     even = lax.rem(tile, 2) == 0
     cells = fresh_out.shape[1]
@@ -505,6 +494,8 @@
         )
         for side in range(2)
     ]
+    middle = pl.ds(LANES, cells - 2 * LANES)
+    copies.append(pltpu.make_async_copy(fresh.at[:, middle], fresh_out.at[:, middle], sem.at[2]))
     for copy in copies:
         copy.start()
     blocks = summed.shape[0]
@@ -591,13 +582,17 @@
     height[...] = corrected + RELAXATION * (force[...] - (fine_total * corrected - beside)) / fine_total
 
 
+def in_hbm(array):
+    return pltpu.with_memory_space_constraint(array, pltpu.HBM)
+
+
 def struct(shape, dtype=F32):
     return jax.ShapeDtypeStruct(shape, dtype)
 
 
 VMEM = pl.BlockSpec(memory_space=pltpu.VMEM)
 SMEM = pl.BlockSpec(memory_space=pltpu.SMEM)
-ANY = pl.BlockSpec(memory_space=pl.ANY)
+ANY = pl.BlockSpec(memory_space=pltpu.HBM)
 PARAMS = pltpu.CompilerParams(vmem_limit_bytes=48 * 1024 * 1024)
 
 
@@ -633,11 +628,34 @@
     swap = [(0, 1), (1, 0)]
     surface = lax.ppermute(surface_out[0], "comp", swap)
     sends = lax.ppermute(send_blocks[0], "comp", swap)
-    old = old_height.reshape(blocks, LANES)
-    owner = fine_owner.reshape(blocks, LANES)
-    diagonal = fine_diagonal.reshape(blocks, LANES)
-    cdiag = coarse_diagonal.reshape(frows, LANES)
-    cowner = coarse_owner.reshape(frows, LANES)
+    raw = (
+        fields[0],
+        old_height.reshape(blocks, LANES),
+        edge_weight[0].reshape(3, blocks, LANES),
+        fine_table[0].reshape(3, blocks, LANES),
+        fine_owner.reshape(blocks, LANES),
+        fine_diagonal.reshape(blocks, LANES),
+        coarse_table[0].reshape(3, frows, LANES),
+        coarse_edge[0].reshape(3, frows, LANES),
+        coarse_diagonal.reshape(frows, LANES),
+        coarse_owner.reshape(frows, LANES),
+        coarse_inverse[0],
+        entry_slot[0],
+        level_rate,
+        level_weight,
+        flux_weight,
+    )
+    loaded = pl.pallas_call(
+        load_kernel,
+        out_shape=[struct(x.shape, x.dtype) for x in raw] + [struct((24, LANES))],
+        in_specs=[ANY] * len(raw),
+        out_specs=[VMEM] * (len(raw) + 1),
+        scratch_shapes=[pltpu.SemaphoreType.DMA((len(raw),))],
+        compiler_params=PARAMS,
+        name="load",
+    )(*[in_hbm(x) for x in raw])
+    current, old, edges, table, owner, diagonal, ctable, cedge, cdiag, cowner, cinverse, slot = loaded[:12]
+    scalars = loaded[-1]
 
     near1, far1, near2, far2, here = pl.pallas_call(
         pack_kernel,
@@ -658,8 +676,7 @@
         compiler_params=PARAMS,
         name="pack",
     )(
-        surface, sends, fields[0], old, edge_weight[0], fine_table[0], owner,
-        coarse_table[0], coarse_edge[0], cdiag, cowner, coarse_inverse[0],
+        surface, sends, current, old, edges, table, owner, ctable, cedge, cdiag, cowner, cinverse,
     )
     one_a, one_b = pair_up(tile_count, 1)
     two_a, two_b = pair_up(tile_count, 2)
@@ -668,26 +685,25 @@
     near1 = lax.ppermute(near1, "tile", one_a)
     near2 = lax.ppermute(near2, "tile", two_a)
 
-    fresh, force_part, beside_old, edges, window, ends_row, ends_lane = pl.pallas_call(
+    fresh, force_part, beside_old, window, ends_row, ends_lane, hot, tiles = pl.pallas_call(
         stencil_kernel,
         out_shape=[
             struct((fields.shape[1], cells)),
             struct((blocks, LANES)),
             struct((blocks, LANES)),
-            struct((3, blocks, LANES)),
             struct((3, blocks, LANES), I32),
             struct((frows, LANES), I32),
             struct((frows, LANES), I32),
+            struct((slots, entries), BF16),
+            struct(remap_tiles.shape[2:], BF16),
         ],
-        in_specs=[SMEM, SMEM] + [VMEM] * 5,
-        out_specs=[VMEM] * 7,
-        scratch_shapes=[pltpu.VMEM((blocks + 16, LANES), F32)],
+        in_specs=[VMEM] * 8 + [ANY],
+        out_specs=[VMEM] * 8,
+        scratch_shapes=[pltpu.VMEM((blocks + 16, LANES), F32), pltpu.SemaphoreType.DMA((1,))],
         compiler_params=PARAMS,
         name="stencil",
-    )(level_rate, level_weight, fields[0], edge_weight[0], fine_table[0], old, owner)
-    fresh_ends = jnp.concatenate([fresh[:, :LANES], fresh[:, cells - LANES :]], axis=1)
-
-    parts = 5
+    )(here, scalars, current, edges, table, old, owner, slot, in_hbm(remap_tiles[0, 0]))
+
     summed, force, smooth, source, frame, ends_new, message = pl.pallas_call(
         forward_kernel,
         out_shape=[
@@ -699,24 +715,22 @@
             struct((fields.shape[1], 2 * LANES)),
             struct((tile_count, 8, LANES)),
         ],
-        in_specs=[SMEM] * 4 + [ANY] + [VMEM] * 20,
+        in_specs=[ANY] + [VMEM] * 22,
         out_specs=[VMEM] * 7,
         scratch_shapes=[
-            pltpu.VMEM((entries, LANES, LANES), BF16),
+            pltpu.SMEM((1, entries), I32),
             pltpu.VMEM((4 * entries, LANES), F32),
             pltpu.VMEM((blocks + 16, LANES), F32),
             pltpu.VMEM((blocks, LANES), F32),
             pltpu.VMEM((blocks, LANES), F32),
             pltpu.VMEM((2, base, LANES), F32),
-            pltpu.SemaphoreType.DMA((parts,)),
+            pltpu.SemaphoreType.DMA((1,)),
         ],
         compiler_params=PARAMS,
         name="forward",
     )(
-        entry_block[0], level_rate, level_weight, flux_weight,
-        remap_tiles[0, 0], near1, far1, near2, far2, here, entry_slot[0], fields[0], edges, window,
-        old, diagonal, force_part, beside_old, ends_row, ends_lane, fresh_ends,
-        coarse_table[0], coarse_edge[0], cdiag, cowner,
+        in_hbm(entry_block[0]), tiles, scalars, near1, far1, near2, far2, here, hot, current, edges, window, old,
+        diagonal, force_part, beside_old, ends_row, ends_lane, fresh, ctable, cedge, cdiag, cowner,
     )
     arrived = lax.all_to_all(message, "tile", split_axis=0, concat_axis=0, tiled=True)
     advanced, received, weights = pl.pallas_call(
@@ -726,16 +740,15 @@
             struct((channels, cells)),
             struct((tile_count, 3 * bottoms, LANES)),
         ],
-        in_specs=[ANY] + [VMEM] * 5,
+        in_specs=[VMEM] * 6,
         out_specs=[ANY, VMEM, VMEM],
         scratch_shapes=[
-            pltpu.SemaphoreType.DMA((2,)),
+            pltpu.SemaphoreType.DMA((3,)),
             pltpu.VMEM((3 * bottoms, bottoms * tile_count), F32),
         ],
-        input_output_aliases={0: 0},
         compiler_params=PARAMS,
         name="prepare",
-    )(fresh, ends_new, summed, near1, far1, coarse_inverse[0])
+    )(fresh, ends_new, summed, near1, far1, cinverse)
     height = pl.pallas_call(
         functools.partial(backward_kernel, frows),
         out_shape=struct((blocks, LANES)),

time: 64.6 us -> 42.4 us (0.66); the launches traced: 63.5 us -> 42.1 us
  local copies, waits for them, and re-layouts: 19.5 us -> 0 us
  waiting for transfers between devices: 12.9 us -> 6.15 us
  Pallas kernels: 16.9 us -> 21 us
  starting transfers between devices: 13.3 us -> 14.2 us
    unnamed x52 -> x0, local copies, waits for them, and re-layouts: 18.8 us -> none
    ppermute x1, waiting for transfers between devices: 5.09 us -> 0.01 us  [per_device(): far1 = lax.ppermute(far1, 'tile', one_b)]
    ppermute x1, starting transfers between devices: 1.15 us -> 4.53 us  [per_device(): far1 = lax.ppermute(far1, 'tile', one_b)]
    ppermute x1, starting transfers between devices: 3.01 us -> 0.01 us  [per_device(): near2 = lax.ppermute(near2, 'tile', two_a)]
    pallas_call x0 -> x1, Pallas kernels: none -> 1.7 us  [per_device(): pl.pallas_call(load_kernel, out_shape=[struct(x.shape, x.dtype) for x in...]
    ppermute x1, starting transfers between devices: 3.55 us -> 1.91 us  [per_device(): far2 = lax.ppermute(far2, 'tile', two_b)]
    ppermute x1, starting transfers between devices: 1.49 us -> 2.99 us  [per_device(): near1 = lax.ppermute(near1, 'tile', one_a)]
    pallas_call x1, Pallas kernels: 7.62 us -> 8.96 us  [per_device(): pl.pallas_call(forward_kernel, out_shape=[struct((blocks, 8, LANES)), str...]
  transfers between devices with their start and end apart: 7 -> 7, of which waited for: 4 -> 1; matrix products, arithmetic and copies ran while one was open for 6% -> 0% of each run, Pallas kernels for 12% -> 24%
where the time goes in v2:
time: 42.4 us; the launch traced here: 42.1 us
  Pallas kernels  21 us (50%)
  starting transfers between devices  14.2 us (33%)
  waiting for transfers between devices  6.15 us (15%)
  between operations  0.73 us (2%)
    pallas_call x1, Pallas kernels, per_device(): pl.pallas_call(forward_kernel, out_shape=[struct((blocks, 8, LANES)), str...  8.96 us
    pallas_call x1, Pallas kernels, per_device(): pl.pallas_call(stencil_kernel, out_shape=[struct((fields.shape[1], cells)...  7.09 us
    all_to_all x1, waiting for transfers between devices, per_device(): lax.all_to_all(message, 'tile', split_axis=0, concat_axis=0, tiled=True)  6.13 us
    ppermute x1, starting transfers between devices, per_device(): far1 = lax.ppermute(far1, 'tile', one_b)  4.53 us
    all_to_all x1, starting transfers between devices, per_device(): lax.all_to_all(message, 'tile', split_axis=0, concat_axis=0, tiled=True)  4.21 us
    ppermute x1, starting transfers between devices, per_device(): near1 = lax.ppermute(near1, 'tile', one_a)  2.99 us
    ppermute x1, starting transfers between devices, per_device(): far2 = lax.ppermute(far2, 'tile', two_b)  1.91 us
    pallas_call x1, Pallas kernels, per_device(): pl.pallas_call(load_kernel, out_shape=[struct(x.shape, x.dtype) for x in...  1.7 us
  transfers between devices with their start and end apart: 7, of which 1 were waited for; matrix products, arithmetic and copies ran while one was open for 0% of the time, Pallas kernels for 24%

profile of v2, /device:TPU:0, one launch (start us, length us, event | category | flops | bytes accessed | tf_op | source)
XLA Modules:
  0.0 42.1 jit_solution(14581955295134492012)
XLA Ops:
  0.6 0.5 %collective-permute-start = (bf16[4,8192]{1,0:T(4,128)(2,1)}, bf16[4,8192]{1,0:T(4,128)(2,1)S(1)}, u32[]{:S(2)}, u32[]{:S(2)}) collective-permute-start(bf16[4,8192]{1,0:T(4,128)(2,1)} %bitcast.36), channel_id=1, source_target_pairs={{0,16},{16,0},{1,17},{17,1},{2,18},{18,2},{3,19},{19,3},{4,20},{20... | collective-permute-start | bytes 196616 | tf_op jit(solution)/shard_map/ppermute | solution.py:629
  1.2 0.1 collective-permute-start.1
  1.2 1.7 %load.1 = (f32[8,8192]{1,0:T(8,128)S(1)}, f32[64,128]{1,0:T(8,128)S(1)}, f32[3,64,128]{2,1,0:T(8,128)S(1)}, s32[3,64,128]{2,1,0:T(8,128)S(1)}, s32[64,128]{1,0:T...) custom-call(f32[8,8192]{1,0:T(8,128)} %bitcast.20, ...), custom_call_target="tpu_custom_call" | custom-call | tf_op jit(solution)/shard_map/load/pallas_call | solution.py:648
  2.9 0.0 collective-permute-done.1.sends
  3.0 0.0 collective-permute-done.surface
  3.0 0.3 pack.1
  3.2 3.0 %collective-permute-start.2 = (bf16[256,128]{1,0:T(8,128)(2,1)S(1)}, bf16[256,128]{1,0:T(8,128)(2,1)S(1)}, u32[]{:S(2)}, u32[]{:S(2)}) collective-permute-start(bf16[256,128]{1,0:T(8,128)(2,1)S(1)} %get-tuple-element.54), channel_id=1, source_target_pairs={{0,1},{1,0},{2,3},{3,2},{4,5},{5,4},{6,7},{7,6},{8,9},{9,8},{10,11... | collective-permute-start | bytes 196616 | tf_op jit(solution)/shard_map/ppermute | solution.py:685
  6.2 4.5 %collective-permute-start.3 = (bf16[256,128]{1,0:T(8,128)(2,1)S(1)}, bf16[256,128]{1,0:T(8,128)(2,1)S(1)}, u32[]{:S(2)}, u32[]{:S(2)}) collective-permute-start(bf16[256,128]{1,0:T(8,128)(2,1)S(1)} %get-tuple-element.55), channel_id=1, source_target_pairs={{1,2},{2,1},{3,4},{4,3},{5,6},{6,5},{7,8},{8,7},{9,10},{10,9},{11,... | collective-permute-start | bytes 196616 | tf_op jit(solution)/shard_map/ppermute | solution.py:683
  10.7 0.0 collective-permute-start.4
  10.7 1.9 %collective-permute-start.5 = (bf16[128,128]{1,0:T(8,128)(2,1)S(1)}, bf16[128,128]{1,0:T(8,128)(2,1)S(1)}, u32[]{:S(2)}, u32[]{:S(2)}) collective-permute-start(bf16[128,128]{1,0:T(8,128)(2,1)S(1)} %get-tuple-element.57), channel_id=1, source_target_pairs={{2,4},{4,2},{3,5},{5,3},{6,8},{8,6},{7,9},{9,7},{10,12},{12,10},{1... | collective-permute-start | bytes 98312 | tf_op jit(solution)/shard_map/ppermute | solution.py:684
  12.7 7.1 %stencil.1 = (f32[8,8192]{1,0:T(8,128)S(1)}, f32[64,128]{1,0:T(8,128)S(1)}, f32[64,128]{1,0:T(8,128)S(1)}, s32[3,64,128]{2,1,0:T(8,128)S(1)}, s32[8,128]{1,0:T(8...) custom-call(bf16[128,128]{1,0:T(8,128)(2,1)S(1)} %get-tuple-element.49.here, ...), custom_call_target="tpu_custom_call" | custom-call | tf_op jit(solution)/shard_map/stencil/pallas_call | solution.py:688
  19.8 0.0 collective-permute-done.4.near2
  19.8 0.0 collective-permute-done.5.far2
  19.8 0.0 collective-permute-done.2.near1
  19.8 0.0 collective-permute-done.3.far1
  19.8 9.0 %forward.1 = (f32[64,8,128]{2,1,0:T(8,128)S(1)}, f32[64,128]{1,0:T(8,128)S(1)}, f32[64,128]{1,0:T(8,128)S(1)}, f32[32,128]{1,0:T(8,128)S(1)}, f32[256,128]{1,0:T...) custom-call(s32[1,160]{1,0:T(1,128)} %bitcast.33, bf16[160,128,128]{2,1,0:T(8,128)(2,1)} %get-tuple-element.53.tiles, ...), custom_call_target="tpu_custom_call" | custom-call | tf_op jit(solution)/shard_map/forward/pallas_call | solution.py:707
  28.8 4.2 %all-to-all-start = ((f32[16,8,128]{2,1,0:T(8,128)}), f32[16,8,128]{2,1,0:T(8,128)S(1)}, u32[]{:S(2)}, u32[]{:S(2)}) async-start(f32[16,8,128]{2,1,0:T(8,128)} %get-tuple-element.69), calls=%async_computation | async-start | bytes 131072 | tf_op jit(solution)/shard_map/all_to_all | solution.py:735
  33.0 1.4 %prepare.1 = (f32[8,8192]{1,0:T(8,128)}, f32[4,8192]{1,0:T(4,128)}, f32[16,48,128]{2,1,0:T(8,128)S(1)}) custom-call(f32[8,8192]{1,0:T(8,128)S(1)} %get-tuple-element.52.fresh, f32[8,256]{1,0:T(8,128)S(1)} %get-tuple-element.65.ends_new, f32[64,8,128]{2,1,0:T(8,128)S(1)} %get-tuple-element.66.summed, bf16[256,128]{1,0:T(8,128)(2,1)S(1)} %collective-permute-done.2.near1, ...), custom_call_target="tpu_custom_call" | custom-call | tf_op jit(solution)/shard_map/prepare/pallas_call | solution.py:736
  34.4 6.1 %all-to-all-done.arrived = f32[16,8,128]{2,1,0:T(8,128)S(1)} async-done(((f32[16,8,128]{2,1,0:T(8,128)}), f32[16,8,128]{2,1,0:T(8,128)S(1)}, u32[]{:S(2)}, u32[]{:S(2)}) %all-to-all-start) | async-done | bytes 65568 | tf_op jit(solution)/shard_map/all_to_all | solution.py:735
  40.5 1.6 %backward.1 = f32[64,128]{1,0:T(8,128)} custom-call(f32[16,8,128]{2,1,0:T(8,128)S(1)} %all-to-all-done.arrived, f32[16,48,128]{2,1,0:T(8,128)S(1)} %get-tuple-element.70.weights, f32[32,128]{1,0:T(8,128)S(1)} %get-tuple-element.71.source, f32[256,128]{1,0:T(8,128)S(1)} %get-tuple-element.72.frame, f32[64,128]{1,0:T(8,128)S(1)} %get-tuple-element.73.force, ...), custom_call_target="tpu_custom_call" | custom-call | tf_op jit(solution)/shard_map/backward/pallas_call | solution.py:752
Async XLA Ops:
  0.6 2.3 %collective-permute-start = (bf16[4,8192]{1,0:T(4,128)(2,1)}, bf16[4,8192]{1,0:T(4,128)(2,1)S(1)}, u32[]{:S(2)}, u32[]{:S(2)}) collective-permute-start(bf16[4,8192]{1,0:T(4,128)(2,1)} %bitcast.36), channel_id=1, source_target_pairs={{0,16},{16,0},{1,17},{17,1},{2,18},{18,2},{3,19},{19,3},{4,20},{20... | collective-permute-start | bytes 196616 | tf_op jit(solution)/shard_map/ppermute | solution.py:629
  1.2 1.8 %collective-permute-start.1 = (s32[1,160]{1,0:T(1,128)}, s32[1,160]{1,0:T(1,128)S(1)}, u32[]{:S(2)}, u32[]{:S(2)}) collective-permute-start(s32[1,160]{1,0:T(1,128)} %bitcast.37), channel_id=1, source_target_pairs={{0,16},{16,0},{1,17},{17,1},{2,18},{18,2},{3,19},{19,3},{4,20},{20... | collective-permute-start | bytes 1928 | tf_op jit(solution)/shard_map/ppermute | solution.py:630
  3.2 16.6 %collective-permute-start.2 = (bf16[256,128]{1,0:T(8,128)(2,1)S(1)}, bf16[256,128]{1,0:T(8,128)(2,1)S(1)}, u32[]{:S(2)}, u32[]{:S(2)}) collective-permute-start(bf16[256,128]{1,0:T(8,128)(2,1)S(1)} %get-tuple-element.54), channel_id=1, source_target_pairs={{0,1},{1,0},{2,3},{3,2},{4,5},{5,4},{6,7},{7,6},{8,9},{9,8},{10,11... | collective-permute-start | bytes 196616 | tf_op jit(solution)/shard_map/ppermute | solution.py:685
  6.2 13.6 %collective-permute-start.3 = (bf16[256,128]{1,0:T(8,128)(2,1)S(1)}, bf16[256,128]{1,0:T(8,128)(2,1)S(1)}, u32[]{:S(2)}, u32[]{:S(2)}) collective-permute-start(bf16[256,128]{1,0:T(8,128)(2,1)S(1)} %get-tuple-element.55), channel_id=1, source_target_pairs={{1,2},{2,1},{3,4},{4,3},{5,6},{6,5},{7,8},{8,7},{9,10},{10,9},{11,... | collective-permute-start | bytes 196616 | tf_op jit(solution)/shard_map/ppermute | solution.py:683
  10.7 9.0 %collective-permute-start.4 = (bf16[128,128]{1,0:T(8,128)(2,1)S(1)}, bf16[128,128]{1,0:T(8,128)(2,1)S(1)}, u32[]{:S(2)}, u32[]{:S(2)}) collective-permute-start(bf16[128,128]{1,0:T(8,128)(2,1)S(1)} %get-tuple-element.56), channel_id=1, source_target_pairs={{0,2},{2,0},{1,3},{3,1},{4,6},{6,4},{5,7},{7,5},{8,10},{10,8},{9,1... | collective-permute-start | bytes 98312 | tf_op jit(solution)/shard_map/ppermute | solution.py:686
  10.7 9.0 %collective-permute-start.5 = (bf16[128,128]{1,0:T(8,128)(2,1)S(1)}, bf16[128,128]{1,0:T(8,128)(2,1)S(1)}, u32[]{:S(2)}, u32[]{:S(2)}) collective-permute-start(bf16[128,128]{1,0:T(8,128)(2,1)S(1)} %get-tuple-element.57), channel_id=1, source_target_pairs={{2,4},{4,2},{3,5},{5,3},{6,8},{8,6},{7,9},{9,7},{10,12},{12,10},{1... | collective-permute-start | bytes 98312 | tf_op jit(solution)/shard_map/ppermute | solution.py:684
  28.8 11.7 %all-to-all-start = ((f32[16,8,128]{2,1,0:T(8,128)}), f32[16,8,128]{2,1,0:T(8,128)S(1)}, u32[]{:S(2)}, u32[]{:S(2)}) async-start(f32[16,8,128]{2,1,0:T(8,128)} %get-tuple-element.69), calls=%async_computation | async-start | bytes 131072 | tf_op jit(solution)/shard_map/all_to_all | solution.py:735

commit v3 on v2

--- a/solution.py
+++ b/solution.py
@@ -1,4 +1,5 @@
 import functools
+import math
 
 import jax
 import jax.numpy as jnp
@@ -53,17 +54,17 @@
 
 def load_kernel(*refs):
     count = (len(refs) - 2) // 2
-    sources, targets = refs[:count], refs[count : 2 * count]
-    scalars, sems = refs[2 * count :]
+    sources, kept, scalars = refs[:count], refs[count : 2 * count - 3], refs[2 * count - 3]
+    spread, sems = refs[2 * count - 2 : 2 * count + 1], refs[2 * count + 1]
     copies = [
         pltpu.make_async_copy(source, target, sems.at[i])
-        for i, (source, target) in enumerate(zip(sources, targets))
+        for i, (source, target) in enumerate(zip(sources, kept + spread))
     ]
     for copy in copies:
         copy.start()
     for copy in copies:
         copy.wait()
-    for i, value in enumerate(targets[-3:]):
+    for i, value in enumerate(spread):
         width = value.shape[1]
         diagonal = lax.broadcasted_iota(I32, (8, width), 0) == lax.broadcasted_iota(I32, (8, width), 1)
         column = jnp.sum(jnp.where(diagonal, wide(value[...]), 0.0), axis=1, keepdims=True)
@@ -153,12 +154,20 @@
 
 
 def stencil_kernel(
-    here, scalars, fields, edge, table, old, owner, slots, tiles,
-    fresh, force, beside_old, window, ends_row, ends_lane, hot, tile_buffer, padded, sem,
+    here, scalars, fields, edge, table, old, owner, slots, entry_block, tiles,
+    fresh, force, beside_old, window, ends_row, ends_lane, hot, member, tile_buffer, padded, sems,
 ):
     del here
-    load = pltpu.make_async_copy(tiles, tile_buffer, sem.at[0])
-    load.start()
+    parts = sems.shape[0]
+    step = tiles.shape[0] // parts
+    loads = [
+        pltpu.make_async_copy(
+            tiles.at[pl.ds(part * step, step)], tile_buffer.at[pl.ds(part * step, step)], sems.at[part]
+        )
+        for part in range(parts)
+    ]
+    for load in loads:
+        load.start()
     blocks = old.shape[0]
     levels = fields.shape[0]
     speed = scalars[pl.ds(0, 8), :]
@@ -200,6 +209,9 @@
     hot[...] = jnp.where(
         lax.broadcasted_iota(I32, hot.shape, 0) == slots[...], 1.0, 0.0
     ).astype(BF16)
+    member[...] = jnp.where(
+        lax.broadcasted_iota(I32, member.shape, 0) == entry_block[...], 1.0, 0.0
+    ).astype(BF16)
 
     firsts = ends_row.shape[0] * LANES
     ident = lax.broadcasted_iota(I32, ends_row.shape, 0) * LANES + lax.broadcasted_iota(
@@ -221,7 +233,8 @@
         lanes = jnp.where(value <= ident, lanes + bit, lanes)
     ends_row[...] = rows
     ends_lane[...] = lanes
-    load.wait()
+    for load in loads:
+        load.wait()
 
 
 def neighbour_sum(padded, edges, window, blocks):
@@ -286,13 +299,11 @@
 
 
 def forward_kernel(
-    entry_block_any, tiles, scalars, near1, far1, near2, far2, here, hot, fields, edges, window, old,
+    tiles, scalars, near1, far1, near2, far2, here, hot, member, fields, edges, window, old,
     diagonal, force_part, beside_old, ends_row, ends_lane, fresh, ctable, cedge, cdiag, cowner,
     summed, force_out, smooth_out, source_out, frame, ends_out, message,
-    entry_block, picked, padded, prefixed, totals, arrivals, sem,
+    picked, products, padded, prefixed, totals, arrivals,
 ):
-    fetch = pltpu.make_async_copy(entry_block_any, entry_block, sem.at[0])
-    fetch.start()
     tile = lax.axis_index("tile")
     tile_count = lax.axis_size("tile")
     even = lax.rem(tile, 2) == 0
@@ -317,19 +328,27 @@
     arrivals[0] = from_left[:base].astype(F32)
     arrivals[1] = from_right[:base].astype(F32)
 
-    summed[...] = jnp.zeros(summed.shape, F32)
-    fetch.wait()
-
-    def pair(number, carry):
-        entry = 2 * number
-        rows = picked[pl.ds(pl.multiple_of(4 * entry, 8), 8), :].astype(BF16)
-        first = dot_nt(rows, tiles[entry])
-        second = dot_nt(rows, tiles[entry + 1])
-        summed[entry_block[0, entry], pl.ds(0, 4), :] += first[0:4]
-        summed[entry_block[0, entry + 1], pl.ds(4, 4), :] += second[4:8]
-        return carry
-
-    lax.fori_loop(0, entries // 2, pair, 0, unroll=8)
+    upper = lax.rem(lax.broadcasted_iota(I32, (16, LANES), 0), 8) < 4
+    for group in range(entries // 4):
+        rows = picked[pl.ds(16 * group, 16), :]
+        rows = jnp.concatenate([jnp.where(upper, rows, 0.0), jnp.where(upper, 0.0, rows)], axis=1)
+        at = 4 * group
+        weights = jnp.concatenate(
+            [
+                jnp.concatenate([tiles[at], tiles[at + 1]], axis=1),
+                jnp.concatenate([tiles[at + 2], tiles[at + 3]], axis=1),
+            ],
+            axis=0,
+        )
+        product = dot_nt(rows.astype(BF16), weights)
+        products[pl.ds(16 * group, 8), :] = product[0:8, :LANES]
+        products[pl.ds(16 * group + 8, 8), :] = product[8:16, LANES:]
+    spread = []
+    for channel in range(4):
+        spread.append(jnp.concatenate(split3(products[pl.ds(channel, entries, stride=4), :]), axis=1))
+    for channel in range(4):
+        value = jnp.dot(member[...], spread[channel], preferred_element_type=F32)
+        summed[channel] = value[:, :LANES] + value[:, LANES : 2 * LANES] + value[:, 2 * LANES :]
 
     speed = scalars[pl.ds(0, 8), :]
     share = scalars[pl.ds(8, 8), :]
@@ -358,8 +377,7 @@
 
     force = force_out[...]
     for channel in range(4):
-        value = summed[:, channel, :] + summed[:, channel + 4, :]
-        force = force + scalars[pl.ds(16 + channel, 1), :] * value
+        force = force + scalars[pl.ds(16 + channel, 1), :] * summed[channel]
     force_out[...] = force
     total = diagonal[...] + edges[0] + edges[1] + edges[2]
     smooth_out[...] = beside_old[...]
@@ -498,9 +516,10 @@
     copies.append(pltpu.make_async_copy(fresh.at[:, middle], fresh_out.at[:, middle], sem.at[2]))
     for copy in copies:
         copy.start()
-    blocks = summed.shape[0]
+    channels, blocks = summed.shape[:2]
     for block in range(blocks):
-        received[:, pl.ds(block * LANES, LANES)] = summed[block, pl.ds(0, 4), :] + summed[block, pl.ds(4, 4), :]
+        for channel in range(channels):
+            received[pl.ds(channel, 1), pl.ds(block * LANES, LANES)] = summed[channel, pl.ds(block, 1), :]
     bottoms, size = cinverse.shape
     halves = size // LANES
     near = near1[pl.ds(INVERSE, 32 * halves), :].astype(F32)
@@ -593,7 +612,7 @@
 VMEM = pl.BlockSpec(memory_space=pltpu.VMEM)
 SMEM = pl.BlockSpec(memory_space=pltpu.SMEM)
 ANY = pl.BlockSpec(memory_space=pltpu.HBM)
-PARAMS = pltpu.CompilerParams(vmem_limit_bytes=48 * 1024 * 1024)
+PARAMS = pltpu.CompilerParams(vmem_limit_bytes=16 * 1024 * 1024)
 
 
 def pair_up(count, distance):
@@ -641,21 +660,25 @@
         coarse_owner.reshape(frows, LANES),
         coarse_inverse[0],
         entry_slot[0],
+        entry_block[0],
         level_rate,
         level_weight,
         flux_weight,
     )
     loaded = pl.pallas_call(
         load_kernel,
-        out_shape=[struct(x.shape, x.dtype) for x in raw] + [struct((24, LANES))],
+        out_shape=[struct(x.shape, x.dtype) for x in raw[:-3]] + [struct((24, LANES))],
         in_specs=[ANY] * len(raw),
-        out_specs=[VMEM] * (len(raw) + 1),
-        scratch_shapes=[pltpu.SemaphoreType.DMA((len(raw),))],
+        out_specs=[VMEM] * (len(raw) - 2),
+        scratch_shapes=[pltpu.VMEM(x.shape, x.dtype) for x in raw[-3:]]
+        + [pltpu.SemaphoreType.DMA((len(raw),))],
         compiler_params=PARAMS,
         name="load",
     )(*[in_hbm(x) for x in raw])
-    current, old, edges, table, owner, diagonal, ctable, cedge, cdiag, cowner, cinverse, slot = loaded[:12]
-    scalars = loaded[-1]
+    (
+        current, old, edges, table, owner, diagonal, ctable, cedge, cdiag, cowner, cinverse,
+        slot, block, scalars,
+    ) = loaded
 
     near1, far1, near2, far2, here = pl.pallas_call(
         pack_kernel,
@@ -685,7 +708,7 @@
     near1 = lax.ppermute(near1, "tile", one_a)
     near2 = lax.ppermute(near2, "tile", two_a)
 
-    fresh, force_part, beside_old, window, ends_row, ends_lane, hot, tiles = pl.pallas_call(
+    fresh, force_part, beside_old, window, ends_row, ends_lane, hot, member, tiles = pl.pallas_call(
         stencil_kernel,
         out_shape=[
             struct((fields.shape[1], cells)),
@@ -695,19 +718,20 @@
             struct((frows, LANES), I32),
             struct((frows, LANES), I32),
             struct((slots, entries), BF16),
-            struct(remap_tiles.shape[2:], BF16),
+            struct((blocks, entries), BF16),
+            pltpu.VMEM(remap_tiles.shape[2:], BF16),
         ],
-        in_specs=[VMEM] * 8 + [ANY],
-        out_specs=[VMEM] * 8,
-        scratch_shapes=[pltpu.VMEM((blocks + 16, LANES), F32), pltpu.SemaphoreType.DMA((1,))],
+        in_specs=[VMEM] * 9 + [ANY],
+        out_specs=[VMEM] * 9,
+        scratch_shapes=[pltpu.VMEM((blocks + 16, LANES), F32), pltpu.SemaphoreType.DMA((math.gcd(entries, 8),))],
         compiler_params=PARAMS,
         name="stencil",
-    )(here, scalars, current, edges, table, old, owner, slot, in_hbm(remap_tiles[0, 0]))
+    )(here, scalars, current, edges, table, old, owner, slot, block, in_hbm(remap_tiles[0, 0]))
 
     summed, force, smooth, source, frame, ends_new, message = pl.pallas_call(
         forward_kernel,
         out_shape=[
-            struct((blocks, 8, LANES)),
+            struct((channels, blocks, LANES)),
             struct((blocks, LANES)),
             struct((blocks, LANES)),
             struct((FRAME, LANES)),
@@ -715,21 +739,20 @@
             struct((fields.shape[1], 2 * LANES)),
             struct((tile_count, 8, LANES)),
         ],
-        in_specs=[ANY] + [VMEM] * 22,
+        in_specs=[VMEM] * 23,
         out_specs=[VMEM] * 7,
         scratch_shapes=[
-            pltpu.SMEM((1, entries), I32),
+            pltpu.VMEM((4 * entries, LANES), F32),
             pltpu.VMEM((4 * entries, LANES), F32),
             pltpu.VMEM((blocks + 16, LANES), F32),
             pltpu.VMEM((blocks, LANES), F32),
             pltpu.VMEM((blocks, LANES), F32),
             pltpu.VMEM((2, base, LANES), F32),
-            pltpu.SemaphoreType.DMA((1,)),
         ],
         compiler_params=PARAMS,
         name="forward",
     )(
-        in_hbm(entry_block[0]), tiles, scalars, near1, far1, near2, far2, here, hot, current, edges, window, old,
+        tiles, scalars, near1, far1, near2, far2, here, hot, member, current, edges, window, old,
         diagonal, force_part, beside_old, ends_row, ends_lane, fresh, ctable, cedge, cdiag, cowner,
     )
     arrived = lax.all_to_all(message, "tile", split_axis=0, concat_axis=0, tiled=True)

time: 42.4 us -> 34.2 us (0.81)
  Pallas kernels: 21 us -> 12.5 us
    pallas_call x1, Pallas kernels: 8.96 us -> 3.65 us  [per_device(): pl.pallas_call(forward_kernel, out_shape=[struct((channels, blocks, LANES...]
    pallas_call x1, Pallas kernels: 7.09 us -> 4.32 us  [per_device(): pl.pallas_call(stencil_kernel, out_shape=[struct((fields.shape[1], cells)...]
    pallas_call x1, Pallas kernels: 1.7 us -> 1.28 us  [per_device(): pl.pallas_call(load_kernel, out_shape=[struct(x.shape, x.dtype) for x in...]
  transfers between devices with their start and end apart: 7 -> 7, of which waited for: 1 -> 2; matrix products, arithmetic and copies ran while one was open for 0% -> 0% of each run, Pallas kernels for 24% -> 21%
where the time goes in v3:
time: 34.2 us; the launch traced here: 34 us
  starting transfers between devices  14.3 us (42%)
  Pallas kernels  12.5 us (37%)
  waiting for transfers between devices  6.42 us (19%)
  between operations  0.7 us (2%)
    all_to_all x1, waiting for transfers between devices, per_device(): lax.all_to_all(message, 'tile', split_axis=0, concat_axis=0, tiled=True)  6.05 us
    ppermute x1, starting transfers between devices, per_device(): far1 = lax.ppermute(far1, 'tile', one_b)  4.52 us
    all_to_all x1, starting transfers between devices, per_device(): lax.all_to_all(message, 'tile', split_axis=0, concat_axis=0, tiled=True)  4.33 us
    pallas_call x1, Pallas kernels, per_device(): pl.pallas_call(stencil_kernel, out_shape=[struct((fields.shape[1], cells)...  4.32 us
    pallas_call x1, Pallas kernels, per_device(): pl.pallas_call(forward_kernel, out_shape=[struct((channels, blocks, LANES...  3.65 us
    ppermute x1, starting transfers between devices, per_device(): near1 = lax.ppermute(near1, 'tile', one_a)  2.99 us
    ppermute x1, starting transfers between devices, per_device(): far2 = lax.ppermute(far2, 'tile', two_b)  1.91 us
    pallas_call x1, Pallas kernels, per_device(): pl.pallas_call(functools.partial(backward_kernel, frows), out_shape=struc...  1.56 us
  transfers between devices with their start and end apart: 7, of which 2 were waited for; matrix products, arithmetic and copies ran while one was open for 0% of the time, Pallas kernels for 21%

profile of v3, /device:TPU:0, one launch (start us, length us, event | category | flops | bytes accessed | tf_op | source)
XLA Modules:
  0.0 34.0 jit_solution(10998007485772038264)
XLA Ops:
  0.6 0.5 %collective-permute-start = (bf16[4,8192]{1,0:T(4,128)(2,1)}, bf16[4,8192]{1,0:T(4,128)(2,1)S(1)}, u32[]{:S(2)}, u32[]{:S(2)}) collective-permute-start(bf16[4,8192]{1,0:T(4,128)(2,1)} %bitcast.36), channel_id=1, source_target_pairs={{0,16},{16,0},{1,17},{17,1},{2,18},{18,2},{3,19},{19,3},{4,20},{20... | collective-permute-start | bytes 196616 | tf_op jit(solution)/shard_map/ppermute | solution.py:648
  1.2 0.1 collective-permute-start.1
  1.2 1.3 %load.1 = (f32[8,8192]{1,0:T(8,128)S(1)}, f32[64,128]{1,0:T(8,128)S(1)}, f32[3,64,128]{2,1,0:T(8,128)S(1)}, s32[3,64,128]{2,1,0:T(8,128)S(1)}, s32[64,128]{1,0:T...) custom-call(f32[8,8192]{1,0:T(8,128)} %bitcast.20, ...), custom_call_target="tpu_custom_call" | custom-call | tf_op jit(solution)/shard_map/load/pallas_call | solution.py:668
  2.5 0.0 collective-permute-done.1.sends
  2.5 0.0 collective-permute-done.surface
  2.5 0.3 pack.1
  2.8 3.0 %collective-permute-start.2 = (bf16[256,128]{1,0:T(8,128)(2,1)S(1)}, bf16[256,128]{1,0:T(8,128)(2,1)S(1)}, u32[]{:S(2)}, u32[]{:S(2)}) collective-permute-start(bf16[256,128]{1,0:T(8,128)(2,1)S(1)} %get-tuple-element.57), channel_id=1, source_target_pairs={{0,1},{1,0},{2,3},{3,2},{4,5},{5,4},{6,7},{7,6},{8,9},{9,8},{10,11... | collective-permute-start | bytes 196616 | tf_op jit(solution)/shard_map/ppermute | solution.py:708
  5.8 4.5 %collective-permute-start.3 = (bf16[256,128]{1,0:T(8,128)(2,1)S(1)}, bf16[256,128]{1,0:T(8,128)(2,1)S(1)}, u32[]{:S(2)}, u32[]{:S(2)}) collective-permute-start(bf16[256,128]{1,0:T(8,128)(2,1)S(1)} %get-tuple-element.58), channel_id=1, source_target_pairs={{1,2},{2,1},{3,4},{4,3},{5,6},{6,5},{7,8},{8,7},{9,10},{10,9},{11,... | collective-permute-start | bytes 196616 | tf_op jit(solution)/shard_map/ppermute | solution.py:706
  10.3 0.0 collective-permute-start.4
  10.3 1.9 %collective-permute-start.5 = (bf16[128,128]{1,0:T(8,128)(2,1)S(1)}, bf16[128,128]{1,0:T(8,128)(2,1)S(1)}, u32[]{:S(2)}, u32[]{:S(2)}) collective-permute-start(bf16[128,128]{1,0:T(8,128)(2,1)S(1)} %get-tuple-element.60), channel_id=1, source_target_pairs={{2,4},{4,2},{3,5},{5,3},{6,8},{8,6},{7,9},{9,7},{10,12},{12,10},{1... | collective-permute-start | bytes 98312 | tf_op jit(solution)/shard_map/ppermute | solution.py:707
  12.2 4.3 %stencil.1 = (f32[8,8192]{1,0:T(8,128)S(1)}, f32[64,128]{1,0:T(8,128)S(1)}, f32[64,128]{1,0:T(8,128)S(1)}, s32[3,64,128]{2,1,0:T(8,128)S(1)}, s32[8,128]{1,0:T(8...) custom-call(bf16[128,128]{1,0:T(8,128)(2,1)S(1)} %get-tuple-element., ...), custom_call_target="tpu_custom_call" | custom-call | tf_op jit(solution)/shard_map/stencil/pallas_call | solution.py:711
  16.6 0.0 collective-permute-done.4.near2
  16.6 0.4 %collective-permute-done.5.far2 = bf16[128,128]{1,0:T(8,128)(2,1)S(1)} collective-permute-done((bf16[128,128]{1,0:T(8,128)(2,1)S(1)}, bf16[128,128]{1,0:T(8,128)(2,1)S(1)}, u32[]{:S(2)}, u32[]{:S(2)}) %collective-permute-start.5) | collective-permute-done | bytes 32800 | tf_op jit(solution)/shard_map/ppermute | solution.py:707
  16.9 0.0 collective-permute-done.2.near1
  16.9 0.0 collective-permute-done.3.far1
  16.9 3.6 %forward.1 = (f32[4,64,128]{2,1,0:T(8,128)S(1)}, f32[64,128]{1,0:T(8,128)S(1)}, f32[64,128]{1,0:T(8,128)S(1)}, f32[32,128]{1,0:T(8,128)S(1)}, f32[256,128]{1,0:T...) custom-call(bf16[160,128,128]{2,1,0:T(8,128)(2,1)S(1)} %get-tuple-element.56.tiles, ...), custom_call_target="tpu_custom_call" | custom-call | tf_op jit(solution)/shard_map/forward/pallas_call | solution.py:731
  20.6 4.3 %all-to-all-start = ((f32[16,8,128]{2,1,0:T(8,128)}), f32[16,8,128]{2,1,0:T(8,128)S(1)}, u32[]{:S(2)}, u32[]{:S(2)}) async-start(f32[16,8,128]{2,1,0:T(8,128)} %get-tuple-element.73), calls=%async_computation | async-start | bytes 131072 | tf_op jit(solution)/shard_map/all_to_all | solution.py:758
  24.9 1.5 %prepare.1 = (f32[8,8192]{1,0:T(8,128)}, f32[4,8192]{1,0:T(4,128)}, f32[16,48,128]{2,1,0:T(8,128)S(1)}) custom-call(f32[8,8192]{1,0:T(8,128)S(1)} %get-tuple-element.55.fresh, f32[8,256]{1,0:T(8,128)S(1)} %get-tuple-element.69.ends_new, f32[4,64,128]{2,1,0:T(8,128)S(1)} %get-tuple-element.70.summed, bf16[256,128]{1,0:T(8,128)(2,1)S(1)} %collective-permute-done.2.near1, ...), custom_call_target="tpu_custom_call" | custom-call | tf_op jit(solution)/shard_map/prepare/pallas_call | solution.py:759
  26.4 6.0 %all-to-all-done.arrived = f32[16,8,128]{2,1,0:T(8,128)S(1)} async-done(((f32[16,8,128]{2,1,0:T(8,128)}), f32[16,8,128]{2,1,0:T(8,128)S(1)}, u32[]{:S(2)}, u32[]{:S(2)}) %all-to-all-start) | async-done | bytes 65568 | tf_op jit(solution)/shard_map/all_to_all | solution.py:758
  32.5 1.6 %backward.1 = f32[64,128]{1,0:T(8,128)} custom-call(f32[16,8,128]{2,1,0:T(8,128)S(1)} %all-to-all-done.arrived, f32[16,48,128]{2,1,0:T(8,128)S(1)} %get-tuple-element.74.weights, f32[32,128]{1,0:T(8,128)S(1)} %get-tuple-element.75.source, f32[256,128]{1,0:T(8,128)S(1)} %get-tuple-element.76.frame, f32[64,128]{1,0:T(8,128)S(1)} %get-tuple-element.77.force, ...), custom_call_target="tpu_custom_call" | custom-call | tf_op jit(solution)/shard_map/backward/pallas_call | solution.py:775
Async XLA Ops:
  0.6 1.9 %collective-permute-start = (bf16[4,8192]{1,0:T(4,128)(2,1)}, bf16[4,8192]{1,0:T(4,128)(2,1)S(1)}, u32[]{:S(2)}, u32[]{:S(2)}) collective-permute-start(bf16[4,8192]{1,0:T(4,128)(2,1)} %bitcast.36), channel_id=1, source_target_pairs={{0,16},{16,0},{1,17},{17,1},{2,18},{18,2},{3,19},{19,3},{4,20},{20... | collective-permute-start | bytes 196616 | tf_op jit(solution)/shard_map/ppermute | solution.py:648
  1.2 1.4 %collective-permute-start.1 = (s32[1,160]{1,0:T(1,128)}, s32[1,160]{1,0:T(1,128)S(1)}, u32[]{:S(2)}, u32[]{:S(2)}) collective-permute-start(s32[1,160]{1,0:T(1,128)} %bitcast.37), channel_id=1, source_target_pairs={{0,16},{16,0},{1,17},{17,1},{2,18},{18,2},{3,19},{19,3},{4,20},{20... | collective-permute-start | bytes 1928 | tf_op jit(solution)/shard_map/ppermute | solution.py:649
  2.8 14.1 %collective-permute-start.2 = (bf16[256,128]{1,0:T(8,128)(2,1)S(1)}, bf16[256,128]{1,0:T(8,128)(2,1)S(1)}, u32[]{:S(2)}, u32[]{:S(2)}) collective-permute-start(bf16[256,128]{1,0:T(8,128)(2,1)S(1)} %get-tuple-element.57), channel_id=1, source_target_pairs={{0,1},{1,0},{2,3},{3,2},{4,5},{5,4},{6,7},{7,6},{8,9},{9,8},{10,11... | collective-permute-start | bytes 196616 | tf_op jit(solution)/shard_map/ppermute | solution.py:708
  5.8 11.1 %collective-permute-start.3 = (bf16[256,128]{1,0:T(8,128)(2,1)S(1)}, bf16[256,128]{1,0:T(8,128)(2,1)S(1)}, u32[]{:S(2)}, u32[]{:S(2)}) collective-permute-start(bf16[256,128]{1,0:T(8,128)(2,1)S(1)} %get-tuple-element.58), channel_id=1, source_target_pairs={{1,2},{2,1},{3,4},{4,3},{5,6},{6,5},{7,8},{8,7},{9,10},{10,9},{11,... | collective-permute-start | bytes 196616 | tf_op jit(solution)/shard_map/ppermute | solution.py:706
  10.3 6.2 %collective-permute-start.4 = (bf16[128,128]{1,0:T(8,128)(2,1)S(1)}, bf16[128,128]{1,0:T(8,128)(2,1)S(1)}, u32[]{:S(2)}, u32[]{:S(2)}) collective-permute-start(bf16[128,128]{1,0:T(8,128)(2,1)S(1)} %get-tuple-element.59), channel_id=1, source_target_pairs={{0,2},{2,0},{1,3},{3,1},{4,6},{6,4},{5,7},{7,5},{8,10},{10,8},{9,1... | collective-permute-start | bytes 98312 | tf_op jit(solution)/shard_map/ppermute | solution.py:709
  10.3 6.6 %collective-permute-start.5 = (bf16[128,128]{1,0:T(8,128)(2,1)S(1)}, bf16[128,128]{1,0:T(8,128)(2,1)S(1)}, u32[]{:S(2)}, u32[]{:S(2)}) collective-permute-start(bf16[128,128]{1,0:T(8,128)(2,1)S(1)} %get-tuple-element.60), channel_id=1, source_target_pairs={{2,4},{4,2},{3,5},{5,3},{6,8},{8,6},{7,9},{9,7},{10,12},{12,10},{1... | collective-permute-start | bytes 98312 | tf_op jit(solution)/shard_map/ppermute | solution.py:707
  20.6 11.9 %all-to-all-start = ((f32[16,8,128]{2,1,0:T(8,128)}), f32[16,8,128]{2,1,0:T(8,128)S(1)}, u32[]{:S(2)}, u32[]{:S(2)}) async-start(f32[16,8,128]{2,1,0:T(8,128)} %get-tuple-element.73), calls=%async_computation | async-start | bytes 131072 | tf_op jit(solution)/shard_map/all_to_all | solution.py:758

commit v4 on v3

--- a/solution.py
+++ b/solution.py
@@ -22,6 +22,10 @@
 INVERSE = 56
 
 FRAME, OWN = 32, 8
+
+
+def sides(far, near, even):
+    return jnp.where(even, far, near), jnp.where(even, near, far)
 
 
 def gather_lanes(table, index):
@@ -73,11 +77,9 @@
 
 def pack_kernel(
     surface, sends, fields, old, edge, table, owner, ctable, cedge, cdiag, cowner, cinverse,
-    near1, far1, near2, far2, here, chunks, left_rows, right_rows,
+    to_right2, far, to_left2, near, here, chunks, left_rows, right_rows,
 ):
-    tile = lax.axis_index("tile")
-    even = lax.rem(tile, 2) == 0
-    low = lax.rem(tile, 4) < 2
+    even = lax.rem(lax.axis_index("tile"), 2) == 0
     cells = fields.shape[1]
     blocks = cells // LANES
     frows = ctable.shape[1]
@@ -137,20 +139,17 @@
         picks.append(dot_tn(hot, source).astype(BF16))
     count = slots // 5
 
-    def chosen(j):
-        return jnp.concatenate([p[j * count : (j + 1) * count] for p in picks], axis=0)
-
-    to_right, to_left = chosen(1), chosen(3)
-    far_right, far_left = chosen(0), chosen(4)
-    here[...] = chosen(2)
-    rim_right = right_rows[...].astype(BF16)
-    rim_left = left_rows[...].astype(BF16)
-    near1[pl.ds(0, base), :] = jnp.where(even, rim_right, rim_left)
-    far1[pl.ds(0, base), :] = jnp.where(even, rim_left, rim_right)
-    near1[pl.ds(base, 4 * count), :] = jnp.where(even, to_right, to_left)
-    far1[pl.ds(base, 4 * count), :] = jnp.where(even, to_left, to_right)
-    near2[...] = jnp.where(low, far_right, far_left)
-    far2[...] = jnp.where(low, far_left, far_right)
+    chosen = [
+        jnp.concatenate([p[j * count : (j + 1) * count] for p in picks], axis=0) for j in range(5)
+    ]
+    here[...] = chosen[2]
+    for out, j in ((to_right2, 0), (to_left2, 4)):
+        out[pl.ds(0, base), :] = jnp.zeros((base, LANES), BF16)
+        out[pl.ds(base, 4 * count), :] = chosen[j]
+    right = jnp.concatenate([right_rows[...].astype(BF16), chosen[1]], axis=0)
+    left = jnp.concatenate([left_rows[...].astype(BF16), chosen[3]], axis=0)
+    far[...] = jnp.where(even, left, right)
+    near[...] = jnp.where(even, right, left)
 
 
 def stencil_kernel(
@@ -299,30 +298,25 @@
 
 
 def forward_kernel(
-    tiles, scalars, near1, far1, near2, far2, here, hot, member, fields, edges, window, old,
+    tiles, scalars, from_left2, far, from_right2, near, here, hot, member, fields, edges, window, old,
     diagonal, force_part, beside_old, ends_row, ends_lane, fresh, ctable, cedge, cdiag, cowner,
     summed, force_out, smooth_out, source_out, frame, ends_out, message,
     picked, products, padded, prefixed, totals, arrivals,
 ):
     tile = lax.axis_index("tile")
     tile_count = lax.axis_size("tile")
-    even = lax.rem(tile, 2) == 0
-    low = lax.rem(tile, 4) < 2
     entries = tiles.shape[0]
     blocks = old.shape[0]
 
-    base = near1.shape[0] - near2.shape[0]
-    near, far = near1[...], far1[...]
-    from_left = jnp.where(even, far, near)
-    from_right = jnp.where(even, near, far)
-    two_near, two_far = near2[...], far2[...]
-    j0 = jnp.where(low, two_far, two_near)
-    j4 = jnp.where(low, two_near, two_far)
-    j1, j3, j2 = from_left[base:], from_right[base:], here[...]
-    each = j0.shape[0] // 4
+    even = lax.rem(tile, 2) == 0
+    base = far.shape[0] - here.shape[0]
+    each = here.shape[0] // 4
+    from_left, from_right = sides(far[...], near[...], even)
+    sources = (from_left2[base:, :], from_left[base:], here[...], from_right[base:], from_right2[base:, :])
     for channel in range(4):
-        span = slice(channel * each, (channel + 1) * each)
-        source = jnp.concatenate([j[span] for j in (j0, j1, j2, j3, j4)], axis=0)
+        source = jnp.concatenate(
+            [rows[channel * each : (channel + 1) * each] for rows in sources], axis=0
+        )
         picked[pl.ds(channel, entries, stride=4), :] = dot_tn(hot[...], source)
 
     arrivals[0] = from_left[:base].astype(F32)
@@ -499,10 +493,9 @@
 
 
 def prepare_kernel(
-    fresh, ends_new, summed, near1, far1, cinverse, fresh_out, received, weights, sem, extended
+    fresh, ends_new, summed, far, near, cinverse, fresh_out, received, weights, sem, extended
 ):
-    tile = lax.axis_index("tile")
-    even = lax.rem(tile, 2) == 0
+    even = lax.rem(lax.axis_index("tile"), 2) == 0
     cells = fresh_out.shape[1]
     copies = [
         pltpu.make_async_copy(
@@ -522,10 +515,8 @@
             received[pl.ds(channel, 1), pl.ds(block * LANES, LANES)] = summed[channel, pl.ds(block, 1), :]
     bottoms, size = cinverse.shape
     halves = size // LANES
-    near = near1[pl.ds(INVERSE, 32 * halves), :].astype(F32)
-    far = far1[pl.ds(INVERSE, 32 * halves), :].astype(F32)
-    left = jnp.where(even, far, near)
-    right = jnp.where(even, near, far)
+    part = pl.ds(INVERSE, 32 * halves)
+    left, right = sides(far[part, :].astype(F32), near[part, :].astype(F32), even)
     for half in range(halves):
         part = pl.ds(half * LANES, LANES)
         for at, block in ((0, left), (2, right)):
@@ -545,12 +536,11 @@
 
 
 def backward_kernel(
-    frame_rows, arrived, weights, source, frame, force, smooth, edges, window, diagonal, owner, near1, far1,
+    frame_rows, arrived, weights, source, frame, force, smooth, edges, window, diagonal, owner, far, near,
     height, frame_source, padded, third_rows,
 ):
     tile = lax.axis_index("tile")
     tile_count = lax.axis_size("tile")
-    even = lax.rem(tile, 2) == 0
     blocks = force.shape[0]
     left = arrived[lax.rem(tile + tile_count - 1, tile_count)]
     right = arrived[lax.rem(tile + 1, tile_count)]
@@ -588,10 +578,12 @@
         )
     corrected = smooth[...] + corrected
     padded[pl.ds(8, blocks), :] = corrected
-    near = near1[pl.ds(16, 16), :].astype(F32)
-    far = far1[pl.ds(16, 16), :].astype(F32)
-    left_owner = jnp.where(even, far, near)[OWNER - 16 : OWNER - 15].astype(I32)
-    right_owner = jnp.where(even, near, far)[OWNER - 16 : OWNER - 15].astype(I32)
+    part = pl.ds(16, 16)
+    even = lax.rem(tile, 2) == 0
+    left_owner, right_owner = [
+        rows[OWNER - 16 : OWNER - 15].astype(I32)
+        for rows in sides(far[part, :].astype(F32), near[part, :].astype(F32), even)
+    ]
     left_rim = left[1:2] + gather_lanes(wide(third_rows[pl.ds(OWN - 1, 1), :]), wide(left_owner))[0:1]
     right_rim = right[1:2] + gather_lanes(wide(third_rows[pl.ds(OWN + frows, 1), :]), wide(right_owner))[0:1]
     padded[pl.ds(7, 1), :] = left_rim
@@ -613,18 +605,6 @@
 SMEM = pl.BlockSpec(memory_space=pltpu.SMEM)
 ANY = pl.BlockSpec(memory_space=pltpu.HBM)
 PARAMS = pltpu.CompilerParams(vmem_limit_bytes=16 * 1024 * 1024)
-
-
-def pair_up(count, distance):
-    period = 2 * distance
-    result = []
-    for start in (0, distance):
-        pairs = []
-        for i in range(count):
-            if (i - start) % period < distance:
-                pairs += [(i, (i + distance) % count), ((i + distance) % count, i)]
-        result.append(pairs)
-    return result
 
 
 def per_device(
@@ -680,15 +660,11 @@
         slot, block, scalars,
     ) = loaded
 
-    near1, far1, near2, far2, here = pl.pallas_call(
+    pick = struct((4 * each, LANES), BF16)
+    both = struct((base + 4 * each, LANES), BF16)
+    to_right2, far, to_left2, near, here = pl.pallas_call(
         pack_kernel,
-        out_shape=[
-            struct((base + 4 * each, LANES), BF16),
-            struct((base + 4 * each, LANES), BF16),
-            struct((4 * each, LANES), BF16),
-            struct((4 * each, LANES), BF16),
-            struct((4 * each, LANES), BF16),
-        ],
+        out_shape=[both, both, both, both, pick],
         in_specs=[VMEM] * 12,
         out_specs=[VMEM] * 5,
         scratch_shapes=[
@@ -701,12 +677,21 @@
     )(
         surface, sends, current, old, edges, table, owner, ctable, cedge, cdiag, cowner, cinverse,
     )
-    one_a, one_b = pair_up(tile_count, 1)
-    two_a, two_b = pair_up(tile_count, 2)
-    far1 = lax.ppermute(far1, "tile", one_b)
-    far2 = lax.ppermute(far2, "tile", two_b)
-    near1 = lax.ppermute(near1, "tile", one_a)
-    near2 = lax.ppermute(near2, "tile", two_a)
+
+    def shifted(array, distance):
+        return lax.ppermute(
+            array, "tile", [(i, (i + distance) % tile_count) for i in range(tile_count)]
+        )
+
+    def swapped(array, start):
+        lower = [i for i in range(tile_count) if i % 2 == start]
+        pairs = [(i, (i + 1) % tile_count) for i in lower]
+        return lax.ppermute(array, "tile", pairs + [(j, i) for i, j in pairs])
+
+    from_left2 = shifted(to_right2, 2)
+    far = swapped(far, 1)
+    from_right2 = shifted(to_left2, -2)
+    near = swapped(near, 0)
 
     fresh, force_part, beside_old, window, ends_row, ends_lane, hot, member, tiles = pl.pallas_call(
         stencil_kernel,
@@ -752,7 +737,7 @@
         compiler_params=PARAMS,
         name="forward",
     )(
-        tiles, scalars, near1, far1, near2, far2, here, hot, member, current, edges, window, old,
+        tiles, scalars, from_left2, far, from_right2, near, here, hot, member, current, edges, window, old,
         diagonal, force_part, beside_old, ends_row, ends_lane, fresh, ctable, cedge, cdiag, cowner,
     )
     arrived = lax.all_to_all(message, "tile", split_axis=0, concat_axis=0, tiled=True)
@@ -771,7 +756,7 @@
         ],
         compiler_params=PARAMS,
         name="prepare",
-    )(fresh, ends_new, summed, near1, far1, cinverse)
+    )(fresh, ends_new, summed, far, near, cinverse)
     height = pl.pallas_call(
         functools.partial(backward_kernel, frows),
         out_shape=struct((blocks, LANES)),
@@ -784,7 +769,7 @@
         ],
         compiler_params=PARAMS,
         name="backward",
-    )(arrived, weights, source, frame, force, smooth, edges, window, diagonal, owner, near1, far1)
+    )(arrived, weights, source, frame, force, smooth, edges, window, diagonal, owner, far, near)
     return advanced[None], received[None], height.reshape(1, cells)
 
 

time: 34.2 us -> 33.4 us (0.977)
  starting transfers between devices: 14.3 us -> 13.8 us
  waiting for transfers between devices: 6.42 us -> 6.06 us
    ppermute x4, waiting for transfers between devices: 0.37 us -> 0.01 us  [the longest x2 0.01 us: shifted(): lax.ppermute(array, 'tile', [(i, (i + distance) % tile_count) for i in ra...]
  transfers between devices with their start and end apart: 7 -> 7, of which waited for: 2 -> 1; matrix products, arithmetic and copies ran while one was open for 0% -> 0% of each run, Pallas kernels for 21% -> 21%
where the time goes in v4:
time: 33.4 us; the launch traced here: 33.2 us
  starting transfers between devices  13.8 us (41%)
  Pallas kernels  12.6 us (38%)
  waiting for transfers between devices  6.06 us (18%)
  between operations  0.72 us (2%)
    all_to_all x1, waiting for transfers between devices, per_device(): lax.all_to_all(message, 'tile', split_axis=0, concat_axis=0, tiled=True)  6.05 us
    ppermute x2, starting transfers between devices, shifted(): lax.ppermute(array, 'tile', [(i, (i + distance) % tile_count) for i in ra...  4.86 us
    ppermute x2, starting transfers between devices, swapped(): return lax.ppermute(array, 'tile', pairs + [(j, i) for i, j in pairs])  4.33 us
    pallas_call x1, Pallas kernels, per_device(): pl.pallas_call(stencil_kernel, out_shape=[struct((fields.shape[1], cells)...  4.32 us
    all_to_all x1, starting transfers between devices, per_device(): lax.all_to_all(message, 'tile', split_axis=0, concat_axis=0, tiled=True)  4.05 us
    pallas_call x1, Pallas kernels, per_device(): pl.pallas_call(forward_kernel, out_shape=[struct((channels, blocks, LANES...  3.69 us
    pallas_call x1, Pallas kernels, per_device(): pl.pallas_call(functools.partial(backward_kernel, frows), out_shape=struc...  1.56 us
    pallas_call x1, Pallas kernels, per_device(): pl.pallas_call(prepare_kernel, out_shape=[struct((fields.shape[1], cells)...  1.48 us
  transfers between devices with their start and end apart: 7, of which 1 were waited for; matrix products, arithmetic and copies ran while one was open for 0% of the time, Pallas kernels for 21%

profile of v4, /device:TPU:0, one launch (start us, length us, event | category | flops | bytes accessed | tf_op | source)
XLA Modules:
  0.0 33.2 jit_solution(12651011488667068902)
XLA Ops:
  0.6 0.5 %collective-permute-start = (bf16[4,8192]{1,0:T(4,128)(2,1)}, bf16[4,8192]{1,0:T(4,128)(2,1)S(1)}, u32[]{:S(2)}, u32[]{:S(2)}) collective-permute-start(bf16[4,8192]{1,0:T(4,128)(2,1)} %bitcast.36), channel_id=1, source_target_pairs={{0,16},{16,0},{1,17},{17,1},{2,18},{18,2},{3,19},{19,3},{4,20},{20... | collective-permute-start | bytes 196616 | tf_op jit(solution)/shard_map/ppermute | solution.py:628
  1.2 0.1 collective-permute-start.1
  1.2 1.3 %load.1 = (f32[8,8192]{1,0:T(8,128)S(1)}, f32[64,128]{1,0:T(8,128)S(1)}, f32[3,64,128]{2,1,0:T(8,128)S(1)}, s32[3,64,128]{2,1,0:T(8,128)S(1)}, s32[64,128]{1,0:T...) custom-call(f32[8,8192]{1,0:T(8,128)} %bitcast.20, ...), custom_call_target="tpu_custom_call" | custom-call | tf_op jit(solution)/shard_map/load/pallas_call | solution.py:648
  2.5 0.0 collective-permute-done.1.sends
  2.5 0.0 collective-permute-done.surface
  2.5 0.3 pack.1
  2.8 3.0 %collective-permute-start.2 = (bf16[256,128]{1,0:T(8,128)(2,1)S(1)}, bf16[256,128]{1,0:T(8,128)(2,1)S(1)}, u32[]{:S(2)}, u32[]{:S(2)}) collective-permute-start(bf16[256,128]{1,0:T(8,128)(2,1)S(1)} %get-tuple-element.57), channel_id=1, source_target_pairs={{0,2},{1,3},{2,4},{3,5},{4,6},{5,7},{6,8},{7,9},{8,10},{9,11},{10,... | collective-permute-start | bytes 196616 | tf_op jit(solution)/shard_map/ppermute | solution.py:682
  5.8 4.1 %collective-permute-start.3 = (bf16[256,128]{1,0:T(8,128)(2,1)S(1)}, bf16[256,128]{1,0:T(8,128)(2,1)S(1)}, u32[]{:S(2)}, u32[]{:S(2)}) collective-permute-start(bf16[256,128]{1,0:T(8,128)(2,1)S(1)} %get-tuple-element.58), channel_id=1, source_target_pairs={{1,2},{3,4},{5,6},{7,8},{9,10},{11,12},{13,14},{15,0},{2,1},{4,3},... | collective-permute-start | bytes 196616 | tf_op jit(solution)/shard_map/ppermute | solution.py:689
  9.9 1.9 %collective-permute-start.4 = (bf16[256,128]{1,0:T(8,128)(2,1)S(1)}, bf16[256,128]{1,0:T(8,128)(2,1)S(1)}, u32[]{:S(2)}, u32[]{:S(2)}) collective-permute-start(bf16[256,128]{1,0:T(8,128)(2,1)S(1)} %get-tuple-element.59), channel_id=1, source_target_pairs={{0,14},{1,15},{2,0},{3,1},{4,2},{5,3},{6,4},{7,5},{8,6},{9,7},{10,... | collective-permute-start | bytes 196616 | tf_op jit(solution)/shard_map/ppermute | solution.py:682
  11.8 0.2 collective-permute-start.5
  12.0 4.3 %stencil.1 = (f32[8,8192]{1,0:T(8,128)S(1)}, f32[64,128]{1,0:T(8,128)S(1)}, f32[64,128]{1,0:T(8,128)S(1)}, s32[3,64,128]{2,1,0:T(8,128)S(1)}, s32[8,128]{1,0:T(8...) custom-call(bf16[128,128]{1,0:T(8,128)(2,1)S(1)} %get-tuple-element., ...), custom_call_target="tpu_custom_call" | custom-call | tf_op jit(solution)/shard_map/stencil/pallas_call | solution.py:696
  16.3 0.0 collective-permute-done.2.from_left2
  16.3 0.0 collective-permute-done.3.far
  16.3 0.0 collective-permute-done.4.from_right2
  16.4 0.0 collective-permute-done.5.near
  16.4 3.7 %forward.1 = (f32[4,64,128]{2,1,0:T(8,128)S(1)}, f32[64,128]{1,0:T(8,128)S(1)}, f32[64,128]{1,0:T(8,128)S(1)}, f32[32,128]{1,0:T(8,128)S(1)}, f32[256,128]{1,0:T...) custom-call(bf16[160,128,128]{2,1,0:T(8,128)(2,1)S(1)} %get-tuple-element.56.tiles, ...), custom_call_target="tpu_custom_call" | custom-call | tf_op jit(solution)/shard_map/forward/pallas_call | solution.py:716
  20.0 4.0 %all-to-all-start = ((f32[16,8,128]{2,1,0:T(8,128)}), f32[16,8,128]{2,1,0:T(8,128)S(1)}, u32[]{:S(2)}, u32[]{:S(2)}) async-start(f32[16,8,128]{2,1,0:T(8,128)} %get-tuple-element.73), calls=%async_computation | async-start | bytes 131072 | tf_op jit(solution)/shard_map/all_to_all | solution.py:743
  24.1 1.5 %prepare.1 = (f32[8,8192]{1,0:T(8,128)}, f32[4,8192]{1,0:T(4,128)}, f32[16,48,128]{2,1,0:T(8,128)S(1)}) custom-call(f32[8,8192]{1,0:T(8,128)S(1)} %get-tuple-element.55.fresh, f32[8,256]{1,0:T(8,128)S(1)} %get-tuple-element.69.ends_new, f32[4,64,128]{2,1,0:T(8,128)S(1)} %get-tuple-element.70.summed, bf16[256,128]{1,0:T(8,128)(2,1)S(1)} %collective-permute-done.3.far, ...), custom_call_target="tpu_custom_call" | custom-call | tf_op jit(solution)/shard_map/prepare/pallas_call | solution.py:744
  25.6 6.0 %all-to-all-done.arrived = f32[16,8,128]{2,1,0:T(8,128)S(1)} async-done(((f32[16,8,128]{2,1,0:T(8,128)}), f32[16,8,128]{2,1,0:T(8,128)S(1)}, u32[]{:S(2)}, u32[]{:S(2)}) %all-to-all-start) | async-done | bytes 65568 | tf_op jit(solution)/shard_map/all_to_all | solution.py:743
  31.6 1.6 %backward.1 = f32[64,128]{1,0:T(8,128)} custom-call(f32[16,8,128]{2,1,0:T(8,128)S(1)} %all-to-all-done.arrived, f32[16,48,128]{2,1,0:T(8,128)S(1)} %get-tuple-element.74.weights, f32[32,128]{1,0:T(8,128)S(1)} %get-tuple-element.75.source, f32[256,128]{1,0:T(8,128)S(1)} %get-tuple-element.76.frame, f32[64,128]{1,0:T(8,128)S(1)} %get-tuple-element.77.force, ...), custom_call_target="tpu_custom_call" | custom-call | tf_op jit(solution)/shard_map/backward/pallas_call | solution.py:760
Async XLA Ops:
  0.6 1.9 %collective-permute-start = (bf16[4,8192]{1,0:T(4,128)(2,1)}, bf16[4,8192]{1,0:T(4,128)(2,1)S(1)}, u32[]{:S(2)}, u32[]{:S(2)}) collective-permute-start(bf16[4,8192]{1,0:T(4,128)(2,1)} %bitcast.36), channel_id=1, source_target_pairs={{0,16},{16,0},{1,17},{17,1},{2,18},{18,2},{3,19},{19,3},{4,20},{20... | collective-permute-start | bytes 196616 | tf_op jit(solution)/shard_map/ppermute | solution.py:628
  1.2 1.4 %collective-permute-start.1 = (s32[1,160]{1,0:T(1,128)}, s32[1,160]{1,0:T(1,128)S(1)}, u32[]{:S(2)}, u32[]{:S(2)}) collective-permute-start(s32[1,160]{1,0:T(1,128)} %bitcast.37), channel_id=1, source_target_pairs={{0,16},{16,0},{1,17},{17,1},{2,18},{18,2},{3,19},{19,3},{4,20},{20... | collective-permute-start | bytes 1928 | tf_op jit(solution)/shard_map/ppermute | solution.py:629
  2.8 13.5 %collective-permute-start.2 = (bf16[256,128]{1,0:T(8,128)(2,1)S(1)}, bf16[256,128]{1,0:T(8,128)(2,1)S(1)}, u32[]{:S(2)}, u32[]{:S(2)}) collective-permute-start(bf16[256,128]{1,0:T(8,128)(2,1)S(1)} %get-tuple-element.57), channel_id=1, source_target_pairs={{0,2},{1,3},{2,4},{3,5},{4,6},{5,7},{6,8},{7,9},{8,10},{9,11},{10,... | collective-permute-start | bytes 196616 | tf_op jit(solution)/shard_map/ppermute | solution.py:682
  5.8 10.5 %collective-permute-start.3 = (bf16[256,128]{1,0:T(8,128)(2,1)S(1)}, bf16[256,128]{1,0:T(8,128)(2,1)S(1)}, u32[]{:S(2)}, u32[]{:S(2)}) collective-permute-start(bf16[256,128]{1,0:T(8,128)(2,1)S(1)} %get-tuple-element.58), channel_id=1, source_target_pairs={{1,2},{3,4},{5,6},{7,8},{9,10},{11,12},{13,14},{15,0},{2,1},{4,3},... | collective-permute-start | bytes 196616 | tf_op jit(solution)/shard_map/ppermute | solution.py:689
  9.9 6.4 %collective-permute-start.4 = (bf16[256,128]{1,0:T(8,128)(2,1)S(1)}, bf16[256,128]{1,0:T(8,128)(2,1)S(1)}, u32[]{:S(2)}, u32[]{:S(2)}) collective-permute-start(bf16[256,128]{1,0:T(8,128)(2,1)S(1)} %get-tuple-element.59), channel_id=1, source_target_pairs={{0,14},{1,15},{2,0},{3,1},{4,2},{5,3},{6,4},{7,5},{8,6},{9,7},{10,... | collective-permute-start | bytes 196616 | tf_op jit(solution)/shard_map/ppermute | solution.py:682
  11.8 4.6 %collective-permute-start.5 = (bf16[256,128]{1,0:T(8,128)(2,1)S(1)}, bf16[256,128]{1,0:T(8,128)(2,1)S(1)}, u32[]{:S(2)}, u32[]{:S(2)}) collective-permute-start(bf16[256,128]{1,0:T(8,128)(2,1)S(1)} %get-tuple-element.60), channel_id=1, source_target_pairs={{0,1},{2,3},{4,5},{6,7},{8,9},{10,11},{12,13},{14,15},{1,0},{3,2},... | collective-permute-start | bytes 196616 | tf_op jit(solution)/shard_map/ppermute | solution.py:689
  20.0 11.6 %all-to-all-start = ((f32[16,8,128]{2,1,0:T(8,128)}), f32[16,8,128]{2,1,0:T(8,128)S(1)}, u32[]{:S(2)}, u32[]{:S(2)}) async-start(f32[16,8,128]{2,1,0:T(8,128)} %get-tuple-element.73), calls=%async_computation | async-start | bytes 131072 | tf_op jit(solution)/shard_map/all_to_all | solution.py:743

commit v5 on v4

--- a/solution.py
+++ b/solution.py
@@ -36,12 +36,9 @@
     return jnp.broadcast_to(row, (count, row.shape[1]))
 
 
-def split3(x):
+def split2(x):
     high = x.astype(BF16)
-    rest = x - high.astype(F32)
-    middle = rest.astype(BF16)
-    low = (rest - middle.astype(F32)).astype(BF16)
-    return high, middle, low
+    return high, (x - high.astype(F32)).astype(BF16)
 
 
 def dot_nt(a, b):
@@ -153,20 +150,22 @@
 
 
 def stencil_kernel(
-    here, scalars, fields, edge, table, old, owner, slots, entry_block, tiles,
-    fresh, force, beside_old, window, ends_row, ends_lane, hot, member, tile_buffer, padded, sems,
+    here, scalars, fields, edge, table, old, diagonal, owner, slots, entry_block, tiles,
+    fresh, force, beside_old, window, ends_row, ends_lane, hot, member, damping, tile_buffer, padded, sems,
 ):
     del here
     parts = sems.shape[0]
     step = tiles.shape[0] // parts
-    loads = [
-        pltpu.make_async_copy(
-            tiles.at[pl.ds(part * step, step)], tile_buffer.at[pl.ds(part * step, step)], sems.at[part]
-        )
-        for part in range(parts)
-    ]
-    for load in loads:
-        load.start()
+
+    def load(part):
+        span = pl.ds(part * step, step)
+        return pltpu.make_async_copy(tiles.at[span], tile_buffer.at[span], sems.at[part])
+
+    def begin(part, carry):
+        load(part).start()
+        return carry
+
+    lax.fori_loop(0, parts, begin, 0)
     blocks = old.shape[0]
     levels = fields.shape[0]
     speed = scalars[pl.ds(0, 8), :]
@@ -174,6 +173,9 @@
     starts = lax.broadcasted_iota(I32, (blocks, LANES), 0) * LANES
     total = edge[0] + edge[1] + edge[2]
     inverse = 1.0 / total
+    fine_total = diagonal[...] + total
+    damping[0] = fine_total
+    damping[1] = RELAXATION / fine_total
     for link in range(3):
         window[link] = table[link] - starts
     blank = jnp.zeros((levels, LANES), F32)
@@ -205,12 +207,17 @@
     padded[pl.ds(8 + blocks, 8), :] = jnp.zeros((8, LANES), F32)
     padded[pl.ds(8, blocks), :] = old[...]
     beside_old[...] = neighbour_sum(padded, edge, window, blocks)
-    hot[...] = jnp.where(
-        lax.broadcasted_iota(I32, hot.shape, 0) == slots[...], 1.0, 0.0
-    ).astype(BF16)
-    member[...] = jnp.where(
-        lax.broadcasted_iota(I32, member.shape, 0) == entry_block[...], 1.0, 0.0
-    ).astype(BF16)
+    names = jnp.where(
+        lax.broadcasted_iota(I32, (slots.shape[1], slots.shape[1]), 0) == slots[...], 1.0, 0.0
+    )
+    hot[...] = jnp.transpose(names).astype(BF16)
+    half = entry_block.shape[1] // 2
+    for part in range(2):
+        member[part] = jnp.where(
+            lax.broadcasted_iota(I32, (blocks, half), 0) == entry_block[:, part * half : (part + 1) * half],
+            1.0,
+            0.0,
+        ).astype(BF16)
 
     firsts = ends_row.shape[0] * LANES
     ident = lax.broadcasted_iota(I32, ends_row.shape, 0) * LANES + lax.broadcasted_iota(
@@ -232,8 +239,8 @@
         lanes = jnp.where(value <= ident, lanes + bit, lanes)
     ends_row[...] = rows
     ends_lane[...] = lanes
-    for load in loads:
-        load.wait()
+    for part in range(parts):
+        load(part).wait()
 
 
 def neighbour_sum(padded, edges, window, blocks):
@@ -291,17 +298,31 @@
     right = jnp.concatenate([triangle(), ones], axis=1)
     count = values.shape[0]
     out = jnp.dot(
-        jnp.concatenate(split3(values), axis=0), right, preferred_element_type=F32
-    )
-    out = out[:count] + out[count : 2 * count] + out[2 * count :]
+        jnp.concatenate(split2(values), axis=0), right, preferred_element_type=F32
+    )
+    out = out[:count] + out[count:]
     return out[:, :LANES], out[:, LANES:]
+
+
+def rows_before(values):
+    sublane = lax.broadcasted_iota(I32, (8, LANES), 0)
+    run = jnp.zeros((8, LANES), F32)
+    result = []
+    for at in range(0, values.shape[0], 8):
+        piece = values[at : at + 8]
+        total = piece
+        for distance in (1, 2, 4):
+            total = total + jnp.where(sublane >= distance, pltpu.roll(total, distance, axis=0), 0.0)
+        result.append(run + (total - piece))
+        run = run + wide(total[7:8])
+    return jnp.concatenate(result, axis=0), run
 
 
 def forward_kernel(
     tiles, scalars, from_left2, far, from_right2, near, here, hot, member, fields, edges, window, old,
-    diagonal, force_part, beside_old, ends_row, ends_lane, fresh, ctable, cedge, cdiag, cowner,
+    damping, force_part, beside_old, ends_row, ends_lane, fresh, ctable, cedge, cdiag, cowner,
     summed, force_out, smooth_out, source_out, frame, ends_out, message,
-    picked, products, padded, prefixed, totals, arrivals,
+    picked, products, padded, prefixed, arrivals,
 ):
     tile = lax.axis_index("tile")
     tile_count = lax.axis_size("tile")
@@ -317,7 +338,7 @@
         source = jnp.concatenate(
             [rows[channel * each : (channel + 1) * each] for rows in sources], axis=0
         )
-        picked[pl.ds(channel, entries, stride=4), :] = dot_tn(hot[...], source)
+        picked[pl.ds(channel, entries, stride=4), :] = jnp.dot(hot[...], source, preferred_element_type=F32)
 
     arrivals[0] = from_left[:base].astype(F32)
     arrivals[1] = from_right[:base].astype(F32)
@@ -337,12 +358,15 @@
         product = dot_nt(rows.astype(BF16), weights)
         products[pl.ds(16 * group, 8), :] = product[0:8, :LANES]
         products[pl.ds(16 * group + 8, 8), :] = product[8:16, LANES:]
-    spread = []
+    half = entries // 2
     for channel in range(4):
-        spread.append(jnp.concatenate(split3(products[pl.ds(channel, entries, stride=4), :]), axis=1))
-    for channel in range(4):
-        value = jnp.dot(member[...], spread[channel], preferred_element_type=F32)
-        summed[channel] = value[:, :LANES] + value[:, LANES : 2 * LANES] + value[:, 2 * LANES :]
+        value = jnp.zeros((blocks, 2 * LANES), F32)
+        for part in range(2):
+            rows = products[pl.ds(4 * half * part + channel, half, stride=4), :]
+            value = value + jnp.dot(
+                member[part], jnp.concatenate(split2(rows), axis=1), preferred_element_type=F32
+            )
+        summed[channel] = value[:, :LANES] + value[:, LANES:]
 
     speed = scalars[pl.ds(0, 8), :]
     share = scalars[pl.ds(8, 8), :]
@@ -373,28 +397,25 @@
     for channel in range(4):
         force = force + scalars[pl.ds(16 + channel, 1), :] * summed[channel]
     force_out[...] = force
-    total = diagonal[...] + edges[0] + edges[1] + edges[2]
+    total, damp = damping[0], damping[1]
     smooth_out[...] = beside_old[...]
     smooth_out[pl.ds(0, 1), :] += beside_extra[0]
     smooth_out[pl.ds(blocks - 1, 1), :] += beside_extra[1]
     previous = old[...]
-    smooth = previous + RELAXATION * (force - (total * previous - smooth_out[...])) / total
+    smooth = previous + damp * (force - (total * previous - smooth_out[...]))
     smooth_out[...] = smooth
     padded[pl.ds(8, blocks), :] = smooth
     residual = force - total * smooth + neighbour_sum(padded, edges, window, blocks)
 
     inner, whole = prefix(residual)
-    prefixed[...] = inner
-    totals[...] = whole
+    before, run = rows_before(whole)
+    prefixed[...] = inner + before
     rows, lanes = ends_row[...], ends_lane[...]
     count = rows.shape[0]
-    run = jnp.zeros((count, LANES), F32)
-    ends = jnp.zeros((count, LANES), F32)
+    ends = run[:count]
     for block in range(blocks):
-        value = gather_lanes(wide(prefixed[pl.ds(block, 1), :], count), lanes) + run
+        value = gather_lanes(wide(prefixed[pl.ds(block, 1), :], count), lanes)
         ends = jnp.where(rows == block, value, ends)
-        run = run + wide(totals[pl.ds(block, 1), :], count)
-    ends = jnp.where(rows == blocks, run, ends)
     own_source = ends - previous_one(ends)
 
     lane = lax.broadcasted_iota(I32, (1, LANES), 1)
@@ -465,20 +486,19 @@
     for link in range(3):
         frame[pl.ds(6 * FRAME, FRAME), :] += frame[pl.ds((3 + link) * FRAME, FRAME), :]
     source = source_out[...]
-    first = RELAXATION * source / frame[pl.ds(6 * FRAME, FRAME), :]
+    first = (RELAXATION / frame[pl.ds(6 * FRAME, FRAME), :]) * source
     residual = (1.0 - RELAXATION) * source + first_level_sum(first, frame)
     codes = frame[pl.ds(7 * FRAME, FRAME), :].astype(I32)
-    pieces = split3(residual)
+    pieces = split2(residual)
     left_side, right_side = [], []
-    bins = lax.broadcasted_iota(I32, (LANES, LANES), 0)
+    bins = lax.broadcasted_iota(I32, (3 * bottoms, LANES), 0)
+    rest = jnp.zeros((LANES - 3 * bottoms, LANES), BF16)
     for row in range(OWN - 2, OWN + frows + 2):
         left_side.append(jnp.concatenate([p[row : row + 1] for p in pieces], axis=0))
-        right_side.append(
-            jnp.where(bins == codes[row : row + 1], 1.0, 0.0).astype(BF16)
-        )
+        named = jnp.where(bins == codes[row : row + 1], 1.0, 0.0).astype(BF16)
+        right_side.append(jnp.concatenate([named, rest], axis=0))
     bottom = dot_nt(jnp.concatenate(left_side, axis=1), jnp.concatenate(right_side, axis=1))
-    bottom = bottom[0:1] + bottom[1:2] + bottom[2:3]
-    bottom = jnp.where(lane < 3 * bottoms, bottom, 0.0)
+    bottom = bottom[0:1] + bottom[1:2]
 
     to_left = jnp.concatenate(
         [bottom, padded[pl.ds(8, 1), :], own_source[0:2], rim_source[0], jnp.zeros((3, LANES), F32)], axis=0
@@ -536,7 +556,7 @@
 
 
 def backward_kernel(
-    frame_rows, arrived, weights, source, frame, force, smooth, edges, window, diagonal, owner, far, near,
+    frame_rows, arrived, weights, source, frame, force, smooth, edges, window, damping, owner, far, near,
     height, frame_source, padded, third_rows,
 ):
     tile = lax.axis_index("tile")
@@ -550,8 +570,7 @@
         partial = partial + weights[other] * wide(arrived[other, pl.ds(0, 1), :], count)
     partial = jnp.concatenate([partial, jnp.zeros((LANES - count, LANES), F32)], axis=0)
     ones = jnp.ones((8, LANES), BF16)
-    pieces = split3(partial)
-    bottom = dot_nt(ones, pieces[0]) + dot_nt(ones, pieces[1]) + dot_nt(ones, pieces[2])
+    bottom = dot_nt(jnp.concatenate([ones, ones], axis=1), jnp.concatenate(split2(partial), axis=1))
 
     frows = frame_rows
     frame_source[...] = source[...]
@@ -562,10 +581,9 @@
     total_source = frame_source[...]
     total = frame[pl.ds(6 * FRAME, FRAME), :]
     codes = frame[pl.ds(7 * FRAME, FRAME), :].astype(I32)
-    second = RELAXATION * total_source / total + gather_lanes(wide(bottom[0:1], FRAME), codes)
-    third = second + RELAXATION * (
-        total_source - total * second + first_level_sum(second, frame)
-    ) / total
+    damp = RELAXATION / total
+    second = damp * total_source + gather_lanes(wide(bottom[0:1], FRAME), codes)
+    third = second + damp * (total_source - total * second + first_level_sum(second, frame))
     third_rows[...] = third
 
     owners = owner[...]
@@ -588,9 +606,8 @@
     right_rim = right[1:2] + gather_lanes(wide(third_rows[pl.ds(OWN + frows, 1), :]), wide(right_owner))[0:1]
     padded[pl.ds(7, 1), :] = left_rim
     padded[pl.ds(8 + blocks, 1), :] = right_rim
-    fine_total = diagonal[...] + edges[0] + edges[1] + edges[2]
     beside = neighbour_sum(padded, edges, window, blocks)
-    height[...] = corrected + RELAXATION * (force[...] - (fine_total * corrected - beside)) / fine_total
+    height[...] = corrected + damping[1] * (force[...] - (damping[0] * corrected - beside))
 
 
 def in_hbm(array):
@@ -693,7 +710,7 @@
     from_right2 = shifted(to_left2, -2)
     near = swapped(near, 0)
 
-    fresh, force_part, beside_old, window, ends_row, ends_lane, hot, member, tiles = pl.pallas_call(
+    fresh, force_part, beside_old, window, ends_row, ends_lane, hot, member, damping, tiles = pl.pallas_call(
         stencil_kernel,
         out_shape=[
             struct((fields.shape[1], cells)),
@@ -702,16 +719,17 @@
             struct((3, blocks, LANES), I32),
             struct((frows, LANES), I32),
             struct((frows, LANES), I32),
-            struct((slots, entries), BF16),
-            struct((blocks, entries), BF16),
+            struct((entries, slots), BF16),
+            struct((2, blocks, entries // 2), BF16),
+            struct((2, blocks, LANES)),
             pltpu.VMEM(remap_tiles.shape[2:], BF16),
         ],
-        in_specs=[VMEM] * 9 + [ANY],
-        out_specs=[VMEM] * 9,
+        in_specs=[VMEM] * 10 + [ANY],
+        out_specs=[VMEM] * 10,
         scratch_shapes=[pltpu.VMEM((blocks + 16, LANES), F32), pltpu.SemaphoreType.DMA((math.gcd(entries, 8),))],
         compiler_params=PARAMS,
         name="stencil",
-    )(here, scalars, current, edges, table, old, owner, slot, block, in_hbm(remap_tiles[0, 0]))
+    )(here, scalars, current, edges, table, old, diagonal, owner, slot, block, in_hbm(remap_tiles[0, 0]))
 
     summed, force, smooth, source, frame, ends_new, message = pl.pallas_call(
         forward_kernel,
@@ -731,14 +749,13 @@
             pltpu.VMEM((4 * entries, LANES), F32),
             pltpu.VMEM((blocks + 16, LANES), F32),
             pltpu.VMEM((blocks, LANES), F32),
-            pltpu.VMEM((blocks, LANES), F32),
             pltpu.VMEM((2, base, LANES), F32),
         ],
         compiler_params=PARAMS,
         name="forward",
     )(
         tiles, scalars, from_left2, far, from_right2, near, here, hot, member, current, edges, window, old,
-        diagonal, force_part, beside_old, ends_row, ends_lane, fresh, ctable, cedge, cdiag, cowner,
+        damping, force_part, beside_old, ends_row, ends_lane, fresh, ctable, cedge, cdiag, cowner,
     )
     arrived = lax.all_to_all(message, "tile", split_axis=0, concat_axis=0, tiled=True)
     advanced, received, weights = pl.pallas_call(
@@ -769,7 +786,7 @@
         ],
         compiler_params=PARAMS,
         name="backward",
-    )(arrived, weights, source, frame, force, smooth, edges, window, diagonal, owner, far, near)
+    )(arrived, weights, source, frame, force, smooth, edges, window, damping, owner, far, near)
     return advanced[None], received[None], height.reshape(1, cells)
 
 

time: 33.4 us -> 33.2 us (level)
  Pallas kernels: 12.6 us -> 10.7 us
  waiting for transfers between devices: 6.06 us -> 7.43 us
    pallas_call x1, Pallas kernels: 4.32 us -> 2.67 us  [per_device(): pl.pallas_call(stencil_kernel, out_shape=[struct((fields.shape[1], cells)...]
    ppermute x2, waiting for transfers between devices: 0.01 us -> 1.24 us  [swapped(): return lax.ppermute(array, 'tile', pairs + [(j, i) for i, j in pairs])]
  transfers between devices with their start and end apart: 7 -> 7, of which waited for: 1 -> 3; matrix products, arithmetic and copies ran while one was open for 0% -> 0% of each run, Pallas kernels for 21% -> 16%
where the time goes in v5:
time: 33.2 us; the launch traced here: 32.9 us
  starting transfers between devices  14.1 us (42%)
  Pallas kernels  10.7 us (32%)
  waiting for transfers between devices  7.43 us (22%)
  between operations  0.71 us (2%)
    all_to_all x1, waiting for transfers between devices, per_device(): lax.all_to_all(message, 'tile', split_axis=0, concat_axis=0, tiled=True)  6.05 us
    ppermute x2, starting transfers between devices, shifted(): lax.ppermute(array, 'tile', [(i, (i + distance) % tile_count) for i in ra...  4.86 us
    all_to_all x1, starting transfers between devices, per_device(): lax.all_to_all(message, 'tile', split_axis=0, concat_axis=0, tiled=True)  4.35 us
    ppermute x2, starting transfers between devices, swapped(): return lax.ppermute(array, 'tile', pairs + [(j, i) for i, j in pairs])  4.33 us
    pallas_call x1, Pallas kernels, per_device(): pl.pallas_call(forward_kernel, out_shape=[struct((channels, blocks, LANES...  3.45 us
    pallas_call x1, Pallas kernels, per_device(): pl.pallas_call(stencil_kernel, out_shape=[struct((fields.shape[1], cells)...  2.67 us
    pallas_call x1, Pallas kernels, per_device(): pl.pallas_call(functools.partial(backward_kernel, frows), out_shape=struc...  1.55 us
    pallas_call x1, Pallas kernels, per_device(): pl.pallas_call(prepare_kernel, out_shape=[struct((fields.shape[1], cells)...  1.48 us
  transfers between devices with their start and end apart: 7, of which 3 were waited for; matrix products, arithmetic and copies ran while one was open for 0% of the time, Pallas kernels for 16%

profile of v5, /device:TPU:0, one launch (start us, length us, event | category | flops | bytes accessed | tf_op | source)
XLA Modules:
  0.0 32.9 jit_solution(6150668802917469453)
XLA Ops:
  0.6 0.5 %collective-permute-start = (bf16[4,8192]{1,0:T(4,128)(2,1)}, bf16[4,8192]{1,0:T(4,128)(2,1)S(1)}, u32[]{:S(2)}, u32[]{:S(2)}) collective-permute-start(bf16[4,8192]{1,0:T(4,128)(2,1)} %bitcast.36), channel_id=1, source_target_pairs={{0,16},{16,0},{1,17},{17,1},{2,18},{18,2},{3,19},{19,3},{4,20},{20... | collective-permute-start | bytes 196616 | tf_op jit(solution)/shard_map/ppermute | solution.py:645
  1.2 0.1 collective-permute-start.1
  1.2 1.3 %load.1 = (f32[8,8192]{1,0:T(8,128)S(1)}, f32[64,128]{1,0:T(8,128)S(1)}, f32[3,64,128]{2,1,0:T(8,128)S(1)}, s32[3,64,128]{2,1,0:T(8,128)S(1)}, s32[64,128]{1,0:T...) custom-call(f32[8,8192]{1,0:T(8,128)} %bitcast.20, ...), custom_call_target="tpu_custom_call" | custom-call | tf_op jit(solution)/shard_map/load/pallas_call | solution.py:665
  2.5 0.0 collective-permute-done.1.sends
  2.5 0.0 collective-permute-done.surface
  2.5 0.3 pack.1
  2.8 3.0 %collective-permute-start.2 = (bf16[256,128]{1,0:T(8,128)(2,1)S(1)}, bf16[256,128]{1,0:T(8,128)(2,1)S(1)}, u32[]{:S(2)}, u32[]{:S(2)}) collective-permute-start(bf16[256,128]{1,0:T(8,128)(2,1)S(1)} %get-tuple-element.59), channel_id=1, source_target_pairs={{0,2},{1,3},{2,4},{3,5},{4,6},{5,7},{6,8},{7,9},{8,10},{9,11},{10,... | collective-permute-start | bytes 196616 | tf_op jit(solution)/shard_map/ppermute | solution.py:699
  5.8 4.1 %collective-permute-start.3 = (bf16[256,128]{1,0:T(8,128)(2,1)S(1)}, bf16[256,128]{1,0:T(8,128)(2,1)S(1)}, u32[]{:S(2)}, u32[]{:S(2)}) collective-permute-start(bf16[256,128]{1,0:T(8,128)(2,1)S(1)} %get-tuple-element.60), channel_id=1, source_target_pairs={{1,2},{3,4},{5,6},{7,8},{9,10},{11,12},{13,14},{15,0},{2,1},{4,3},... | collective-permute-start | bytes 196616 | tf_op jit(solution)/shard_map/ppermute | solution.py:706
  9.9 1.9 %collective-permute-start.4 = (bf16[256,128]{1,0:T(8,128)(2,1)S(1)}, bf16[256,128]{1,0:T(8,128)(2,1)S(1)}, u32[]{:S(2)}, u32[]{:S(2)}) collective-permute-start(bf16[256,128]{1,0:T(8,128)(2,1)S(1)} %get-tuple-element.61), channel_id=1, source_target_pairs={{0,14},{1,15},{2,0},{3,1},{4,2},{5,3},{6,4},{7,5},{8,6},{9,7},{10,... | collective-permute-start | bytes 196616 | tf_op jit(solution)/shard_map/ppermute | solution.py:699
  11.8 0.2 collective-permute-start.5
  12.0 2.7 %stencil.1 = (f32[8,8192]{1,0:T(8,128)S(1)}, f32[64,128]{1,0:T(8,128)S(1)}, f32[64,128]{1,0:T(8,128)S(1)}, s32[3,64,128]{2,1,0:T(8,128)S(1)}, s32[8,128]{1,0:T(8...) custom-call(bf16[128,128]{1,0:T(8,128)(2,1)S(1)} %get-tuple-element., ...), custom_call_target="tpu_custom_call" | custom-call | tf_op jit(solution)/shard_map/stencil/pallas_call | solution.py:713
  14.7 0.0 collective-permute-done.2.from_left2
  14.7 0.0 collective-permute-done.3.far
  14.7 0.1 collective-permute-done.4.from_right2
  14.8 1.2 %collective-permute-done.5.near = bf16[256,128]{1,0:T(8,128)(2,1)S(1)} collective-permute-done((bf16[256,128]{1,0:T(8,128)(2,1)S(1)}, bf16[256,128]{1,0:T(8,128)(2,1)S(1)}, u32[]{:S(2)}, u32[]{:S(2)}) %collective-permute-start.5) | collective-permute-done | bytes 65568 | tf_op jit(solution)/shard_map/ppermute | solution.py:706
  16.1 3.4 %forward.1 = (f32[4,64,128]{2,1,0:T(8,128)S(1)}, f32[64,128]{1,0:T(8,128)S(1)}, f32[64,128]{1,0:T(8,128)S(1)}, f32[32,128]{1,0:T(8,128)S(1)}, f32[256,128]{1,0:T...) custom-call(bf16[160,128,128]{2,1,0:T(8,128)(2,1)S(1)} %get-tuple-element.58.tiles, ...), custom_call_target="tpu_custom_call" | custom-call | tf_op jit(solution)/shard_map/forward/pallas_call | solution.py:734
  19.5 4.3 %all-to-all-start = ((f32[16,8,128]{2,1,0:T(8,128)}), f32[16,8,128]{2,1,0:T(8,128)S(1)}, u32[]{:S(2)}, u32[]{:S(2)}) async-start(f32[16,8,128]{2,1,0:T(8,128)} %get-tuple-element.75), calls=%async_computation | async-start | bytes 131072 | tf_op jit(solution)/shard_map/all_to_all | solution.py:760
  23.9 1.5 %prepare.1 = (f32[8,8192]{1,0:T(8,128)}, f32[4,8192]{1,0:T(4,128)}, f32[16,48,128]{2,1,0:T(8,128)S(1)}) custom-call(f32[8,8192]{1,0:T(8,128)S(1)} %get-tuple-element.57.fresh, f32[8,256]{1,0:T(8,128)S(1)} %get-tuple-element.71.ends_new, f32[4,64,128]{2,1,0:T(8,128)S(1)} %get-tuple-element.72.summed, bf16[256,128]{1,0:T(8,128)(2,1)S(1)} %collective-permute-done.3.far, ...), custom_call_target="tpu_custom_call" | custom-call | tf_op jit(solution)/shard_map/prepare/pallas_call | solution.py:761
  25.3 6.0 %all-to-all-done.arrived = f32[16,8,128]{2,1,0:T(8,128)S(1)} async-done(((f32[16,8,128]{2,1,0:T(8,128)}), f32[16,8,128]{2,1,0:T(8,128)S(1)}, u32[]{:S(2)}, u32[]{:S(2)}) %all-to-all-start) | async-done | bytes 65568 | tf_op jit(solution)/shard_map/all_to_all | solution.py:760
  31.4 1.6 %backward.1 = f32[64,128]{1,0:T(8,128)} custom-call(f32[16,8,128]{2,1,0:T(8,128)S(1)} %all-to-all-done.arrived, f32[16,48,128]{2,1,0:T(8,128)S(1)} %get-tuple-element.76.weights, f32[32,128]{1,0:T(8,128)S(1)} %get-tuple-element.77.source, f32[256,128]{1,0:T(8,128)S(1)} %get-tuple-element.78.frame, f32[64,128]{1,0:T(8,128)S(1)} %get-tuple-element.79.force, ...), custom_call_target="tpu_custom_call" | custom-call | tf_op jit(solution)/shard_map/backward/pallas_call | solution.py:777
Async XLA Ops:
  0.6 1.9 %collective-permute-start = (bf16[4,8192]{1,0:T(4,128)(2,1)}, bf16[4,8192]{1,0:T(4,128)(2,1)S(1)}, u32[]{:S(2)}, u32[]{:S(2)}) collective-permute-start(bf16[4,8192]{1,0:T(4,128)(2,1)} %bitcast.36), channel_id=1, source_target_pairs={{0,16},{16,0},{1,17},{17,1},{2,18},{18,2},{3,19},{19,3},{4,20},{20... | collective-permute-start | bytes 196616 | tf_op jit(solution)/shard_map/ppermute | solution.py:645
  1.2 1.4 %collective-permute-start.1 = (s32[1,160]{1,0:T(1,128)}, s32[1,160]{1,0:T(1,128)S(1)}, u32[]{:S(2)}, u32[]{:S(2)}) collective-permute-start(s32[1,160]{1,0:T(1,128)} %bitcast.37), channel_id=1, source_target_pairs={{0,16},{16,0},{1,17},{17,1},{2,18},{18,2},{3,19},{19,3},{4,20},{20... | collective-permute-start | bytes 1928 | tf_op jit(solution)/shard_map/ppermute | solution.py:646
  2.8 11.9 %collective-permute-start.2 = (bf16[256,128]{1,0:T(8,128)(2,1)S(1)}, bf16[256,128]{1,0:T(8,128)(2,1)S(1)}, u32[]{:S(2)}, u32[]{:S(2)}) collective-permute-start(bf16[256,128]{1,0:T(8,128)(2,1)S(1)} %get-tuple-element.59), channel_id=1, source_target_pairs={{0,2},{1,3},{2,4},{3,5},{4,6},{5,7},{6,8},{7,9},{8,10},{9,11},{10,... | collective-permute-start | bytes 196616 | tf_op jit(solution)/shard_map/ppermute | solution.py:699
  5.8 8.9 %collective-permute-start.3 = (bf16[256,128]{1,0:T(8,128)(2,1)S(1)}, bf16[256,128]{1,0:T(8,128)(2,1)S(1)}, u32[]{:S(2)}, u32[]{:S(2)}) collective-permute-start(bf16[256,128]{1,0:T(8,128)(2,1)S(1)} %get-tuple-element.60), channel_id=1, source_target_pairs={{1,2},{3,4},{5,6},{7,8},{9,10},{11,12},{13,14},{15,0},{2,1},{4,3},... | collective-permute-start | bytes 196616 | tf_op jit(solution)/shard_map/ppermute | solution.py:706
  9.9 4.9 %collective-permute-start.4 = (bf16[256,128]{1,0:T(8,128)(2,1)S(1)}, bf16[256,128]{1,0:T(8,128)(2,1)S(1)}, u32[]{:S(2)}, u32[]{:S(2)}) collective-permute-start(bf16[256,128]{1,0:T(8,128)(2,1)S(1)} %get-tuple-element.61), channel_id=1, source_target_pairs={{0,14},{1,15},{2,0},{3,1},{4,2},{5,3},{6,4},{7,5},{8,6},{9,7},{10,... | collective-permute-start | bytes 196616 | tf_op jit(solution)/shard_map/ppermute | solution.py:699
  11.8 4.3 %collective-permute-start.5 = (bf16[256,128]{1,0:T(8,128)(2,1)S(1)}, bf16[256,128]{1,0:T(8,128)(2,1)S(1)}, u32[]{:S(2)}, u32[]{:S(2)}) collective-permute-start(bf16[256,128]{1,0:T(8,128)(2,1)S(1)} %get-tuple-element.62), channel_id=1, source_target_pairs={{0,1},{2,3},{4,5},{6,7},{8,9},{10,11},{12,13},{14,15},{1,0},{3,2},... | collective-permute-start | bytes 196616 | tf_op jit(solution)/shard_map/ppermute | solution.py:706
  19.5 11.9 %all-to-all-start = ((f32[16,8,128]{2,1,0:T(8,128)}), f32[16,8,128]{2,1,0:T(8,128)S(1)}, u32[]{:S(2)}, u32[]{:S(2)}) async-start(f32[16,8,128]{2,1,0:T(8,128)} %get-tuple-element.75), calls=%async_computation | async-start | bytes 131072 | tf_op jit(solution)/shard_map/all_to_all | solution.py:760

commit v6 on v5

--- a/solution.py
+++ b/solution.py
@@ -320,10 +320,31 @@
 
 def forward_kernel(
     tiles, scalars, from_left2, far, from_right2, near, here, hot, member, fields, edges, window, old,
-    damping, force_part, beside_old, ends_row, ends_lane, fresh, ctable, cedge, cdiag, cowner,
-    summed, force_out, smooth_out, source_out, frame, ends_out, message,
-    picked, products, padded, prefixed, arrivals,
+    damping, force_part, beside_old, ends_row, ends_lane, fresh, ctable, cedge, cdiag, cowner, cinverse,
+    force_out, smooth_out, source_out, frame, weights_out, fresh_out, received_out, message_out,
+    picked, products, padded, prefixed, arrivals, extended, ends, received, message, sems,
 ):
+    cells = fresh.shape[1]
+    middle = pl.ds(LANES, cells - 2 * LANES)
+    copies = [pltpu.make_async_copy(fresh.at[:, middle], fresh_out.at[:, middle], sems.at[0])]
+    for side in range(2):
+        copies.append(
+            pltpu.make_async_copy(
+                ends.at[side], fresh_out.at[:, pl.ds(side * (cells - LANES), LANES)], sems.at[1 + side]
+            )
+        )
+    copies.append(pltpu.make_async_copy(received, received_out, sems.at[3]))
+    copies.append(pltpu.make_async_copy(message, message_out, sems.at[4]))
+
+    def begin(which):
+        def body(_, carry):
+            for copy in which:
+                copy.start()
+            return carry
+
+        lax.fori_loop(0, 1 + lax.axis_index("tile") // lax.axis_size("tile"), body, 0)
+
+    begin(copies[:1])
     tile = lax.axis_index("tile")
     tile_count = lax.axis_size("tile")
     entries = tiles.shape[0]
@@ -358,16 +379,6 @@
         product = dot_nt(rows.astype(BF16), weights)
         products[pl.ds(16 * group, 8), :] = product[0:8, :LANES]
         products[pl.ds(16 * group + 8, 8), :] = product[8:16, LANES:]
-    half = entries // 2
-    for channel in range(4):
-        value = jnp.zeros((blocks, 2 * LANES), F32)
-        for part in range(2):
-            rows = products[pl.ds(4 * half * part + channel, half, stride=4), :]
-            value = value + jnp.dot(
-                member[part], jnp.concatenate(split2(rows), axis=1), preferred_element_type=F32
-            )
-        summed[channel] = value[:, :LANES] + value[:, LANES:]
-
     speed = scalars[pl.ds(0, 8), :]
     share = scalars[pl.ds(8, 8), :]
     force_out[...] = force_part[...]
@@ -389,14 +400,28 @@
             extra = extra + weight * gather_lanes(halo, index)
             extra_old = extra_old + weight * gather_lanes(wide(halo_old), index)
         change = speed * extra / wide(total)
-        ends_out[:, pl.ds(side * LANES, LANES)] = fresh[:, pl.ds(block * LANES, LANES)] + change
+        ends[side] = fresh[:, pl.ds(block * LANES, LANES)] + change
         force_out[pl.ds(block, 1), :] += jnp.sum(change * share, axis=0, keepdims=True)
         beside_extra.append(extra_old[0:1])
 
+    inverse_windows(arrivals.at[0], cinverse, arrivals.at[1], extended, weights_out)
+
     force = force_out[...]
+    half = entries // 2
     for channel in range(4):
-        force = force + scalars[pl.ds(16 + channel, 1), :] * summed[channel]
+        value = jnp.zeros((blocks, 2 * LANES), F32)
+        for part in range(2):
+            rows = products[pl.ds(4 * half * part + channel, half, stride=4), :]
+            value = value + jnp.dot(
+                member[part], jnp.concatenate(split2(rows), axis=1), preferred_element_type=F32
+            )
+        value = value[:, :LANES] + value[:, LANES:]
+        for block in range(blocks):
+            received[pl.ds(channel, 1), pl.ds(block * LANES, LANES)] = value[block : block + 1]
+        force = force + scalars[pl.ds(16 + channel, 1), :] * value
+
     force_out[...] = force
+    begin(copies[1:4])
     total, damp = damping[0], damping[1]
     smooth_out[...] = beside_old[...]
     smooth_out[pl.ds(0, 1), :] += beside_extra[0]
@@ -412,11 +437,11 @@
     prefixed[...] = inner + before
     rows, lanes = ends_row[...], ends_lane[...]
     count = rows.shape[0]
-    ends = run[:count]
+    marks = run[:count]
     for block in range(blocks):
         value = gather_lanes(wide(prefixed[pl.ds(block, 1), :], count), lanes)
-        ends = jnp.where(rows == block, value, ends)
-    own_source = ends - previous_one(ends)
+        marks = jnp.where(rows == block, value, marks)
+    own_source = marks - previous_one(marks)
 
     lane = lax.broadcasted_iota(I32, (1, LANES), 1)
     rim_rows, rim_counts = [], []
@@ -510,49 +535,28 @@
     for other in range(message.shape[0]):
         message[other] = to_right
     message[lax.rem(tile + tile_count - 1, tile_count)] = to_left
-
-
-def prepare_kernel(
-    fresh, ends_new, summed, far, near, cinverse, fresh_out, received, weights, sem, extended
-):
-    even = lax.rem(lax.axis_index("tile"), 2) == 0
-    cells = fresh_out.shape[1]
-    copies = [
-        pltpu.make_async_copy(
-            ends_new.at[:, pl.ds(side * LANES, LANES)],
-            fresh_out.at[:, pl.ds(side * (cells - LANES), LANES)],
-            sem.at[side],
-        )
-        for side in range(2)
-    ]
-    middle = pl.ds(LANES, cells - 2 * LANES)
-    copies.append(pltpu.make_async_copy(fresh.at[:, middle], fresh_out.at[:, middle], sem.at[2]))
+    copies[4].start()
     for copy in copies:
-        copy.start()
-    channels, blocks = summed.shape[:2]
-    for block in range(blocks):
-        for channel in range(channels):
-            received[pl.ds(channel, 1), pl.ds(block * LANES, LANES)] = summed[channel, pl.ds(block, 1), :]
-    bottoms, size = cinverse.shape
+        copy.wait()
+
+
+def inverse_windows(left, own, right, extended, weights):
+    bottoms, size = own.shape
     halves = size // LANES
-    part = pl.ds(INVERSE, 32 * halves)
-    left, right = sides(far[part, :].astype(F32), near[part, :].astype(F32), even)
     for half in range(halves):
         part = pl.ds(half * LANES, LANES)
         for at, block in ((0, left), (2, right)):
+            high, low = INVERSE + 16 * half, INVERSE + 16 * (halves + half)
             extended[pl.ds(at * bottoms, bottoms), part] = (
-                block[16 * half : 16 * half + 16]
-                + block[16 * (halves + half) : 16 * (halves + half) + 16]
+                block[pl.ds(high, bottoms), :] + block[pl.ds(low, bottoms), :]
             )
-        extended[pl.ds(bottoms, bottoms), part] = cinverse[:, part]
+        extended[pl.ds(bottoms, bottoms), part] = own[:, part]
     table = extended[...]
     lane = lax.broadcasted_iota(I32, (3 * bottoms, LANES), 1)
     for other in range(weights.shape[0]):
         shift = (size - (other - 1) * bottoms) % size
         turned = pltpu.roll(table, shift, axis=1) if shift else table
         weights[other] = jnp.where(lane < 3 * bottoms, turned[:, :LANES], 0.0)
-    for copy in copies:
-        copy.wait()
 
 
 def backward_kernel(
@@ -731,49 +735,39 @@
         name="stencil",
     )(here, scalars, current, edges, table, old, diagonal, owner, slot, block, in_hbm(remap_tiles[0, 0]))
 
-    summed, force, smooth, source, frame, ends_new, message = pl.pallas_call(
+    force, smooth, source, frame, weights, advanced, received, message = pl.pallas_call(
         forward_kernel,
         out_shape=[
-            struct((channels, blocks, LANES)),
             struct((blocks, LANES)),
             struct((blocks, LANES)),
             struct((FRAME, LANES)),
             struct((8 * FRAME, LANES)),
-            struct((fields.shape[1], 2 * LANES)),
+            struct((tile_count, 3 * bottoms, LANES)),
+            struct((fields.shape[1], cells)),
+            struct((channels, cells)),
             struct((tile_count, 8, LANES)),
         ],
-        in_specs=[VMEM] * 23,
-        out_specs=[VMEM] * 7,
+        in_specs=[VMEM] * 24,
+        out_specs=[VMEM] * 5 + [ANY] * 3,
         scratch_shapes=[
             pltpu.VMEM((4 * entries, LANES), F32),
             pltpu.VMEM((4 * entries, LANES), F32),
             pltpu.VMEM((blocks + 16, LANES), F32),
             pltpu.VMEM((blocks, LANES), F32),
             pltpu.VMEM((2, base, LANES), F32),
+            pltpu.VMEM((3 * bottoms, bottoms * tile_count), F32),
+            pltpu.VMEM((2, fields.shape[1], LANES), F32),
+            pltpu.VMEM((channels, cells), F32),
+            pltpu.VMEM((tile_count, 8, LANES), F32),
+            pltpu.SemaphoreType.DMA((5,)),
         ],
         compiler_params=PARAMS,
         name="forward",
     )(
         tiles, scalars, from_left2, far, from_right2, near, here, hot, member, current, edges, window, old,
-        damping, force_part, beside_old, ends_row, ends_lane, fresh, ctable, cedge, cdiag, cowner,
+        damping, force_part, beside_old, ends_row, ends_lane, fresh, ctable, cedge, cdiag, cowner, cinverse,
     )
     arrived = lax.all_to_all(message, "tile", split_axis=0, concat_axis=0, tiled=True)
-    advanced, received, weights = pl.pallas_call(
-        prepare_kernel,
-        out_shape=[
-            struct((fields.shape[1], cells)),
-            struct((channels, cells)),
-            struct((tile_count, 3 * bottoms, LANES)),
-        ],
-        in_specs=[VMEM] * 6,
-        out_specs=[ANY, VMEM, VMEM],
-        scratch_shapes=[
-            pltpu.SemaphoreType.DMA((3,)),
-            pltpu.VMEM((3 * bottoms, bottoms * tile_count), F32),
-        ],
-        compiler_params=PARAMS,
-        name="prepare",
-    )(fresh, ends_new, summed, far, near, cinverse)
     height = pl.pallas_call(
         functools.partial(backward_kernel, frows),
         out_shape=struct((blocks, LANES)),

time: 33.2 us -> 32.4 us (0.976)
  blocking collectives: 0 us -> 11.7 us
  waiting for transfers between devices: 7.43 us -> 1.38 us
  starting transfers between devices: 14.1 us -> 9.78 us
  Pallas kernels: 10.7 us -> 8.73 us
    all_to_all x0 -> x1, blocking collectives: none -> 11.7 us  [per_device(): lax.all_to_all(message, 'tile', split_axis=0, concat_axis=0, tiled=True)]
    all_to_all x1 -> x0, waiting for transfers between devices: 6.05 us -> none  [per_device(): lax.all_to_all(message, 'tile', split_axis=0, concat_axis=0, tiled=True)]
    all_to_all x1 -> x0, starting transfers between devices: 4.35 us -> none  [per_device(): lax.all_to_all(message, 'tile', split_axis=0, concat_axis=0, tiled=True)]
    pallas_call x2 -> x1, Pallas kernels: 4.93 us -> 2.97 us  [per_device(): pl.pallas_call(forward_kernel, out_shape=[struct((blocks, LANES)), struct...]
  transfers between devices with their start and end apart: 7 -> 6, of which waited for: 3 -> 2; matrix products, arithmetic and copies ran while one was open for 0% -> 0% of each run, Pallas kernels for 16% -> 12%
where the time goes in v6:
time: 32.4 us; the launch traced here: 32.3 us
  blocking collectives  11.7 us (36%)
  starting transfers between devices  9.78 us (30%)
  Pallas kernels  8.73 us (27%)
  waiting for transfers between devices  1.38 us (4%)
  between operations  0.7 us (2%)
    all_to_all x1, blocking collectives, per_device(): lax.all_to_all(message, 'tile', split_axis=0, concat_axis=0, tiled=True)  11.7 us
    ppermute x2, starting transfers between devices, shifted(): lax.ppermute(array, 'tile', [(i, (i + distance) % tile_count) for i in ra...  4.85 us
    ppermute x2, starting transfers between devices, swapped(): return lax.ppermute(array, 'tile', pairs + [(j, i) for i, j in pairs])  4.33 us
    pallas_call x1, Pallas kernels, per_device(): pl.pallas_call(forward_kernel, out_shape=[struct((blocks, LANES)), struct...  2.97 us
    pallas_call x1, Pallas kernels, per_device(): pl.pallas_call(stencil_kernel, out_shape=[struct((fields.shape[1], cells)...  2.67 us
    pallas_call x1, Pallas kernels, per_device(): pl.pallas_call(functools.partial(backward_kernel, frows), out_shape=struc...  1.55 us
    pallas_call x1, Pallas kernels, per_device(): pl.pallas_call(load_kernel, out_shape=[struct(x.shape, x.dtype) for x in...  1.28 us
    ppermute x2, waiting for transfers between devices, swapped(): return lax.ppermute(array, 'tile', pairs + [(j, i) for i, j in pairs])  1.24 us
  transfers between devices with their start and end apart: 6, of which 2 were waited for; matrix products, arithmetic and copies ran while one was open for 0% of the time, Pallas kernels for 12%

profile of v6, /device:TPU:0, one launch (start us, length us, event | category | flops | bytes accessed | tf_op | source)
XLA Modules:
  0.0 32.3 jit_solution(8000526463137198603)
XLA Ops:
  0.6 0.5 %collective-permute-start = (bf16[4,8192]{1,0:T(4,128)(2,1)}, bf16[4,8192]{1,0:T(4,128)(2,1)S(1)}, u32[]{:S(2)}, u32[]{:S(2)}) collective-permute-start(bf16[4,8192]{1,0:T(4,128)(2,1)} %bitcast.36), channel_id=1, source_target_pairs={{0,16},{16,0},{1,17},{17,1},{2,18},{18,2},{3,19},{19,3},{4,20},{20... | collective-permute-start | bytes 196616 | tf_op jit(solution)/shard_map/ppermute | solution.py:649
  1.2 0.1 collective-permute-start.1
  1.2 1.3 %load.1 = (f32[8,8192]{1,0:T(8,128)S(1)}, f32[64,128]{1,0:T(8,128)S(1)}, f32[3,64,128]{2,1,0:T(8,128)S(1)}, s32[3,64,128]{2,1,0:T(8,128)S(1)}, s32[64,128]{1,0:T...) custom-call(f32[8,8192]{1,0:T(8,128)} %bitcast.20, ...), custom_call_target="tpu_custom_call" | custom-call | tf_op jit(solution)/shard_map/load/pallas_call | solution.py:669
  2.5 0.0 collective-permute-done.1.sends
  2.5 0.0 collective-permute-done.surface
  2.5 0.3 pack.1
  2.8 3.0 %collective-permute-start.2 = (bf16[256,128]{1,0:T(8,128)(2,1)S(1)}, bf16[256,128]{1,0:T(8,128)(2,1)S(1)}, u32[]{:S(2)}, u32[]{:S(2)}) collective-permute-start(bf16[256,128]{1,0:T(8,128)(2,1)S(1)} %get-tuple-element.56), channel_id=1, source_target_pairs={{0,2},{1,3},{2,4},{3,5},{4,6},{5,7},{6,8},{7,9},{8,10},{9,11},{10,... | collective-permute-start | bytes 196616 | tf_op jit(solution)/shard_map/ppermute | solution.py:703
  5.8 4.1 %collective-permute-start.3 = (bf16[256,128]{1,0:T(8,128)(2,1)S(1)}, bf16[256,128]{1,0:T(8,128)(2,1)S(1)}, u32[]{:S(2)}, u32[]{:S(2)}) collective-permute-start(bf16[256,128]{1,0:T(8,128)(2,1)S(1)} %get-tuple-element.57), channel_id=1, source_target_pairs={{1,2},{3,4},{5,6},{7,8},{9,10},{11,12},{13,14},{15,0},{2,1},{4,3},... | collective-permute-start | bytes 196616 | tf_op jit(solution)/shard_map/ppermute | solution.py:710
  9.9 1.9 %collective-permute-start.4 = (bf16[256,128]{1,0:T(8,128)(2,1)S(1)}, bf16[256,128]{1,0:T(8,128)(2,1)S(1)}, u32[]{:S(2)}, u32[]{:S(2)}) collective-permute-start(bf16[256,128]{1,0:T(8,128)(2,1)S(1)} %get-tuple-element.58), channel_id=1, source_target_pairs={{0,14},{1,15},{2,0},{3,1},{4,2},{5,3},{6,4},{7,5},{8,6},{9,7},{10,... | collective-permute-start | bytes 196616 | tf_op jit(solution)/shard_map/ppermute | solution.py:703
  11.8 0.2 collective-permute-start.5
  12.0 2.7 %stencil.1 = (f32[8,8192]{1,0:T(8,128)S(1)}, f32[64,128]{1,0:T(8,128)S(1)}, f32[64,128]{1,0:T(8,128)S(1)}, s32[3,64,128]{2,1,0:T(8,128)S(1)}, s32[8,128]{1,0:T(8...) custom-call(bf16[128,128]{1,0:T(8,128)(2,1)S(1)} %get-tuple-element., ...), custom_call_target="tpu_custom_call" | custom-call | tf_op jit(solution)/shard_map/stencil/pallas_call | solution.py:717
  14.7 0.0 collective-permute-done.2.from_left2
  14.7 0.0 collective-permute-done.3.far
  14.7 0.1 collective-permute-done.4.from_right2
  14.8 1.2 %collective-permute-done.5.near = bf16[256,128]{1,0:T(8,128)(2,1)S(1)} collective-permute-done((bf16[256,128]{1,0:T(8,128)(2,1)S(1)}, bf16[256,128]{1,0:T(8,128)(2,1)S(1)}, u32[]{:S(2)}, u32[]{:S(2)}) %collective-permute-start.5) | collective-permute-done | bytes 65568 | tf_op jit(solution)/shard_map/ppermute | solution.py:710
  16.1 3.0 %forward.1 = (f32[64,128]{1,0:T(8,128)S(1)}, f32[64,128]{1,0:T(8,128)S(1)}, f32[32,128]{1,0:T(8,128)S(1)}, f32[256,128]{1,0:T(8,128)S(1)}, f32[16,48,128]{2,1,0:...) custom-call(bf16[160,128,128]{2,1,0:T(8,128)(2,1)S(1)} %get-tuple-element.55.tiles, ...), custom_call_target="tpu_custom_call" | custom-call | tf_op jit(solution)/shard_map/forward/pallas_call | solution.py:738
  19.0 11.7 %all_to_all.5.arrived = f32[16,8,128]{2,1,0:T(8,128)S(1)} all-to-all(f32[16,8,128]{2,1,0:T(8,128)S(1)} %get-tuple-element.71), channel_id=1, replica_groups=mesh['comp'=2,'tile'=16] {'tile'}, dimensions={0} | all-to-all | bytes 131072 | tf_op jit(solution)/shard_map/all_to_all | solution.py:770
  30.7 1.6 %backward.1 = f32[64,128]{1,0:T(8,128)} custom-call(f32[16,8,128]{2,1,0:T(8,128)S(1)} %all_to_all.5.arrived, f32[16,48,128]{2,1,0:T(8,128)S(1)} %get-tuple-element.72.weights, f32[32,128]{1,0:T(8,128)S(1)} %get-tuple-element.73.source, f32[256,128]{1,0:T(8,128)S(1)} %get-tuple-element.74.frame, f32[64,128]{1,0:T(8,128)S(1)} %get-tuple-element.75.force, ...), custom_call_target="tpu_custom_call" | custom-call | tf_op jit(solution)/shard_map/backward/pallas_call | solution.py:771
Async XLA Ops:
  0.6 1.9 %collective-permute-start = (bf16[4,8192]{1,0:T(4,128)(2,1)}, bf16[4,8192]{1,0:T(4,128)(2,1)S(1)}, u32[]{:S(2)}, u32[]{:S(2)}) collective-permute-start(bf16[4,8192]{1,0:T(4,128)(2,1)} %bitcast.36), channel_id=1, source_target_pairs={{0,16},{16,0},{1,17},{17,1},{2,18},{18,2},{3,19},{19,3},{4,20},{20... | collective-permute-start | bytes 196616 | tf_op jit(solution)/shard_map/ppermute | solution.py:649
  1.2 1.4 %collective-permute-start.1 = (s32[1,160]{1,0:T(1,128)}, s32[1,160]{1,0:T(1,128)S(1)}, u32[]{:S(2)}, u32[]{:S(2)}) collective-permute-start(s32[1,160]{1,0:T(1,128)} %bitcast.37), channel_id=1, source_target_pairs={{0,16},{16,0},{1,17},{17,1},{2,18},{18,2},{3,19},{19,3},{4,20},{20... | collective-permute-start | bytes 1928 | tf_op jit(solution)/shard_map/ppermute | solution.py:650
  2.8 11.9 %collective-permute-start.2 = (bf16[256,128]{1,0:T(8,128)(2,1)S(1)}, bf16[256,128]{1,0:T(8,128)(2,1)S(1)}, u32[]{:S(2)}, u32[]{:S(2)}) collective-permute-start(bf16[256,128]{1,0:T(8,128)(2,1)S(1)} %get-tuple-element.56), channel_id=1, source_target_pairs={{0,2},{1,3},{2,4},{3,5},{4,6},{5,7},{6,8},{7,9},{8,10},{9,11},{10,... | collective-permute-start | bytes 196616 | tf_op jit(solution)/shard_map/ppermute | solution.py:703
  5.8 8.9 %collective-permute-start.3 = (bf16[256,128]{1,0:T(8,128)(2,1)S(1)}, bf16[256,128]{1,0:T(8,128)(2,1)S(1)}, u32[]{:S(2)}, u32[]{:S(2)}) collective-permute-start(bf16[256,128]{1,0:T(8,128)(2,1)S(1)} %get-tuple-element.57), channel_id=1, source_target_pairs={{1,2},{3,4},{5,6},{7,8},{9,10},{11,12},{13,14},{15,0},{2,1},{4,3},... | collective-permute-start | bytes 196616 | tf_op jit(solution)/shard_map/ppermute | solution.py:710
  9.9 4.9 %collective-permute-start.4 = (bf16[256,128]{1,0:T(8,128)(2,1)S(1)}, bf16[256,128]{1,0:T(8,128)(2,1)S(1)}, u32[]{:S(2)}, u32[]{:S(2)}) collective-permute-start(bf16[256,128]{1,0:T(8,128)(2,1)S(1)} %get-tuple-element.58), channel_id=1, source_target_pairs={{0,14},{1,15},{2,0},{3,1},{4,2},{5,3},{6,4},{7,5},{8,6},{9,7},{10,... | collective-permute-start | bytes 196616 | tf_op jit(solution)/shard_map/ppermute | solution.py:703
  11.8 4.3 %collective-permute-start.5 = (bf16[256,128]{1,0:T(8,128)(2,1)S(1)}, bf16[256,128]{1,0:T(8,128)(2,1)S(1)}, u32[]{:S(2)}, u32[]{:S(2)}) collective-permute-start(bf16[256,128]{1,0:T(8,128)(2,1)S(1)} %get-tuple-element.59), channel_id=1, source_target_pairs={{0,1},{2,3},{4,5},{6,7},{8,9},{10,11},{12,13},{14,15},{1,0},{3,2},... | collective-permute-start | bytes 196616 | tf_op jit(solution)/shard_map/ppermute | solution.py:710

commit v7 on v6

--- a/solution.py
+++ b/solution.py
@@ -23,6 +23,8 @@
 
 FRAME, OWN = 32, 8
 
+MIDDLE = 32
+
 
 def sides(far, near, even):
     return jnp.where(even, far, near), jnp.where(even, near, far)
@@ -54,22 +56,15 @@
 
 
 def load_kernel(*refs):
-    count = (len(refs) - 2) // 2
-    sources, kept, scalars = refs[:count], refs[count : 2 * count - 3], refs[2 * count - 3]
-    spread, sems = refs[2 * count - 2 : 2 * count + 1], refs[2 * count + 1]
+    count = len(refs) // 2
     copies = [
-        pltpu.make_async_copy(source, target, sems.at[i])
-        for i, (source, target) in enumerate(zip(sources, kept + spread))
+        pltpu.make_async_copy(source, target, refs[-1].at[i])
+        for i, (source, target) in enumerate(zip(refs[:count], refs[count : 2 * count]))
     ]
     for copy in copies:
         copy.start()
     for copy in copies:
         copy.wait()
-    for i, value in enumerate(spread):
-        width = value.shape[1]
-        diagonal = lax.broadcasted_iota(I32, (8, width), 0) == lax.broadcasted_iota(I32, (8, width), 1)
-        column = jnp.sum(jnp.where(diagonal, wide(value[...]), 0.0), axis=1, keepdims=True)
-        scalars[pl.ds(8 * i, 8), :] = jnp.broadcast_to(column, (8, LANES))
 
 
 def pack_kernel(
@@ -150,10 +145,20 @@
 
 
 def stencil_kernel(
-    here, scalars, fields, edge, table, old, diagonal, owner, slots, entry_block, tiles,
-    fresh, force, beside_old, window, ends_row, ends_lane, hot, member, damping, tile_buffer, padded, sems,
+    here, fields, edge, table, old, owner, tiles, rate, level_weight, flux_weight, diagonal_in, slots_in, block_in,
+    fresh, force, beside_old, window, ends_row, ends_lane, hot, member, damping, scalars, tile_buffer,
+    padded, rate_row, level_row, flux_row, diagonal, slots, entry_block, small_sems, sems,
 ):
     del here
+    small = [
+        pltpu.make_async_copy(source, target, small_sems.at[i])
+        for i, (source, target) in enumerate(
+            (
+                (rate, rate_row), (level_weight, level_row), (flux_weight, flux_row),
+                (diagonal_in, diagonal), (slots_in, slots), (block_in, entry_block),
+            )
+        )
+    ]
     parts = sems.shape[0]
     step = tiles.shape[0] // parts
 
@@ -162,63 +167,18 @@
         return pltpu.make_async_copy(tiles.at[span], tile_buffer.at[span], sems.at[part])
 
     def begin(part, carry):
-        load(part).start()
+        if part is None:
+            for copy in small:
+                copy.start()
+        else:
+            load(part).start()
         return carry
 
+    once = 1 + lax.axis_index("tile") // lax.axis_size("tile")
+    lax.fori_loop(0, once, lambda _, carry: begin(None, carry), 0)
     lax.fori_loop(0, parts, begin, 0)
     blocks = old.shape[0]
     levels = fields.shape[0]
-    speed = scalars[pl.ds(0, 8), :]
-    share = scalars[pl.ds(8, 8), :]
-    starts = lax.broadcasted_iota(I32, (blocks, LANES), 0) * LANES
-    total = edge[0] + edge[1] + edge[2]
-    inverse = 1.0 / total
-    fine_total = diagonal[...] + total
-    damping[0] = fine_total
-    damping[1] = RELAXATION / fine_total
-    for link in range(3):
-        window[link] = table[link] - starts
-    blank = jnp.zeros((levels, LANES), F32)
-
-    def chunk(block):
-        if 0 <= block < blocks:
-            return fields[:, pl.ds(block * LANES, LANES)]
-        return blank
-
-    before, here, after = blank, chunk(0), chunk(1)
-    for block in range(blocks):
-        row = slice(block, block + 1)
-        beside = jnp.zeros((levels, LANES), F32)
-        for link in range(3):
-            place = wide(window[link, pl.ds(block, 1), :])
-            index = lax.bitwise_and(place, LANES - 1)
-            value = jnp.where(
-                place < LANES,
-                gather_lanes(before, index),
-                jnp.where(place < 2 * LANES, gather_lanes(here, index), gather_lanes(after, index)),
-            )
-            beside = beside + wide(edge[link, pl.ds(block, 1), :]) * value
-        result = here + speed * ((beside - wide(total[row]) * here) * wide(inverse[row]))
-        fresh[:, pl.ds(block * LANES, LANES)] = result
-        force[pl.ds(block, 1), :] = jnp.sum(result * share, axis=0, keepdims=True)
-        before, here, after = here, after, chunk(block + 2)
-
-    padded[pl.ds(0, 8), :] = jnp.zeros((8, LANES), F32)
-    padded[pl.ds(8 + blocks, 8), :] = jnp.zeros((8, LANES), F32)
-    padded[pl.ds(8, blocks), :] = old[...]
-    beside_old[...] = neighbour_sum(padded, edge, window, blocks)
-    names = jnp.where(
-        lax.broadcasted_iota(I32, (slots.shape[1], slots.shape[1]), 0) == slots[...], 1.0, 0.0
-    )
-    hot[...] = jnp.transpose(names).astype(BF16)
-    half = entry_block.shape[1] // 2
-    for part in range(2):
-        member[part] = jnp.where(
-            lax.broadcasted_iota(I32, (blocks, half), 0) == entry_block[:, part * half : (part + 1) * half],
-            1.0,
-            0.0,
-        ).astype(BF16)
-
     firsts = ends_row.shape[0] * LANES
     ident = lax.broadcasted_iota(I32, ends_row.shape, 0) * LANES + lax.broadcasted_iota(
         I32, ends_row.shape, 1
@@ -239,6 +199,64 @@
         lanes = jnp.where(value <= ident, lanes + bit, lanes)
     ends_row[...] = rows
     ends_lane[...] = lanes
+    for copy in small:
+        copy.wait()
+    for i, value in enumerate((rate_row, level_row, flux_row)):
+        width = value.shape[1]
+        same = lax.broadcasted_iota(I32, (8, width), 0) == lax.broadcasted_iota(I32, (8, width), 1)
+        column = jnp.sum(jnp.where(same, wide(value[...]), 0.0), axis=1, keepdims=True)
+        scalars[pl.ds(8 * i, 8), :] = jnp.broadcast_to(column, (8, LANES))
+    speed = scalars[pl.ds(0, 8), :]
+    share = scalars[pl.ds(8, 8), :]
+    starts = lax.broadcasted_iota(I32, (blocks, LANES), 0) * LANES
+    total = edge[0] + edge[1] + edge[2]
+    inverse = 1.0 / total
+    fine_total = diagonal[...] + total
+    damping[0] = fine_total
+    damping[1] = RELAXATION / fine_total
+    for link in range(3):
+        window[link] = table[link] - starts
+    blank = jnp.zeros((levels, LANES), F32)
+
+    def chunk(block):
+        if 0 <= block < blocks:
+            return fields[:, pl.ds(block * LANES, LANES)]
+        return blank
+
+    before, here, after = blank, chunk(0), chunk(1)
+    for block in range(blocks):
+        row = slice(block, block + 1)
+        beside = jnp.zeros((levels, LANES), F32)
+        for link in range(3):
+            place = wide(window[link, pl.ds(block, 1), :])
+            index = lax.bitwise_and(place, LANES - 1)
+            value = jnp.where(
+                place < LANES,
+                gather_lanes(before, index),
+                jnp.where(place < 2 * LANES, gather_lanes(here, index), gather_lanes(after, index)),
+            )
+            beside = beside + wide(edge[link, pl.ds(block, 1), :]) * value
+        result = here + speed * ((beside - wide(total[row]) * here) * wide(inverse[row]))
+        fresh[:, pl.ds(block * LANES, LANES)] = result
+        force[pl.ds(block, 1), :] = jnp.sum(result * share, axis=0, keepdims=True)
+        before, here, after = here, after, chunk(block + 2)
+
+    padded[pl.ds(0, 8), :] = jnp.zeros((8, LANES), F32)
+    padded[pl.ds(8 + blocks, 8), :] = jnp.zeros((8, LANES), F32)
+    padded[pl.ds(8, blocks), :] = old[...]
+    beside_old[...] = neighbour_sum(padded, edge, window, blocks)
+    names = jnp.where(
+        lax.broadcasted_iota(I32, (slots.shape[1], slots.shape[1]), 0) == slots[...], 1.0, 0.0
+    )
+    hot[...] = jnp.transpose(names).astype(BF16)
+    half = entry_block.shape[1] // 2
+    for part in range(2):
+        member[part] = jnp.where(
+            lax.broadcasted_iota(I32, (blocks, half), 0) == entry_block[:, part * half : (part + 1) * half],
+            1.0,
+            0.0,
+        ).astype(BF16)
+
     for part in range(parts):
         load(part).wait()
 
@@ -517,19 +535,31 @@
     pieces = split2(residual)
     left_side, right_side = [], []
     bins = lax.broadcasted_iota(I32, (3 * bottoms, LANES), 0)
-    rest = jnp.zeros((LANES - 3 * bottoms, LANES), BF16)
+    rest = [jnp.zeros((rows, LANES), BF16) for rows in (MIDDLE, LANES - MIDDLE - 3 * bottoms)]
     for row in range(OWN - 2, OWN + frows + 2):
         left_side.append(jnp.concatenate([p[row : row + 1] for p in pieces], axis=0))
         named = jnp.where(bins == codes[row : row + 1], 1.0, 0.0).astype(BF16)
-        right_side.append(jnp.concatenate([named, rest], axis=0))
+        right_side.append(jnp.concatenate([rest[0], named, rest[1]], axis=0))
     bottom = dot_nt(jnp.concatenate(left_side, axis=1), jnp.concatenate(right_side, axis=1))
     bottom = bottom[0:1] + bottom[1:2]
 
+    reach = LANES // 8
     to_left = jnp.concatenate(
-        [bottom, padded[pl.ds(8, 1), :], own_source[0:2], rim_source[0], jnp.zeros((3, LANES), F32)], axis=0
+        [
+            jnp.where(lane < reach, own_source[1:2], bottom),
+            padded[pl.ds(8, 1), :],
+            own_source[0:1],
+            rim_source[0],
+        ],
+        axis=0,
     )
     to_right = jnp.concatenate(
-        [bottom, padded[pl.ds(7 + blocks, 1), :], own_source[frows - 2 : frows], rim_source[1], jnp.zeros((3, LANES), F32)],
+        [
+            jnp.where(lane >= LANES - reach, own_source[frows - 2 : frows - 1], bottom),
+            padded[pl.ds(7 + blocks, 1), :],
+            own_source[frows - 1 : frows],
+            rim_source[1],
+        ],
         axis=0,
     )
     for other in range(message.shape[0]):
@@ -554,9 +584,11 @@
     table = extended[...]
     lane = lax.broadcasted_iota(I32, (3 * bottoms, LANES), 1)
     for other in range(weights.shape[0]):
-        shift = (size - (other - 1) * bottoms) % size
+        shift = (size + MIDDLE - (other - 1) * bottoms) % size
         turned = pltpu.roll(table, shift, axis=1) if shift else table
-        weights[other] = jnp.where(lane < 3 * bottoms, turned[:, :LANES], 0.0)
+        weights[other] = jnp.where(
+            lane >= MIDDLE, jnp.where(lane < MIDDLE + 3 * bottoms, turned[:, :LANES], 0.0), 0.0
+        )
 
 
 def backward_kernel(
@@ -578,10 +610,14 @@
 
     frows = frame_rows
     frame_source[...] = source[...]
-    frame_source[pl.ds(OWN - 2, 2), :] += left[2:4]
-    frame_source[pl.ds(OWN, 1), :] += left[4:5]
-    frame_source[pl.ds(OWN + frows - 1, 1), :] += right[4:5]
-    frame_source[pl.ds(OWN + frows, 2), :] += right[2:4]
+    lane = lax.broadcasted_iota(I32, (1, LANES), 1)
+    reach = LANES // 8
+    frame_source[pl.ds(OWN - 2, 1), :] += jnp.where(lane >= LANES - reach, left[0:1], 0.0)
+    frame_source[pl.ds(OWN - 1, 1), :] += left[2:3]
+    frame_source[pl.ds(OWN, 1), :] += left[3:4]
+    frame_source[pl.ds(OWN + frows - 1, 1), :] += right[3:4]
+    frame_source[pl.ds(OWN + frows, 1), :] += right[2:3]
+    frame_source[pl.ds(OWN + frows + 1, 1), :] += jnp.where(lane < reach, right[0:1], 0.0)
     total_source = frame_source[...]
     total = frame[pl.ds(6 * FRAME, FRAME), :]
     codes = frame[pl.ds(7 * FRAME, FRAME), :].astype(I32)
@@ -654,32 +690,21 @@
         edge_weight[0].reshape(3, blocks, LANES),
         fine_table[0].reshape(3, blocks, LANES),
         fine_owner.reshape(blocks, LANES),
-        fine_diagonal.reshape(blocks, LANES),
         coarse_table[0].reshape(3, frows, LANES),
         coarse_edge[0].reshape(3, frows, LANES),
         coarse_diagonal.reshape(frows, LANES),
         coarse_owner.reshape(frows, LANES),
         coarse_inverse[0],
-        entry_slot[0],
-        entry_block[0],
-        level_rate,
-        level_weight,
-        flux_weight,
-    )
-    loaded = pl.pallas_call(
+    )
+    current, old, edges, table, owner, ctable, cedge, cdiag, cowner, cinverse = pl.pallas_call(
         load_kernel,
-        out_shape=[struct(x.shape, x.dtype) for x in raw[:-3]] + [struct((24, LANES))],
+        out_shape=[struct(x.shape, x.dtype) for x in raw],
         in_specs=[ANY] * len(raw),
-        out_specs=[VMEM] * (len(raw) - 2),
-        scratch_shapes=[pltpu.VMEM(x.shape, x.dtype) for x in raw[-3:]]
-        + [pltpu.SemaphoreType.DMA((len(raw),))],
+        out_specs=[VMEM] * len(raw),
+        scratch_shapes=[pltpu.SemaphoreType.DMA((len(raw),))],
         compiler_params=PARAMS,
         name="load",
     )(*[in_hbm(x) for x in raw])
-    (
-        current, old, edges, table, owner, diagonal, ctable, cedge, cdiag, cowner, cinverse,
-        slot, block, scalars,
-    ) = loaded
 
     pick = struct((4 * each, LANES), BF16)
     both = struct((base + 4 * each, LANES), BF16)
@@ -714,7 +739,10 @@
     from_right2 = shifted(to_left2, -2)
     near = swapped(near, 0)
 
-    fresh, force_part, beside_old, window, ends_row, ends_lane, hot, member, damping, tiles = pl.pallas_call(
+    late = (
+        level_rate, level_weight, flux_weight, fine_diagonal.reshape(blocks, LANES), entry_slot[0], entry_block[0]
+    )
+    fresh, force_part, beside_old, window, ends_row, ends_lane, hot, member, damping, scalars, tiles = pl.pallas_call(
         stencil_kernel,
         out_shape=[
             struct((fields.shape[1], cells)),
@@ -726,14 +754,17 @@
             struct((entries, slots), BF16),
             struct((2, blocks, entries // 2), BF16),
             struct((2, blocks, LANES)),
+            struct((24, LANES)),
             pltpu.VMEM(remap_tiles.shape[2:], BF16),
         ],
-        in_specs=[VMEM] * 10 + [ANY],
-        out_specs=[VMEM] * 10,
-        scratch_shapes=[pltpu.VMEM((blocks + 16, LANES), F32), pltpu.SemaphoreType.DMA((math.gcd(entries, 8),))],
+        in_specs=[VMEM] * 6 + [ANY] * 7,
+        out_specs=[VMEM] * 11,
+        scratch_shapes=[pltpu.VMEM((blocks + 16, LANES), F32)]
+        + [pltpu.VMEM(x.shape, x.dtype) for x in late]
+        + [pltpu.SemaphoreType.DMA((len(late),)), pltpu.SemaphoreType.DMA((math.gcd(entries, 8),))],
         compiler_params=PARAMS,
         name="stencil",
-    )(here, scalars, current, edges, table, old, diagonal, owner, slot, block, in_hbm(remap_tiles[0, 0]))
+    )(here, current, edges, table, old, owner, *[in_hbm(x) for x in (remap_tiles[0, 0],) + late])
 
     force, smooth, source, frame, weights, advanced, received, message = pl.pallas_call(
         forward_kernel,
@@ -745,7 +776,7 @@
             struct((tile_count, 3 * bottoms, LANES)),
             struct((fields.shape[1], cells)),
             struct((channels, cells)),
-            struct((tile_count, 8, LANES)),
+            struct((tile_count, 4, LANES)),
         ],
         in_specs=[VMEM] * 24,
         out_specs=[VMEM] * 5 + [ANY] * 3,
@@ -758,7 +789,7 @@
             pltpu.VMEM((3 * bottoms, bottoms * tile_count), F32),
             pltpu.VMEM((2, fields.shape[1], LANES), F32),
             pltpu.VMEM((channels, cells), F32),
-            pltpu.VMEM((tile_count, 8, LANES), F32),
+            pltpu.VMEM((tile_count, 4, LANES), F32),
             pltpu.SemaphoreType.DMA((5,)),
         ],
         compiler_params=PARAMS,

time: 32.4 us -> 32.4 us (level)
  no operation moved by 1% of the time
where the time goes in v7:
time: 32.4 us; the launch traced here: 32.1 us
  blocking collectives  11.7 us (36%)
  starting transfers between devices  9.67 us (30%)
  Pallas kernels  8.79 us (27%)
  waiting for transfers between devices  1.34 us (4%)
  between operations  0.68 us (2%)
    all_to_all x1, blocking collectives, per_device(): lax.all_to_all(message, 'tile', split_axis=0, concat_axis=0, tiled=True)  11.7 us
    ppermute x2, starting transfers between devices, shifted(): lax.ppermute(array, 'tile', [(i, (i + distance) % tile_count) for i in ra...  4.75 us
    ppermute x2, starting transfers between devices, swapped(): return lax.ppermute(array, 'tile', pairs + [(j, i) for i, j in pairs])  4.33 us
    pallas_call x1, Pallas kernels, per_device(): pl.pallas_call(forward_kernel, out_shape=[struct((blocks, LANES)), struct...  3 us
    pallas_call x1, Pallas kernels, per_device(): pl.pallas_call(stencil_kernel, out_shape=[struct((fields.shape[1], cells)...  2.84 us
    pallas_call x1, Pallas kernels, per_device(): pl.pallas_call(functools.partial(backward_kernel, frows), out_shape=struc...  1.55 us
    ppermute x2, waiting for transfers between devices, swapped(): return lax.ppermute(array, 'tile', pairs + [(j, i) for i, j in pairs])  1.16 us
    pallas_call x1, Pallas kernels, per_device(): pl.pallas_call(load_kernel, out_shape=[struct(x.shape, x.dtype) for x in...  1.13 us
  transfers between devices with their start and end apart: 6, of which 2 were waited for; matrix products, arithmetic and copies ran while one was open for 0% of the time, Pallas kernels for 12%

profile of v7, /device:TPU:0, one launch (start us, length us, event | category | flops | bytes accessed | tf_op | source)
XLA Modules:
  0.0 32.1 jit_solution(13872584571261962294)
XLA Ops:
  0.6 0.5 %collective-permute-start = (bf16[4,8192]{1,0:T(4,128)(2,1)}, bf16[4,8192]{1,0:T(4,128)(2,1)S(1)}, u32[]{:S(2)}, u32[]{:S(2)}) collective-permute-start(bf16[4,8192]{1,0:T(4,128)(2,1)} %bitcast.36), channel_id=1, source_target_pairs={{0,16},{16,0},{1,17},{17,1},{2,18},{18,2},{3,19},{19,3},{4,20},{20... | collective-permute-start | bytes 196616 | tf_op jit(solution)/shard_map/ppermute | solution.py:685
  1.2 0.1 collective-permute-start.1
  1.2 1.1 %load.1 = (f32[8,8192]{1,0:T(8,128)S(1)}, f32[64,128]{1,0:T(8,128)S(1)}, f32[3,64,128]{2,1,0:T(8,128)S(1)}, s32[3,64,128]{2,1,0:T(8,128)S(1)}, s32[64,128]{1,0:T...) custom-call(f32[8,8192]{1,0:T(8,128)} %bitcast.20, ...), custom_call_target="tpu_custom_call" | custom-call | tf_op jit(solution)/shard_map/load/pallas_call | solution.py:699
  2.4 0.1 collective-permute-done.1.sends
  2.5 0.0 collective-permute-done.surface
  2.5 0.3 pack.1
  2.8 2.9 %collective-permute-start.2 = (bf16[256,128]{1,0:T(8,128)(2,1)S(1)}, bf16[256,128]{1,0:T(8,128)(2,1)S(1)}, u32[]{:S(2)}, u32[]{:S(2)}) collective-permute-start(bf16[256,128]{1,0:T(8,128)(2,1)S(1)} %get-tuple-element.50), channel_id=1, source_target_pairs={{0,2},{1,3},{2,4},{3,5},{4,6},{5,7},{6,8},{7,9},{8,10},{9,11},{10,... | collective-permute-start | bytes 196616 | tf_op jit(solution)/shard_map/ppermute | solution.py:728
  5.7 4.1 %collective-permute-start.3 = (bf16[256,128]{1,0:T(8,128)(2,1)S(1)}, bf16[256,128]{1,0:T(8,128)(2,1)S(1)}, u32[]{:S(2)}, u32[]{:S(2)}) collective-permute-start(bf16[256,128]{1,0:T(8,128)(2,1)S(1)} %get-tuple-element.51), channel_id=1, source_target_pairs={{1,2},{3,4},{5,6},{7,8},{9,10},{11,12},{13,14},{15,0},{2,1},{4,3},... | collective-permute-start | bytes 196616 | tf_op jit(solution)/shard_map/ppermute | solution.py:735
  9.8 1.9 %collective-permute-start.4 = (bf16[256,128]{1,0:T(8,128)(2,1)S(1)}, bf16[256,128]{1,0:T(8,128)(2,1)S(1)}, u32[]{:S(2)}, u32[]{:S(2)}) collective-permute-start(bf16[256,128]{1,0:T(8,128)(2,1)S(1)} %get-tuple-element.52), channel_id=1, source_target_pairs={{0,14},{1,15},{2,0},{3,1},{4,2},{5,3},{6,4},{7,5},{8,6},{9,7},{10,... | collective-permute-start | bytes 196616 | tf_op jit(solution)/shard_map/ppermute | solution.py:728
  11.6 0.2 collective-permute-start.5
  11.8 2.8 %stencil.1 = (f32[8,8192]{1,0:T(8,128)S(1)}, f32[64,128]{1,0:T(8,128)S(1)}, f32[64,128]{1,0:T(8,128)S(1)}, s32[3,64,128]{2,1,0:T(8,128)S(1)}, s32[8,128]{1,0:T(8...) custom-call(bf16[128,128]{1,0:T(8,128)(2,1)S(1)} %get-tuple-element., ...), custom_call_target="tpu_custom_call" | custom-call | tf_op jit(solution)/shard_map/stencil/pallas_call | solution.py:745
  14.7 0.0 collective-permute-done.2.from_left2
  14.7 0.0 collective-permute-done.3.far
  14.7 0.0 collective-permute-done.4.from_right2
  14.8 1.2 %collective-permute-done.5.near = bf16[256,128]{1,0:T(8,128)(2,1)S(1)} collective-permute-done((bf16[256,128]{1,0:T(8,128)(2,1)S(1)}, bf16[256,128]{1,0:T(8,128)(2,1)S(1)}, u32[]{:S(2)}, u32[]{:S(2)}) %collective-permute-start.5) | collective-permute-done | bytes 65568 | tf_op jit(solution)/shard_map/ppermute | solution.py:735
  15.9 3.0 %forward.1 = (f32[64,128]{1,0:T(8,128)S(1)}, f32[64,128]{1,0:T(8,128)S(1)}, f32[32,128]{1,0:T(8,128)S(1)}, f32[256,128]{1,0:T(8,128)S(1)}, f32[16,48,128]{2,1,0:...) custom-call(bf16[160,128,128]{2,1,0:T(8,128)(2,1)S(1)} %get-tuple-element.48.tiles, ...), custom_call_target="tpu_custom_call" | custom-call | tf_op jit(solution)/shard_map/forward/pallas_call | solution.py:769
  18.9 11.7 %all_to_all.5.arrived = f32[16,4,128]{2,1,0:T(4,128)S(1)} all-to-all(f32[16,4,128]{2,1,0:T(4,128)S(1)} %get-tuple-element.65), channel_id=1, replica_groups=mesh['comp'=2,'tile'=16] {'tile'}, dimensions={0} | all-to-all | bytes 65536 | tf_op jit(solution)/shard_map/all_to_all | solution.py:801
  30.6 1.6 %backward.1 = f32[64,128]{1,0:T(8,128)} custom-call(f32[16,4,128]{2,1,0:T(4,128)S(1)} %all_to_all.5.arrived, f32[16,48,128]{2,1,0:T(8,128)S(1)} %get-tuple-element.66.weights, f32[32,128]{1,0:T(8,128)S(1)} %get-tuple-element.67.source, f32[256,128]{1,0:T(8,128)S(1)} %get-tuple-element.68.frame, f32[64,128]{1,0:T(8,128)S(1)} %get-tuple-element.69.force, ...), custom_call_target="tpu_custom_call" | custom-call | tf_op jit(solution)/shard_map/backward/pallas_call | solution.py:802
Async XLA Ops:
  0.6 1.9 %collective-permute-start = (bf16[4,8192]{1,0:T(4,128)(2,1)}, bf16[4,8192]{1,0:T(4,128)(2,1)S(1)}, u32[]{:S(2)}, u32[]{:S(2)}) collective-permute-start(bf16[4,8192]{1,0:T(4,128)(2,1)} %bitcast.36), channel_id=1, source_target_pairs={{0,16},{16,0},{1,17},{17,1},{2,18},{18,2},{3,19},{19,3},{4,20},{20... | collective-permute-start | bytes 196616 | tf_op jit(solution)/shard_map/ppermute | solution.py:685
  1.2 1.4 %collective-permute-start.1 = (s32[1,160]{1,0:T(1,128)}, s32[1,160]{1,0:T(1,128)S(1)}, u32[]{:S(2)}, u32[]{:S(2)}) collective-permute-start(s32[1,160]{1,0:T(1,128)} %bitcast.37), channel_id=1, source_target_pairs={{0,16},{16,0},{1,17},{17,1},{2,18},{18,2},{3,19},{19,3},{4,20},{20... | collective-permute-start | bytes 1928 | tf_op jit(solution)/shard_map/ppermute | solution.py:686
  2.8 11.9 %collective-permute-start.2 = (bf16[256,128]{1,0:T(8,128)(2,1)S(1)}, bf16[256,128]{1,0:T(8,128)(2,1)S(1)}, u32[]{:S(2)}, u32[]{:S(2)}) collective-permute-start(bf16[256,128]{1,0:T(8,128)(2,1)S(1)} %get-tuple-element.50), channel_id=1, source_target_pairs={{0,2},{1,3},{2,4},{3,5},{4,6},{5,7},{6,8},{7,9},{8,10},{9,11},{10,... | collective-permute-start | bytes 196616 | tf_op jit(solution)/shard_map/ppermute | solution.py:728
  5.7 9.0 %collective-permute-start.3 = (bf16[256,128]{1,0:T(8,128)(2,1)S(1)}, bf16[256,128]{1,0:T(8,128)(2,1)S(1)}, u32[]{:S(2)}, u32[]{:S(2)}) collective-permute-start(bf16[256,128]{1,0:T(8,128)(2,1)S(1)} %get-tuple-element.51), channel_id=1, source_target_pairs={{1,2},{3,4},{5,6},{7,8},{9,10},{11,12},{13,14},{15,0},{2,1},{4,3},... | collective-permute-start | bytes 196616 | tf_op jit(solution)/shard_map/ppermute | solution.py:735
  9.8 5.0 %collective-permute-start.4 = (bf16[256,128]{1,0:T(8,128)(2,1)S(1)}, bf16[256,128]{1,0:T(8,128)(2,1)S(1)}, u32[]{:S(2)}, u32[]{:S(2)}) collective-permute-start(bf16[256,128]{1,0:T(8,128)(2,1)S(1)} %get-tuple-element.52), channel_id=1, source_target_pairs={{0,14},{1,15},{2,0},{3,1},{4,2},{5,3},{6,4},{7,5},{8,6},{9,7},{10,... | collective-permute-start | bytes 196616 | tf_op jit(solution)/shard_map/ppermute | solution.py:728
  11.6 4.3 %collective-permute-start.5 = (bf16[256,128]{1,0:T(8,128)(2,1)S(1)}, bf16[256,128]{1,0:T(8,128)(2,1)S(1)}, u32[]{:S(2)}, u32[]{:S(2)}) collective-permute-start(bf16[256,128]{1,0:T(8,128)(2,1)S(1)} %get-tuple-element.53), channel_id=1, source_target_pairs={{0,1},{2,3},{4,5},{6,7},{8,9},{10,11},{12,13},{14,15},{1,0},{3,2},... | collective-permute-start | bytes 196616 | tf_op jit(solution)/shard_map/ppermute | solution.py:735

commit v8 on v7

--- a/solution.py
+++ b/solution.py
@@ -26,8 +26,45 @@
 MIDDLE = 32
 
 
-def sides(far, near, even):
-    return jnp.where(even, far, near), jnp.where(even, near, far)
+PLANS = {
+    16: (
+        (1, 1, 1, 1, 1, 2, 2, -1, 2, 2, -1, 2, 2, 2, -2, 1),
+        (-1, 2, 2, -2, -2, 1, -1, 2, -1, 1, -2, 1, 1, -2, 2, -1),
+        (-2, -2, -2, -1, -1, -1, 1, -2, -2, -1, 1, -2, -2, -1, -1, 2),
+        (2, -1, -1, 2, 2, -2, -2, 1, 1, -2, 2, -1, -1, 1, 1, -2),
+    ),
+}
+DISTANCES = (-1, 1, -2, 2)
+
+
+def exchange_plan(count):
+    if count in PLANS:
+        return PLANS[count]
+    near = [1 if i % 2 == 0 else -1 for i in range(count)]
+    return ([2] * count, [-d for d in near], [-2] * count, near)
+
+
+def lookup(tile, values):
+    result = jnp.int32(values[0])
+    for i, value in enumerate(values):
+        result = jnp.where(tile == i, jnp.int32(value), result)
+    return result
+
+
+def arrived_by(tile, plan, distance):
+    count = len(plan[0])
+    found = []
+    for i in range(count):
+        sender = (i - distance) % count
+        found.append([op[sender] for op in plan].index(distance))
+    return lookup(tile, found)
+
+
+def chosen_rows(which, refs, rows):
+    value = refs[0][rows, :]
+    for i, ref in enumerate(refs[1:]):
+        value = jnp.where(which == i + 1, ref[rows, :], value)
+    return value
 
 
 def gather_lanes(table, index):
@@ -68,10 +105,10 @@
 
 
 def pack_kernel(
-    surface, sends, fields, old, edge, table, owner, ctable, cedge, cdiag, cowner, cinverse,
-    to_right2, far, to_left2, near, here, chunks, left_rows, right_rows,
+    plan, surface, sends, fields, old, edge, table, owner, ctable, cedge, cdiag, cowner, cinverse,
+    out0, out1, out2, out3, here, chunks, left_rows, right_rows, packed,
 ):
-    even = lax.rem(lax.axis_index("tile"), 2) == 0
+    tile = lax.axis_index("tile")
     cells = fields.shape[1]
     blocks = cells // LANES
     frows = ctable.shape[1]
@@ -135,13 +172,12 @@
         jnp.concatenate([p[j * count : (j + 1) * count] for p in picks], axis=0) for j in range(5)
     ]
     here[...] = chosen[2]
-    for out, j in ((to_right2, 0), (to_left2, 4)):
-        out[pl.ds(0, base), :] = jnp.zeros((base, LANES), BF16)
-        out[pl.ds(base, 4 * count), :] = chosen[j]
-    right = jnp.concatenate([right_rows[...].astype(BF16), chosen[1]], axis=0)
-    left = jnp.concatenate([left_rows[...].astype(BF16), chosen[3]], axis=0)
-    far[...] = jnp.where(even, left, right)
-    near[...] = jnp.where(even, right, left)
+    rims = {-1: left_rows[...].astype(BF16), 1: right_rows[...].astype(BF16)}
+    for at, distance in enumerate(DISTANCES):
+        packed[at, pl.ds(0, base), :] = rims.get(distance, jnp.zeros((base, LANES), BF16))
+        packed[at, pl.ds(base, 4 * count), :] = chosen[2 - distance]
+    for out, op in zip((out0, out1, out2, out3), plan):
+        out[...] = packed[lookup(tile, [DISTANCES.index(distance) for distance in op])]
 
 
 def stencil_kernel(
@@ -337,9 +373,9 @@
 
 
 def forward_kernel(
-    tiles, scalars, from_left2, far, from_right2, near, here, hot, member, fields, edges, window, old,
+    plan, tiles, scalars, message0, message1, message2, message3, here, hot, member, fields, edges, window, old,
     damping, force_part, beside_old, ends_row, ends_lane, fresh, ctable, cedge, cdiag, cowner, cinverse,
-    force_out, smooth_out, source_out, frame, weights_out, fresh_out, received_out, message_out,
+    force_out, smooth_out, source_out, frame, weights_out, rim_owner, fresh_out, received_out, message_out,
     picked, products, padded, prefixed, arrivals, extended, ends, received, message, sems,
 ):
     cells = fresh.shape[1]
@@ -368,19 +404,23 @@
     entries = tiles.shape[0]
     blocks = old.shape[0]
 
-    even = lax.rem(tile, 2) == 0
-    base = far.shape[0] - here.shape[0]
+    messages = (message0, message1, message2, message3)
+    base = message0.shape[0] - here.shape[0]
     each = here.shape[0] // 4
-    from_left, from_right = sides(far[...], near[...], even)
-    sources = (from_left2[base:, :], from_left[base:], here[...], from_right[base:], from_right2[base:, :])
+    found = {distance: arrived_by(tile, plan, distance) for distance in DISTANCES}
+    sources = [
+        chosen_rows(found[distance], messages, pl.ds(base, 4 * each)) if distance else here[...]
+        for distance in (2, 1, 0, -1, -2)
+    ]
     for channel in range(4):
         source = jnp.concatenate(
             [rows[channel * each : (channel + 1) * each] for rows in sources], axis=0
         )
         picked[pl.ds(channel, entries, stride=4), :] = jnp.dot(hot[...], source, preferred_element_type=F32)
 
-    arrivals[0] = from_left[:base].astype(F32)
-    arrivals[1] = from_right[:base].astype(F32)
+    for side, distance in enumerate((1, -1)):
+        arrivals[side] = chosen_rows(found[distance], messages, pl.ds(0, base)).astype(F32)
+        rim_owner[side] = wide(arrivals[side, pl.ds(OWNER, 1), :]).astype(I32)
 
     upper = lax.rem(lax.broadcasted_iota(I32, (16, LANES), 0), 8) < 4
     for group in range(entries // 4):
@@ -592,7 +632,7 @@
 
 
 def backward_kernel(
-    frame_rows, arrived, weights, source, frame, force, smooth, edges, window, damping, owner, far, near,
+    frame_rows, arrived, weights, source, frame, force, smooth, edges, window, damping, owner, rim_owner,
     height, frame_source, padded, third_rows,
 ):
     tile = lax.axis_index("tile")
@@ -636,14 +676,8 @@
         )
     corrected = smooth[...] + corrected
     padded[pl.ds(8, blocks), :] = corrected
-    part = pl.ds(16, 16)
-    even = lax.rem(tile, 2) == 0
-    left_owner, right_owner = [
-        rows[OWNER - 16 : OWNER - 15].astype(I32)
-        for rows in sides(far[part, :].astype(F32), near[part, :].astype(F32), even)
-    ]
-    left_rim = left[1:2] + gather_lanes(wide(third_rows[pl.ds(OWN - 1, 1), :]), wide(left_owner))[0:1]
-    right_rim = right[1:2] + gather_lanes(wide(third_rows[pl.ds(OWN + frows, 1), :]), wide(right_owner))[0:1]
+    left_rim = left[1:2] + gather_lanes(wide(third_rows[pl.ds(OWN - 1, 1), :]), rim_owner[0])[0:1]
+    right_rim = right[1:2] + gather_lanes(wide(third_rows[pl.ds(OWN + frows, 1), :]), rim_owner[1])[0:1]
     padded[pl.ds(7, 1), :] = left_rim
     padded[pl.ds(8 + blocks, 1), :] = right_rim
     beside = neighbour_sum(padded, edges, window, blocks)
@@ -708,8 +742,9 @@
 
     pick = struct((4 * each, LANES), BF16)
     both = struct((base + 4 * each, LANES), BF16)
-    to_right2, far, to_left2, near, here = pl.pallas_call(
-        pack_kernel,
+    plan = exchange_plan(tile_count)
+    *messages, here = pl.pallas_call(
+        functools.partial(pack_kernel, plan),
         out_shape=[both, both, both, both, pick],
         in_specs=[VMEM] * 12,
         out_specs=[VMEM] * 5,
@@ -717,6 +752,7 @@
             pltpu.VMEM((channels * blocks, LANES), F32),
             pltpu.VMEM((base, LANES), F32),
             pltpu.VMEM((base, LANES), F32),
+            pltpu.VMEM((4, base + 4 * each, LANES), BF16),
         ],
         compiler_params=PARAMS,
         name="pack",
@@ -724,20 +760,10 @@
         surface, sends, current, old, edges, table, owner, ctable, cedge, cdiag, cowner, cinverse,
     )
 
-    def shifted(array, distance):
-        return lax.ppermute(
-            array, "tile", [(i, (i + distance) % tile_count) for i in range(tile_count)]
-        )
-
-    def swapped(array, start):
-        lower = [i for i in range(tile_count) if i % 2 == start]
-        pairs = [(i, (i + 1) % tile_count) for i in lower]
-        return lax.ppermute(array, "tile", pairs + [(j, i) for i, j in pairs])
-
-    from_left2 = shifted(to_right2, 2)
-    far = swapped(far, 1)
-    from_right2 = shifted(to_left2, -2)
-    near = swapped(near, 0)
+    messages = [
+        lax.ppermute(message, "tile", [(i, (i + op[i]) % tile_count) for i in range(tile_count)])
+        for message, op in zip(messages, plan)
+    ]
 
     late = (
         level_rate, level_weight, flux_weight, fine_diagonal.reshape(blocks, LANES), entry_slot[0], entry_block[0]
@@ -766,20 +792,21 @@
         name="stencil",
     )(here, current, edges, table, old, owner, *[in_hbm(x) for x in (remap_tiles[0, 0],) + late])
 
-    force, smooth, source, frame, weights, advanced, received, message = pl.pallas_call(
-        forward_kernel,
+    force, smooth, source, frame, weights, rim_owner, advanced, received, message = pl.pallas_call(
+        functools.partial(forward_kernel, plan),
         out_shape=[
             struct((blocks, LANES)),
             struct((blocks, LANES)),
             struct((FRAME, LANES)),
             struct((8 * FRAME, LANES)),
             struct((tile_count, 3 * bottoms, LANES)),
+            struct((2, 8, LANES), I32),
             struct((fields.shape[1], cells)),
             struct((channels, cells)),
             struct((tile_count, 4, LANES)),
         ],
         in_specs=[VMEM] * 24,
-        out_specs=[VMEM] * 5 + [ANY] * 3,
+        out_specs=[VMEM] * 6 + [ANY] * 3,
         scratch_shapes=[
             pltpu.VMEM((4 * entries, LANES), F32),
             pltpu.VMEM((4 * entries, LANES), F32),
@@ -795,14 +822,14 @@
         compiler_params=PARAMS,
         name="forward",
     )(
-        tiles, scalars, from_left2, far, from_right2, near, here, hot, member, current, edges, window, old,
+        tiles, scalars, *messages, here, hot, member, current, edges, window, old,
         damping, force_part, beside_old, ends_row, ends_lane, fresh, ctable, cedge, cdiag, cowner, cinverse,
     )
     arrived = lax.all_to_all(message, "tile", split_axis=0, concat_axis=0, tiled=True)
     height = pl.pallas_call(
         functools.partial(backward_kernel, frows),
         out_shape=struct((blocks, LANES)),
-        in_specs=[VMEM] * 12,
+        in_specs=[VMEM] * 11,
         out_specs=VMEM,
         scratch_shapes=[
             pltpu.VMEM((FRAME, LANES), F32),
@@ -811,7 +838,7 @@
         ],
         compiler_params=PARAMS,
         name="backward",
-    )(arrived, weights, source, frame, force, smooth, edges, window, damping, owner, far, near)
+    )(arrived, weights, source, frame, force, smooth, edges, window, damping, owner, rim_owner)
     return advanced[None], received[None], height.reshape(1, cells)
 
 

time: 32.4 us -> 32.1 us (level)
  waiting for transfers between devices: 1.34 us -> 0.54 us
  blocking collectives: 11.7 us -> 12.3 us
    ppermute x4, waiting for transfers between devices: 1.21 us -> 0.41 us  [per_device(): lax.ppermute(message, 'tile', [(i, (i + op[i]) % tile_count) for i in ran...]
    all_to_all x1, blocking collectives: 11.7 us -> 12.3 us  [per_device(): lax.all_to_all(message, 'tile', split_axis=0, concat_axis=0, tiled=True)]
where the time goes in v8:
time: 32.1 us; the launch traced here: 31.9 us
  blocking collectives  12.3 us (38%)
  starting transfers between devices  9.54 us (30%)
  Pallas kernels  8.82 us (27%)
  between operations  0.69 us (2%)
  waiting for transfers between devices  0.54 us (2%)
    all_to_all x1, blocking collectives, per_device(): lax.all_to_all(message, 'tile', split_axis=0, concat_axis=0, tiled=True)  12.3 us
    ppermute x4, starting transfers between devices, per_device(): lax.ppermute(message, 'tile', [(i, (i + op[i]) % tile_count) for i in ran...  8.94 us
    pallas_call x1, Pallas kernels, per_device(): pl.pallas_call(functools.partial(forward_kernel, plan), out_shape=[struct...  3.04 us
    pallas_call x1, Pallas kernels, per_device(): pl.pallas_call(stencil_kernel, out_shape=[struct((fields.shape[1], cells)...  2.84 us
    pallas_call x1, Pallas kernels, per_device(): pl.pallas_call(functools.partial(backward_kernel, frows), out_shape=struc...  1.55 us
    pallas_call x1, Pallas kernels, per_device(): pl.pallas_call(load_kernel, out_shape=[struct(x.shape, x.dtype) for x in...  1.13 us
  transfers between devices with their start and end apart: 6, of which 2 were waited for; matrix products, arithmetic and copies ran while one was open for 0% of the time, Pallas kernels for 12%

profile of v8, /device:TPU:0, one launch (start us, length us, event | category | flops | bytes accessed | tf_op | source)
XLA Modules:
  0.0 31.9 jit_solution(6835251679544485874)
XLA Ops:
  0.6 0.5 %collective-permute-start = (bf16[4,8192]{1,0:T(4,128)(2,1)}, bf16[4,8192]{1,0:T(4,128)(2,1)S(1)}, u32[]{:S(2)}, u32[]{:S(2)}) collective-permute-start(bf16[4,8192]{1,0:T(4,128)(2,1)} %bitcast.36), channel_id=1, source_target_pairs={{0,16},{16,0},{1,17},{17,1},{2,18},{18,2},{3,19},{19,3},{4,20},{20... | collective-permute-start | bytes 196616 | tf_op jit(solution)/shard_map/ppermute | solution.py:719
  1.2 0.1 collective-permute-start.1
  1.2 1.1 %load.1 = (f32[8,8192]{1,0:T(8,128)S(1)}, f32[64,128]{1,0:T(8,128)S(1)}, f32[3,64,128]{2,1,0:T(8,128)S(1)}, s32[3,64,128]{2,1,0:T(8,128)S(1)}, s32[64,128]{1,0:T...) custom-call(f32[8,8192]{1,0:T(8,128)} %bitcast.20, ...), custom_call_target="tpu_custom_call" | custom-call | tf_op jit(solution)/shard_map/load/pallas_call | solution.py:733
  2.4 0.1 collective-permute-done.1.sends
  2.5 0.0 collective-permute-done.surface
  2.5 0.3 pack.1
  2.8 2.9 %collective-permute-start.2 = (bf16[256,128]{1,0:T(8,128)(2,1)S(1)}, bf16[256,128]{1,0:T(8,128)(2,1)S(1)}, u32[]{:S(2)}, u32[]{:S(2)}) collective-permute-start(bf16[256,128]{1,0:T(8,128)(2,1)S(1)} %get-tuple-element.51), channel_id=1, source_target_pairs={{0,1},{1,2},{2,3},{3,4},{4,5},{5,7},{6,8},{7,6},{8,10},{9,11},{10,... | collective-permute-start | bytes 196616 | tf_op jit(solution)/shard_map/ppermute | solution.py:764
  5.6 4.1 %collective-permute-start.3 = (bf16[256,128]{1,0:T(8,128)(2,1)S(1)}, bf16[256,128]{1,0:T(8,128)(2,1)S(1)}, u32[]{:S(2)}, u32[]{:S(2)}) collective-permute-start(bf16[256,128]{1,0:T(8,128)(2,1)S(1)} %get-tuple-element.52), channel_id=1, source_target_pairs={{0,15},{1,3},{2,4},{3,1},{4,2},{5,6},{6,5},{7,9},{8,7},{9,10},{10,... | collective-permute-start | bytes 196616 | tf_op jit(solution)/shard_map/ppermute | solution.py:764
  9.7 0.7 %collective-permute-start.4 = (bf16[256,128]{1,0:T(8,128)(2,1)S(1)}, bf16[256,128]{1,0:T(8,128)(2,1)S(1)}, u32[]{:S(2)}, u32[]{:S(2)}) collective-permute-start(bf16[256,128]{1,0:T(8,128)(2,1)S(1)} %get-tuple-element.53), channel_id=1, source_target_pairs={{0,14},{1,15},{2,0},{3,2},{4,3},{5,4},{6,7},{7,5},{8,6},{9,8},{10,... | collective-permute-start | bytes 196616 | tf_op jit(solution)/shard_map/ppermute | solution.py:764
  10.4 1.4 %collective-permute-start.5 = (bf16[256,128]{1,0:T(8,128)(2,1)S(1)}, bf16[256,128]{1,0:T(8,128)(2,1)S(1)}, u32[]{:S(2)}, u32[]{:S(2)}) collective-permute-start(bf16[256,128]{1,0:T(8,128)(2,1)S(1)} %get-tuple-element.54), channel_id=1, source_target_pairs={{0,2},{1,0},{2,1},{3,5},{4,6},{5,3},{6,4},{7,8},{8,9},{9,7},{10,12... | collective-permute-start | bytes 196616 | tf_op jit(solution)/shard_map/ppermute | solution.py:764
  11.7 2.8 %stencil.1 = (f32[8,8192]{1,0:T(8,128)S(1)}, f32[64,128]{1,0:T(8,128)S(1)}, f32[64,128]{1,0:T(8,128)S(1)}, s32[3,64,128]{2,1,0:T(8,128)S(1)}, s32[8,128]{1,0:T(8...) custom-call(bf16[128,128]{1,0:T(8,128)(2,1)S(1)} %get-tuple-element., ...), custom_call_target="tpu_custom_call" | custom-call | tf_op jit(solution)/shard_map/stencil/pallas_call | solution.py:771
  14.6 0.0 collective-permute-done.2.message0
  14.6 0.0 collective-permute-done.3.message1
  14.6 0.4 %collective-permute-done.4.message2 = bf16[256,128]{1,0:T(8,128)(2,1)S(1)} collective-permute-done((bf16[256,128]{1,0:T(8,128)(2,1)S(1)}, bf16[256,128]{1,0:T(8,128)(2,1)S(1)}, u32[]{:S(2)}, u32[]{:S(2)}) %collective-permute-start.4) | collective-permute-done | bytes 65568 | tf_op jit(solution)/shard_map/ppermute | solution.py:764
  15.0 0.0 collective-permute-done.5.message3
  15.0 3.0 %forward.1 = (f32[64,128]{1,0:T(8,128)S(1)}, f32[64,128]{1,0:T(8,128)S(1)}, f32[32,128]{1,0:T(8,128)S(1)}, f32[256,128]{1,0:T(8,128)S(1)}, f32[16,48,128]{2,1,0:...) custom-call(bf16[160,128,128]{2,1,0:T(8,128)(2,1)S(1)} %get-tuple-el, ...), custom_call_target="tpu_custom_call" | custom-call | tf_op jit(solution)/shard_map/forward/pallas_call | solution.py:795
  18.0 12.3 %all_to_all.5.arrived = f32[16,4,128]{2,1,0:T(4,128)S(1)} all-to-all(f32[16,4,128]{2,1,0:T(4,128)S(1)} %get-tuple-element.66), channel_id=1, replica_groups=mesh['comp'=2,'tile'=16] {'tile'}, dimensions={0} | all-to-all | bytes 65536 | tf_op jit(solution)/shard_map/all_to_all | solution.py:828
  30.3 1.6 %backward.1 = f32[64,128]{1,0:T(8,128)} custom-call(f32[16,4,128]{2,1,0:T(4,128)S(1)} %all_to_all.5.arrived, f32[16,48,128]{2,1,0:T(8,128)S(1)} %get-tuple-element.67.weights, f32[32,128]{1,0:T(8,128)S(1)} %get-tuple-element.68.source, f32[256,128]{1,0:T(8,128)S(1)} %get-tuple-element.69.frame, f32[64,128]{1,0:T(8,128)S(1)} %get-tuple-element.70.force, ...), custom_call_target="tpu_custom_call" | custom-call | tf_op jit(solution)/shard_map/backward/pallas_call | solution.py:829
Async XLA Ops:
  0.6 1.9 %collective-permute-start = (bf16[4,8192]{1,0:T(4,128)(2,1)}, bf16[4,8192]{1,0:T(4,128)(2,1)S(1)}, u32[]{:S(2)}, u32[]{:S(2)}) collective-permute-start(bf16[4,8192]{1,0:T(4,128)(2,1)} %bitcast.36), channel_id=1, source_target_pairs={{0,16},{16,0},{1,17},{17,1},{2,18},{18,2},{3,19},{19,3},{4,20},{20... | collective-permute-start | bytes 196616 | tf_op jit(solution)/shard_map/ppermute | solution.py:719
  1.2 1.4 %collective-permute-start.1 = (s32[1,160]{1,0:T(1,128)}, s32[1,160]{1,0:T(1,128)S(1)}, u32[]{:S(2)}, u32[]{:S(2)}) collective-permute-start(s32[1,160]{1,0:T(1,128)} %bitcast.37), channel_id=1, source_target_pairs={{0,16},{16,0},{1,17},{17,1},{2,18},{18,2},{3,19},{19,3},{4,20},{20... | collective-permute-start | bytes 1928 | tf_op jit(solution)/shard_map/ppermute | solution.py:720
  2.8 11.8 %collective-permute-start.2 = (bf16[256,128]{1,0:T(8,128)(2,1)S(1)}, bf16[256,128]{1,0:T(8,128)(2,1)S(1)}, u32[]{:S(2)}, u32[]{:S(2)}) collective-permute-start(bf16[256,128]{1,0:T(8,128)(2,1)S(1)} %get-tuple-element.51), channel_id=1, source_target_pairs={{0,1},{1,2},{2,3},{3,4},{4,5},{5,7},{6,8},{7,6},{8,10},{9,11},{10,... | collective-permute-start | bytes 196616 | tf_op jit(solution)/shard_map/ppermute | solution.py:764
  5.6 8.9 %collective-permute-start.3 = (bf16[256,128]{1,0:T(8,128)(2,1)S(1)}, bf16[256,128]{1,0:T(8,128)(2,1)S(1)}, u32[]{:S(2)}, u32[]{:S(2)}) collective-permute-start(bf16[256,128]{1,0:T(8,128)(2,1)S(1)} %get-tuple-element.52), channel_id=1, source_target_pairs={{0,15},{1,3},{2,4},{3,1},{4,2},{5,6},{6,5},{7,9},{8,7},{9,10},{10,... | collective-permute-start | bytes 196616 | tf_op jit(solution)/shard_map/ppermute | solution.py:764
  9.7 5.3 %collective-permute-start.4 = (bf16[256,128]{1,0:T(8,128)(2,1)S(1)}, bf16[256,128]{1,0:T(8,128)(2,1)S(1)}, u32[]{:S(2)}, u32[]{:S(2)}) collective-permute-start(bf16[256,128]{1,0:T(8,128)(2,1)S(1)} %get-tuple-element.53), channel_id=1, source_target_pairs={{0,14},{1,15},{2,0},{3,2},{4,3},{5,4},{6,7},{7,5},{8,6},{9,8},{10,... | collective-permute-start | bytes 196616 | tf_op jit(solution)/shard_map/ppermute | solution.py:764
  10.4 4.6 %collective-permute-start.5 = (bf16[256,128]{1,0:T(8,128)(2,1)S(1)}, bf16[256,128]{1,0:T(8,128)(2,1)S(1)}, u32[]{:S(2)}, u32[]{:S(2)}) collective-permute-start(bf16[256,128]{1,0:T(8,128)(2,1)S(1)} %get-tuple-element.54), channel_id=1, source_target_pairs={{0,2},{1,0},{2,1},{3,5},{4,6},{5,3},{6,4},{7,8},{8,9},{9,7},{10,12... | collective-permute-start | bytes 196616 | tf_op jit(solution)/shard_map/ppermute | solution.py:764

commit v9 on v8

--- a/solution.py
+++ b/solution.py
@@ -604,7 +604,8 @@
     )
     for other in range(message.shape[0]):
         message[other] = to_right
-    message[lax.rem(tile + tile_count - 1, tile_count)] = to_left
+    for group in range(2):
+        message[group * tile_count + lax.rem(tile + tile_count - 1, tile_count)] = to_left
     copies[4].start()
     for copy in copies:
         copy.wait()
@@ -638,6 +639,7 @@
     tile = lax.axis_index("tile")
     tile_count = lax.axis_size("tile")
     blocks = force.shape[0]
+    arrived = arrived.at[pl.ds(lax.axis_index("comp") * tile_count, tile_count)]
     left = arrived[lax.rem(tile + tile_count - 1, tile_count)]
     right = arrived[lax.rem(tile + 1, tile_count)]
     count = weights.shape[1]
@@ -803,7 +805,7 @@
             struct((2, 8, LANES), I32),
             struct((fields.shape[1], cells)),
             struct((channels, cells)),
-            struct((tile_count, 4, LANES)),
+            struct((2 * tile_count, 4, LANES)),
         ],
         in_specs=[VMEM] * 24,
         out_specs=[VMEM] * 6 + [ANY] * 3,
@@ -816,7 +818,7 @@
             pltpu.VMEM((3 * bottoms, bottoms * tile_count), F32),
             pltpu.VMEM((2, fields.shape[1], LANES), F32),
             pltpu.VMEM((channels, cells), F32),
-            pltpu.VMEM((tile_count, 4, LANES), F32),
+            pltpu.VMEM((2 * tile_count, 4, LANES), F32),
             pltpu.SemaphoreType.DMA((5,)),
         ],
         compiler_params=PARAMS,
@@ -825,7 +827,7 @@
         tiles, scalars, *messages, here, hot, member, current, edges, window, old,
         damping, force_part, beside_old, ends_row, ends_lane, fresh, ctable, cedge, cdiag, cowner, cinverse,
     )
-    arrived = lax.all_to_all(message, "tile", split_axis=0, concat_axis=0, tiled=True)
+    arrived = lax.all_to_all(message, ("comp", "tile"), split_axis=0, concat_axis=0, tiled=True)
     height = pl.pallas_call(
         functools.partial(backward_kernel, frows),
         out_shape=struct((blocks, LANES)),

time: 32.1 us -> 31 us (0.966)
  blocking collectives: 12.3 us -> 11.2 us
    all_to_all x1, blocking collectives: 12.3 us -> 11.2 us  [per_device(): lax.all_to_all(message, ('comp', 'tile'), split_axis=0, concat_axis=0, ti...]
  transfers between devices with their start and end apart: 6 -> 6, of which waited for: 2 -> 2; matrix products, arithmetic and copies ran while one was open for 0% -> 0% of each run, Pallas kernels for 12% -> 13%
where the time goes in v9:
time: 31 us; the launch traced here: 30.8 us
  blocking collectives  11.2 us (36%)
  starting transfers between devices  9.54 us (31%)
  Pallas kernels  8.87 us (29%)
  between operations  0.69 us (2%)
  waiting for transfers between devices  0.54 us (2%)
    all_to_all x1, blocking collectives, per_device(): lax.all_to_all(message, ('comp', 'tile'), split_axis=0, concat_axis=0, ti...  11.2 us
    ppermute x4, starting transfers between devices, per_device(): lax.ppermute(message, 'tile', [(i, (i + op[i]) % tile_count) for i in ran...  8.94 us
    pallas_call x1, Pallas kernels, per_device(): pl.pallas_call(functools.partial(forward_kernel, plan), out_shape=[struct...  3.09 us
    pallas_call x1, Pallas kernels, per_device(): pl.pallas_call(stencil_kernel, out_shape=[struct((fields.shape[1], cells)...  2.84 us
    pallas_call x1, Pallas kernels, per_device(): pl.pallas_call(functools.partial(backward_kernel, frows), out_shape=struc...  1.55 us
    pallas_call x1, Pallas kernels, per_device(): pl.pallas_call(load_kernel, out_shape=[struct(x.shape, x.dtype) for x in...  1.13 us
  transfers between devices with their start and end apart: 6, of which 2 were waited for; matrix products, arithmetic and copies ran while one was open for 0% of the time, Pallas kernels for 13%

profile of v9, /device:TPU:0, one launch (start us, length us, event | category | flops | bytes accessed | tf_op | source)
XLA Modules:
  0.0 30.8 jit_solution(15007399441834879152)
XLA Ops:
  0.6 0.5 %collective-permute-start = (bf16[4,8192]{1,0:T(4,128)(2,1)}, bf16[4,8192]{1,0:T(4,128)(2,1)S(1)}, u32[]{:S(2)}, u32[]{:S(2)}) collective-permute-start(bf16[4,8192]{1,0:T(4,128)(2,1)} %bitcast.36), channel_id=1, source_target_pairs={{0,16},{16,0},{1,17},{17,1},{2,18},{18,2},{3,19},{19,3},{4,20},{20... | collective-permute-start | bytes 196616 | tf_op jit(solution)/shard_map/ppermute | solution.py:721
  1.2 0.1 collective-permute-start.1
  1.2 1.1 %load.1 = (f32[8,8192]{1,0:T(8,128)S(1)}, f32[64,128]{1,0:T(8,128)S(1)}, f32[3,64,128]{2,1,0:T(8,128)S(1)}, s32[3,64,128]{2,1,0:T(8,128)S(1)}, s32[64,128]{1,0:T...) custom-call(f32[8,8192]{1,0:T(8,128)} %bitcast.20, ...), custom_call_target="tpu_custom_call" | custom-call | tf_op jit(solution)/shard_map/load/pallas_call | solution.py:735
  2.4 0.1 collective-permute-done.1.sends
  2.5 0.0 collective-permute-done.surface
  2.5 0.3 pack.1
  2.8 2.9 %collective-permute-start.2 = (bf16[256,128]{1,0:T(8,128)(2,1)S(1)}, bf16[256,128]{1,0:T(8,128)(2,1)S(1)}, u32[]{:S(2)}, u32[]{:S(2)}) collective-permute-start(bf16[256,128]{1,0:T(8,128)(2,1)S(1)} %get-tuple-element.51), channel_id=1, source_target_pairs={{0,1},{1,2},{2,3},{3,4},{4,5},{5,7},{6,8},{7,6},{8,10},{9,11},{10,... | collective-permute-start | bytes 196616 | tf_op jit(solution)/shard_map/ppermute | solution.py:766
  5.6 4.1 %collective-permute-start.3 = (bf16[256,128]{1,0:T(8,128)(2,1)S(1)}, bf16[256,128]{1,0:T(8,128)(2,1)S(1)}, u32[]{:S(2)}, u32[]{:S(2)}) collective-permute-start(bf16[256,128]{1,0:T(8,128)(2,1)S(1)} %get-tuple-element.52), channel_id=1, source_target_pairs={{0,15},{1,3},{2,4},{3,1},{4,2},{5,6},{6,5},{7,9},{8,7},{9,10},{10,... | collective-permute-start | bytes 196616 | tf_op jit(solution)/shard_map/ppermute | solution.py:766
  9.7 0.7 %collective-permute-start.4 = (bf16[256,128]{1,0:T(8,128)(2,1)S(1)}, bf16[256,128]{1,0:T(8,128)(2,1)S(1)}, u32[]{:S(2)}, u32[]{:S(2)}) collective-permute-start(bf16[256,128]{1,0:T(8,128)(2,1)S(1)} %get-tuple-element.53), channel_id=1, source_target_pairs={{0,14},{1,15},{2,0},{3,2},{4,3},{5,4},{6,7},{7,5},{8,6},{9,8},{10,... | collective-permute-start | bytes 196616 | tf_op jit(solution)/shard_map/ppermute | solution.py:766
  10.4 1.4 %collective-permute-start.5 = (bf16[256,128]{1,0:T(8,128)(2,1)S(1)}, bf16[256,128]{1,0:T(8,128)(2,1)S(1)}, u32[]{:S(2)}, u32[]{:S(2)}) collective-permute-start(bf16[256,128]{1,0:T(8,128)(2,1)S(1)} %get-tuple-element.54), channel_id=1, source_target_pairs={{0,2},{1,0},{2,1},{3,5},{4,6},{5,3},{6,4},{7,8},{8,9},{9,7},{10,12... | collective-permute-start | bytes 196616 | tf_op jit(solution)/shard_map/ppermute | solution.py:766
  11.7 2.8 %stencil.1 = (f32[8,8192]{1,0:T(8,128)S(1)}, f32[64,128]{1,0:T(8,128)S(1)}, f32[64,128]{1,0:T(8,128)S(1)}, s32[3,64,128]{2,1,0:T(8,128)S(1)}, s32[8,128]{1,0:T(8...) custom-call(bf16[128,128]{1,0:T(8,128)(2,1)S(1)} %get-tuple-element., ...), custom_call_target="tpu_custom_call" | custom-call | tf_op jit(solution)/shard_map/stencil/pallas_call | solution.py:773
  14.6 0.0 collective-permute-done.2.message0
  14.6 0.0 collective-permute-done.3.message1
  14.6 0.4 %collective-permute-done.4.message2 = bf16[256,128]{1,0:T(8,128)(2,1)S(1)} collective-permute-done((bf16[256,128]{1,0:T(8,128)(2,1)S(1)}, bf16[256,128]{1,0:T(8,128)(2,1)S(1)}, u32[]{:S(2)}, u32[]{:S(2)}) %collective-permute-start.4) | collective-permute-done | bytes 65568 | tf_op jit(solution)/shard_map/ppermute | solution.py:766
  15.0 0.0 collective-permute-done.5.message3
  15.0 3.1 %forward.1 = (f32[64,128]{1,0:T(8,128)S(1)}, f32[64,128]{1,0:T(8,128)S(1)}, f32[32,128]{1,0:T(8,128)S(1)}, f32[256,128]{1,0:T(8,128)S(1)}, f32[16,48,128]{2,1,0:...) custom-call(bf16[160,128,128]{2,1,0:T(8,128)(2,1)S(1)} %get-tuple-el, ...), custom_call_target="tpu_custom_call" | custom-call | tf_op jit(solution)/shard_map/forward/pallas_call | solution.py:797
  18.1 11.2 %all_to_all.5.arrived = f32[32,4,128]{2,1,0:T(4,128)S(1)} all-to-all(f32[32,4,128]{2,1,0:T(4,128)S(1)} %get-tuple-element.66), channel_id=1, replica_groups=mesh['comp'=2,'tile'=16] {'comp','tile'}, dimensions={0} | all-to-all | bytes 131072 | tf_op jit(solution)/shard_map/all_to_all | solution.py:830
  29.3 1.6 %backward.1 = f32[64,128]{1,0:T(8,128)} custom-call(f32[32,4,128]{2,1,0:T(4,128)S(1)} %all_to_all.5.arrived, f32[16,48,128]{2,1,0:T(8,128)S(1)} %get-tuple-element.67.weights, f32[32,128]{1,0:T(8,128)S(1)} %get-tuple-element.68.source, f32[256,128]{1,0:T(8,128)S(1)} %get-tuple-element.69.frame, f32[64,128]{1,0:T(8,128)S(1)} %get-tuple-element.70.force, ...), custom_call_target="tpu_custom_call" | custom-call | tf_op jit(solution)/shard_map/backward/pallas_call | solution.py:831
Async XLA Ops:
  0.6 1.9 %collective-permute-start = (bf16[4,8192]{1,0:T(4,128)(2,1)}, bf16[4,8192]{1,0:T(4,128)(2,1)S(1)}, u32[]{:S(2)}, u32[]{:S(2)}) collective-permute-start(bf16[4,8192]{1,0:T(4,128)(2,1)} %bitcast.36), channel_id=1, source_target_pairs={{0,16},{16,0},{1,17},{17,1},{2,18},{18,2},{3,19},{19,3},{4,20},{20... | collective-permute-start | bytes 196616 | tf_op jit(solution)/shard_map/ppermute | solution.py:721
  1.2 1.4 %collective-permute-start.1 = (s32[1,160]{1,0:T(1,128)}, s32[1,160]{1,0:T(1,128)S(1)}, u32[]{:S(2)}, u32[]{:S(2)}) collective-permute-start(s32[1,160]{1,0:T(1,128)} %bitcast.37), channel_id=1, source_target_pairs={{0,16},{16,0},{1,17},{17,1},{2,18},{18,2},{3,19},{19,3},{4,20},{20... | collective-permute-start | bytes 1928 | tf_op jit(solution)/shard_map/ppermute | solution.py:722
  2.8 11.8 %collective-permute-start.2 = (bf16[256,128]{1,0:T(8,128)(2,1)S(1)}, bf16[256,128]{1,0:T(8,128)(2,1)S(1)}, u32[]{:S(2)}, u32[]{:S(2)}) collective-permute-start(bf16[256,128]{1,0:T(8,128)(2,1)S(1)} %get-tuple-element.51), channel_id=1, source_target_pairs={{0,1},{1,2},{2,3},{3,4},{4,5},{5,7},{6,8},{7,6},{8,10},{9,11},{10,... | collective-permute-start | bytes 196616 | tf_op jit(solution)/shard_map/ppermute | solution.py:766
  5.6 8.9 %collective-permute-start.3 = (bf16[256,128]{1,0:T(8,128)(2,1)S(1)}, bf16[256,128]{1,0:T(8,128)(2,1)S(1)}, u32[]{:S(2)}, u32[]{:S(2)}) collective-permute-start(bf16[256,128]{1,0:T(8,128)(2,1)S(1)} %get-tuple-element.52), channel_id=1, source_target_pairs={{0,15},{1,3},{2,4},{3,1},{4,2},{5,6},{6,5},{7,9},{8,7},{9,10},{10,... | collective-permute-start | bytes 196616 | tf_op jit(solution)/shard_map/ppermute | solution.py:766
  9.7 5.3 %collective-permute-start.4 = (bf16[256,128]{1,0:T(8,128)(2,1)S(1)}, bf16[256,128]{1,0:T(8,128)(2,1)S(1)}, u32[]{:S(2)}, u32[]{:S(2)}) collective-permute-start(bf16[256,128]{1,0:T(8,128)(2,1)S(1)} %get-tuple-element.53), channel_id=1, source_target_pairs={{0,14},{1,15},{2,0},{3,2},{4,3},{5,4},{6,7},{7,5},{8,6},{9,8},{10,... | collective-permute-start | bytes 196616 | tf_op jit(solution)/shard_map/ppermute | solution.py:766
  10.4 4.6 %collective-permute-start.5 = (bf16[256,128]{1,0:T(8,128)(2,1)S(1)}, bf16[256,128]{1,0:T(8,128)(2,1)S(1)}, u32[]{:S(2)}, u32[]{:S(2)}) collective-permute-start(bf16[256,128]{1,0:T(8,128)(2,1)S(1)} %get-tuple-element.54), channel_id=1, source_target_pairs={{0,2},{1,0},{2,1},{3,5},{4,6},{5,3},{6,4},{7,8},{8,9},{9,7},{10,12... | collective-permute-start | bytes 196616 | tf_op jit(solution)/shard_map/ppermute | solution.py:766

commit v10 on v9

--- a/solution.py
+++ b/solution.py
@@ -88,8 +88,8 @@
     return lax.dot_general(a, b, (((0,), (0,)), ((), ())), preferred_element_type=F32)
 
 
-def pick_base(inverse_blocks):
-    return -(-(INVERSE + 32 * inverse_blocks) // 16) * 16
+def pick_base(bottoms, size):
+    return -(-(INVERSE + 2 * bottoms * (size // LANES)) // 16) * 16
 
 
 def load_kernel(*refs):
@@ -113,7 +113,8 @@
     blocks = cells // LANES
     frows = ctable.shape[1]
     firsts = frows * LANES
-    base = pick_base(cinverse.shape[1] // LANES)
+    bottoms = cinverse.shape[0]
+    base = pick_base(*cinverse.shape)
     lane = lax.broadcasted_iota(I32, (1, LANES), 1)
 
     for rows, at_left in ((right_rows, False), (left_rows, True)):
@@ -148,11 +149,11 @@
         halves = cinverse.shape[1] // LANES
         for half in range(halves):
             both(
-                INVERSE + 16 * half,
-                INVERSE + 16 * (halves + half),
+                INVERSE + bottoms * half,
+                INVERSE + bottoms * (halves + half),
                 cinverse[:, pl.ds(half * LANES, LANES)],
             )
-        end = INVERSE + 32 * halves
+        end = INVERSE + 2 * bottoms * halves
         if base > end:
             rows[pl.ds(end, base - end), :] = jnp.zeros((base - end, LANES), F32)
 
@@ -542,7 +543,7 @@
     frame[...] = jnp.zeros(frame.shape, F32)
     frame[pl.ds(6 * FRAME, FRAME), :] = jnp.ones((FRAME, LANES), F32)
     frame[pl.ds(7 * FRAME, FRAME), :] = jnp.full((FRAME, LANES), 127.0, F32)
-    bottoms = 16
+    bottoms = cinverse.shape[0]
     at_cell = lax.broadcasted_iota(I32, (frows, LANES), 0) * LANES + lax.broadcasted_iota(
         I32, (frows, LANES), 1
     )
@@ -617,7 +618,7 @@
     for half in range(halves):
         part = pl.ds(half * LANES, LANES)
         for at, block in ((0, left), (2, right)):
-            high, low = INVERSE + 16 * half, INVERSE + 16 * (halves + half)
+            high, low = INVERSE + bottoms * half, INVERSE + bottoms * (halves + half)
             extended[pl.ds(at * bottoms, bottoms), part] = (
                 block[pl.ds(high, bottoms), :] + block[pl.ds(low, bottoms), :]
             )
@@ -643,9 +644,11 @@
     left = arrived[lax.rem(tile + tile_count - 1, tile_count)]
     right = arrived[lax.rem(tile + 1, tile_count)]
     count = weights.shape[1]
-    partial = jnp.zeros((count, LANES), F32)
+    sums = [jnp.zeros((count, LANES), F32)] * 4
     for other in range(weights.shape[0]):
-        partial = partial + weights[other] * wide(arrived[other, pl.ds(0, 1), :], count)
+        part = weights[other] * wide(arrived[other, pl.ds(0, 1), :], count)
+        sums[other % 4] = sums[other % 4] + part
+    partial = (sums[0] + sums[1]) + (sums[2] + sums[3])
     partial = jnp.concatenate([partial, jnp.zeros((LANES - count, LANES), F32)], axis=0)
     ones = jnp.ones((8, LANES), BF16)
     bottom = dot_nt(jnp.concatenate([ones, ones], axis=1), jnp.concatenate(split2(partial), axis=1))
@@ -714,9 +717,8 @@
     channels = surface_out.shape[1]
     slots = send_blocks.shape[2]
     each = slots // 5
-    halves = coarse_inverse.shape[2] // LANES
     bottoms = coarse_inverse.shape[1]
-    base = pick_base(halves)
+    base = pick_base(*coarse_inverse.shape[1:])
     swap = [(0, 1), (1, 0)]
     surface = lax.ppermute(surface_out[0], "comp", swap)
     sends = lax.ppermute(send_blocks[0], "comp", swap)

time: 31 us -> 31 us (level)
  no operation moved by 1% of the time
where the time goes in v10:
time: 31 us; the launch traced here: 30.8 us
  blocking collectives  11.2 us (36%)
  starting transfers between devices  9.54 us (31%)
  Pallas kernels  8.87 us (29%)
  between operations  0.69 us (2%)
  waiting for transfers between devices  0.54 us (2%)
    all_to_all x1, blocking collectives, per_device(): lax.all_to_all(message, ('comp', 'tile'), split_axis=0, concat_axis=0, ti...  11.2 us
    ppermute x4, starting transfers between devices, per_device(): lax.ppermute(message, 'tile', [(i, (i + op[i]) % tile_count) for i in ran...  8.94 us
    pallas_call x1, Pallas kernels, per_device(): pl.pallas_call(functools.partial(forward_kernel, plan), out_shape=[struct...  3.09 us
    pallas_call x1, Pallas kernels, per_device(): pl.pallas_call(stencil_kernel, out_shape=[struct((fields.shape[1], cells)...  2.84 us
    pallas_call x1, Pallas kernels, per_device(): pl.pallas_call(functools.partial(backward_kernel, frows), out_shape=struc...  1.55 us
    pallas_call x1, Pallas kernels, per_device(): pl.pallas_call(load_kernel, out_shape=[struct(x.shape, x.dtype) for x in...  1.13 us
  transfers between devices with their start and end apart: 6, of which 2 were waited for; matrix products, arithmetic and copies ran while one was open for 0% of the time, Pallas kernels for 13%

profile of v10, /device:TPU:0, one launch (start us, length us, event | category | flops | bytes accessed | tf_op | source)
XLA Modules:
  0.0 30.8 jit_solution(6819560383941175236)
XLA Ops:
  0.6 0.5 %collective-permute-start = (bf16[4,8192]{1,0:T(4,128)(2,1)}, bf16[4,8192]{1,0:T(4,128)(2,1)S(1)}, u32[]{:S(2)}, u32[]{:S(2)}) collective-permute-start(bf16[4,8192]{1,0:T(4,128)(2,1)} %bitcast.36), channel_id=1, source_target_pairs={{0,16},{16,0},{1,17},{17,1},{2,18},{18,2},{3,19},{19,3},{4,20},{20... | collective-permute-start | bytes 196616 | tf_op jit(solution)/shard_map/ppermute | solution.py:723
  1.2 0.1 collective-permute-start.1
  1.2 1.1 %load.1 = (f32[8,8192]{1,0:T(8,128)S(1)}, f32[64,128]{1,0:T(8,128)S(1)}, f32[3,64,128]{2,1,0:T(8,128)S(1)}, s32[3,64,128]{2,1,0:T(8,128)S(1)}, s32[64,128]{1,0:T...) custom-call(f32[8,8192]{1,0:T(8,128)} %bitcast.20, ...), custom_call_target="tpu_custom_call" | custom-call | tf_op jit(solution)/shard_map/load/pallas_call | solution.py:737
  2.4 0.1 collective-permute-done.1.sends
  2.5 0.0 collective-permute-done.surface
  2.5 0.3 pack.1
  2.8 2.9 %collective-permute-start.2 = (bf16[256,128]{1,0:T(8,128)(2,1)S(1)}, bf16[256,128]{1,0:T(8,128)(2,1)S(1)}, u32[]{:S(2)}, u32[]{:S(2)}) collective-permute-start(bf16[256,128]{1,0:T(8,128)(2,1)S(1)} %get-tuple-element.51), channel_id=1, source_target_pairs={{0,1},{1,2},{2,3},{3,4},{4,5},{5,7},{6,8},{7,6},{8,10},{9,11},{10,... | collective-permute-start | bytes 196616 | tf_op jit(solution)/shard_map/ppermute | solution.py:768
  5.6 4.1 %collective-permute-start.3 = (bf16[256,128]{1,0:T(8,128)(2,1)S(1)}, bf16[256,128]{1,0:T(8,128)(2,1)S(1)}, u32[]{:S(2)}, u32[]{:S(2)}) collective-permute-start(bf16[256,128]{1,0:T(8,128)(2,1)S(1)} %get-tuple-element.52), channel_id=1, source_target_pairs={{0,15},{1,3},{2,4},{3,1},{4,2},{5,6},{6,5},{7,9},{8,7},{9,10},{10,... | collective-permute-start | bytes 196616 | tf_op jit(solution)/shard_map/ppermute | solution.py:768
  9.7 0.7 %collective-permute-start.4 = (bf16[256,128]{1,0:T(8,128)(2,1)S(1)}, bf16[256,128]{1,0:T(8,128)(2,1)S(1)}, u32[]{:S(2)}, u32[]{:S(2)}) collective-permute-start(bf16[256,128]{1,0:T(8,128)(2,1)S(1)} %get-tuple-element.53), channel_id=1, source_target_pairs={{0,14},{1,15},{2,0},{3,2},{4,3},{5,4},{6,7},{7,5},{8,6},{9,8},{10,... | collective-permute-start | bytes 196616 | tf_op jit(solution)/shard_map/ppermute | solution.py:768
  10.4 1.4 %collective-permute-start.5 = (bf16[256,128]{1,0:T(8,128)(2,1)S(1)}, bf16[256,128]{1,0:T(8,128)(2,1)S(1)}, u32[]{:S(2)}, u32[]{:S(2)}) collective-permute-start(bf16[256,128]{1,0:T(8,128)(2,1)S(1)} %get-tuple-element.54), channel_id=1, source_target_pairs={{0,2},{1,0},{2,1},{3,5},{4,6},{5,3},{6,4},{7,8},{8,9},{9,7},{10,12... | collective-permute-start | bytes 196616 | tf_op jit(solution)/shard_map/ppermute | solution.py:768
  11.7 2.8 %stencil.1 = (f32[8,8192]{1,0:T(8,128)S(1)}, f32[64,128]{1,0:T(8,128)S(1)}, f32[64,128]{1,0:T(8,128)S(1)}, s32[3,64,128]{2,1,0:T(8,128)S(1)}, s32[8,128]{1,0:T(8...) custom-call(bf16[128,128]{1,0:T(8,128)(2,1)S(1)} %get-tuple-element., ...), custom_call_target="tpu_custom_call" | custom-call | tf_op jit(solution)/shard_map/stencil/pallas_call | solution.py:775
  14.6 0.0 collective-permute-done.2.message0
  14.6 0.0 collective-permute-done.3.message1
  14.6 0.4 %collective-permute-done.4.message2 = bf16[256,128]{1,0:T(8,128)(2,1)S(1)} collective-permute-done((bf16[256,128]{1,0:T(8,128)(2,1)S(1)}, bf16[256,128]{1,0:T(8,128)(2,1)S(1)}, u32[]{:S(2)}, u32[]{:S(2)}) %collective-permute-start.4) | collective-permute-done | bytes 65568 | tf_op jit(solution)/shard_map/ppermute | solution.py:768
  15.0 0.0 collective-permute-done.5.message3
  15.0 3.1 %forward.1 = (f32[64,128]{1,0:T(8,128)S(1)}, f32[64,128]{1,0:T(8,128)S(1)}, f32[32,128]{1,0:T(8,128)S(1)}, f32[256,128]{1,0:T(8,128)S(1)}, f32[16,48,128]{2,1,0:...) custom-call(bf16[160,128,128]{2,1,0:T(8,128)(2,1)S(1)} %get-tuple-el, ...), custom_call_target="tpu_custom_call" | custom-call | tf_op jit(solution)/shard_map/forward/pallas_call | solution.py:799
  18.1 11.2 %all_to_all.5.arrived = f32[32,4,128]{2,1,0:T(4,128)S(1)} all-to-all(f32[32,4,128]{2,1,0:T(4,128)S(1)} %get-tuple-element.66), channel_id=1, replica_groups=mesh['comp'=2,'tile'=16] {'comp','tile'}, dimensions={0} | all-to-all | bytes 131072 | tf_op jit(solution)/shard_map/all_to_all | solution.py:832
  29.3 1.5 %backward.1 = f32[64,128]{1,0:T(8,128)} custom-call(f32[32,4,128]{2,1,0:T(4,128)S(1)} %all_to_all.5.arrived, f32[16,48,128]{2,1,0:T(8,128)S(1)} %get-tuple-element.67.weights, f32[32,128]{1,0:T(8,128)S(1)} %get-tuple-element.68.source, f32[256,128]{1,0:T(8,128)S(1)} %get-tuple-element.69.frame, f32[64,128]{1,0:T(8,128)S(1)} %get-tuple-element.70.force, ...), custom_call_target="tpu_custom_call" | custom-call | tf_op jit(solution)/shard_map/backward/pallas_call | solution.py:833
Async XLA Ops:
  0.6 1.9 %collective-permute-start = (bf16[4,8192]{1,0:T(4,128)(2,1)}, bf16[4,8192]{1,0:T(4,128)(2,1)S(1)}, u32[]{:S(2)}, u32[]{:S(2)}) collective-permute-start(bf16[4,8192]{1,0:T(4,128)(2,1)} %bitcast.36), channel_id=1, source_target_pairs={{0,16},{16,0},{1,17},{17,1},{2,18},{18,2},{3,19},{19,3},{4,20},{20... | collective-permute-start | bytes 196616 | tf_op jit(solution)/shard_map/ppermute | solution.py:723
  1.2 1.4 %collective-permute-start.1 = (s32[1,160]{1,0:T(1,128)}, s32[1,160]{1,0:T(1,128)S(1)}, u32[]{:S(2)}, u32[]{:S(2)}) collective-permute-start(s32[1,160]{1,0:T(1,128)} %bitcast.37), channel_id=1, source_target_pairs={{0,16},{16,0},{1,17},{17,1},{2,18},{18,2},{3,19},{19,3},{4,20},{20... | collective-permute-start | bytes 1928 | tf_op jit(solution)/shard_map/ppermute | solution.py:724
  2.8 11.8 %collective-permute-start.2 = (bf16[256,128]{1,0:T(8,128)(2,1)S(1)}, bf16[256,128]{1,0:T(8,128)(2,1)S(1)}, u32[]{:S(2)}, u32[]{:S(2)}) collective-permute-start(bf16[256,128]{1,0:T(8,128)(2,1)S(1)} %get-tuple-element.51), channel_id=1, source_target_pairs={{0,1},{1,2},{2,3},{3,4},{4,5},{5,7},{6,8},{7,6},{8,10},{9,11},{10,... | collective-permute-start | bytes 196616 | tf_op jit(solution)/shard_map/ppermute | solution.py:768
  5.6 8.9 %collective-permute-start.3 = (bf16[256,128]{1,0:T(8,128)(2,1)S(1)}, bf16[256,128]{1,0:T(8,128)(2,1)S(1)}, u32[]{:S(2)}, u32[]{:S(2)}) collective-permute-start(bf16[256,128]{1,0:T(8,128)(2,1)S(1)} %get-tuple-element.52), channel_id=1, source_target_pairs={{0,15},{1,3},{2,4},{3,1},{4,2},{5,6},{6,5},{7,9},{8,7},{9,10},{10,... | collective-permute-start | bytes 196616 | tf_op jit(solution)/shard_map/ppermute | solution.py:768
  9.7 5.3 %collective-permute-start.4 = (bf16[256,128]{1,0:T(8,128)(2,1)S(1)}, bf16[256,128]{1,0:T(8,128)(2,1)S(1)}, u32[]{:S(2)}, u32[]{:S(2)}) collective-permute-start(bf16[256,128]{1,0:T(8,128)(2,1)S(1)} %get-tuple-element.53), channel_id=1, source_target_pairs={{0,14},{1,15},{2,0},{3,2},{4,3},{5,4},{6,7},{7,5},{8,6},{9,8},{10,... | collective-permute-start | bytes 196616 | tf_op jit(solution)/shard_map/ppermute | solution.py:768
  10.4 4.6 %collective-permute-start.5 = (bf16[256,128]{1,0:T(8,128)(2,1)S(1)}, bf16[256,128]{1,0:T(8,128)(2,1)S(1)}, u32[]{:S(2)}, u32[]{:S(2)}) collective-permute-start(bf16[256,128]{1,0:T(8,128)(2,1)S(1)} %get-tuple-element.54), channel_id=1, source_target_pairs={{0,2},{1,0},{2,1},{3,5},{4,6},{5,3},{6,4},{7,8},{8,9},{9,7},{10,12... | collective-permute-start | bytes 196616 | tf_op jit(solution)/shard_map/ppermute | solution.py:768

commit v11 on v10

--- a/solution.py
+++ b/solution.py
@@ -570,7 +570,9 @@
     for link in range(3):
         frame[pl.ds(6 * FRAME, FRAME), :] += frame[pl.ds((3 + link) * FRAME, FRAME), :]
     source = source_out[...]
-    first = (RELAXATION / frame[pl.ds(6 * FRAME, FRAME), :]) * source
+    damp_first = RELAXATION / frame[pl.ds(6 * FRAME, FRAME), :]
+    frame[pl.ds(8 * FRAME, FRAME), :] = damp_first
+    first = damp_first * source
     residual = (1.0 - RELAXATION) * source + first_level_sum(first, frame)
     codes = frame[pl.ds(7 * FRAME, FRAME), :].astype(I32)
     pieces = split2(residual)
@@ -666,7 +668,7 @@
     total_source = frame_source[...]
     total = frame[pl.ds(6 * FRAME, FRAME), :]
     codes = frame[pl.ds(7 * FRAME, FRAME), :].astype(I32)
-    damp = RELAXATION / total
+    damp = frame[pl.ds(8 * FRAME, FRAME), :]
     second = damp * total_source + gather_lanes(wide(bottom[0:1], FRAME), codes)
     third = second + damp * (total_source - total * second + first_level_sum(second, frame))
     third_rows[...] = third
@@ -802,7 +804,7 @@
             struct((blocks, LANES)),
             struct((blocks, LANES)),
             struct((FRAME, LANES)),
-            struct((8 * FRAME, LANES)),
+            struct((9 * FRAME, LANES)),
             struct((tile_count, 3 * bottoms, LANES)),
             struct((2, 8, LANES), I32),
             struct((fields.shape[1], cells)),

time: 31 us -> 31 us (level)
  no operation moved by 1% of the time
where the time goes in v11:
time: 31 us; the launch traced here: 30.8 us
  blocking collectives  11.2 us (36%)
  starting transfers between devices  9.54 us (31%)
  Pallas kernels  8.87 us (29%)
  between operations  0.69 us (2%)
  waiting for transfers between devices  0.54 us (2%)
    all_to_all x1, blocking collectives, per_device(): lax.all_to_all(message, ('comp', 'tile'), split_axis=0, concat_axis=0, ti...  11.2 us
    ppermute x4, starting transfers between devices, per_device(): lax.ppermute(message, 'tile', [(i, (i + op[i]) % tile_count) for i in ran...  8.94 us
    pallas_call x1, Pallas kernels, per_device(): pl.pallas_call(functools.partial(forward_kernel, plan), out_shape=[struct...  3.09 us
    pallas_call x1, Pallas kernels, per_device(): pl.pallas_call(stencil_kernel, out_shape=[struct((fields.shape[1], cells)...  2.84 us
    pallas_call x1, Pallas kernels, per_device(): pl.pallas_call(functools.partial(backward_kernel, frows), out_shape=struc...  1.55 us
    pallas_call x1, Pallas kernels, per_device(): pl.pallas_call(load_kernel, out_shape=[struct(x.shape, x.dtype) for x in...  1.13 us
  transfers between devices with their start and end apart: 6, of which 2 were waited for; matrix products, arithmetic and copies ran while one was open for 0% of the time, Pallas kernels for 13%

profile of v11, /device:TPU:0, one launch (start us, length us, event | category | flops | bytes accessed | tf_op | source)
XLA Modules:
  0.0 30.8 jit_solution(4881155342582954956)
XLA Ops:
  0.6 0.5 %collective-permute-start = (bf16[4,8192]{1,0:T(4,128)(2,1)}, bf16[4,8192]{1,0:T(4,128)(2,1)S(1)}, u32[]{:S(2)}, u32[]{:S(2)}) collective-permute-start(bf16[4,8192]{1,0:T(4,128)(2,1)} %bitcast.36), channel_id=1, source_target_pairs={{0,16},{16,0},{1,17},{17,1},{2,18},{18,2},{3,19},{19,3},{4,20},{20... | collective-permute-start | bytes 196616 | tf_op jit(solution)/shard_map/ppermute | solution.py:725
  1.2 0.1 collective-permute-start.1
  1.2 1.1 %load.1 = (f32[8,8192]{1,0:T(8,128)S(1)}, f32[64,128]{1,0:T(8,128)S(1)}, f32[3,64,128]{2,1,0:T(8,128)S(1)}, s32[3,64,128]{2,1,0:T(8,128)S(1)}, s32[64,128]{1,0:T...) custom-call(f32[8,8192]{1,0:T(8,128)} %bitcast.20, ...), custom_call_target="tpu_custom_call" | custom-call | tf_op jit(solution)/shard_map/load/pallas_call | solution.py:739
  2.4 0.1 collective-permute-done.1.sends
  2.5 0.0 collective-permute-done.surface
  2.5 0.3 pack.1
  2.8 2.9 %collective-permute-start.2 = (bf16[256,128]{1,0:T(8,128)(2,1)S(1)}, bf16[256,128]{1,0:T(8,128)(2,1)S(1)}, u32[]{:S(2)}, u32[]{:S(2)}) collective-permute-start(bf16[256,128]{1,0:T(8,128)(2,1)S(1)} %get-tuple-element.51), channel_id=1, source_target_pairs={{0,1},{1,2},{2,3},{3,4},{4,5},{5,7},{6,8},{7,6},{8,10},{9,11},{10,... | collective-permute-start | bytes 196616 | tf_op jit(solution)/shard_map/ppermute | solution.py:770
  5.6 4.1 %collective-permute-start.3 = (bf16[256,128]{1,0:T(8,128)(2,1)S(1)}, bf16[256,128]{1,0:T(8,128)(2,1)S(1)}, u32[]{:S(2)}, u32[]{:S(2)}) collective-permute-start(bf16[256,128]{1,0:T(8,128)(2,1)S(1)} %get-tuple-element.52), channel_id=1, source_target_pairs={{0,15},{1,3},{2,4},{3,1},{4,2},{5,6},{6,5},{7,9},{8,7},{9,10},{10,... | collective-permute-start | bytes 196616 | tf_op jit(solution)/shard_map/ppermute | solution.py:770
  9.7 0.7 %collective-permute-start.4 = (bf16[256,128]{1,0:T(8,128)(2,1)S(1)}, bf16[256,128]{1,0:T(8,128)(2,1)S(1)}, u32[]{:S(2)}, u32[]{:S(2)}) collective-permute-start(bf16[256,128]{1,0:T(8,128)(2,1)S(1)} %get-tuple-element.53), channel_id=1, source_target_pairs={{0,14},{1,15},{2,0},{3,2},{4,3},{5,4},{6,7},{7,5},{8,6},{9,8},{10,... | collective-permute-start | bytes 196616 | tf_op jit(solution)/shard_map/ppermute | solution.py:770
  10.4 1.4 %collective-permute-start.5 = (bf16[256,128]{1,0:T(8,128)(2,1)S(1)}, bf16[256,128]{1,0:T(8,128)(2,1)S(1)}, u32[]{:S(2)}, u32[]{:S(2)}) collective-permute-start(bf16[256,128]{1,0:T(8,128)(2,1)S(1)} %get-tuple-element.54), channel_id=1, source_target_pairs={{0,2},{1,0},{2,1},{3,5},{4,6},{5,3},{6,4},{7,8},{8,9},{9,7},{10,12... | collective-permute-start | bytes 196616 | tf_op jit(solution)/shard_map/ppermute | solution.py:770
  11.7 2.8 %stencil.1 = (f32[8,8192]{1,0:T(8,128)S(1)}, f32[64,128]{1,0:T(8,128)S(1)}, f32[64,128]{1,0:T(8,128)S(1)}, s32[3,64,128]{2,1,0:T(8,128)S(1)}, s32[8,128]{1,0:T(8...) custom-call(bf16[128,128]{1,0:T(8,128)(2,1)S(1)} %get-tuple-element., ...), custom_call_target="tpu_custom_call" | custom-call | tf_op jit(solution)/shard_map/stencil/pallas_call | solution.py:777
  14.6 0.0 collective-permute-done.2.message0
  14.6 0.0 collective-permute-done.3.message1
  14.6 0.4 %collective-permute-done.4.message2 = bf16[256,128]{1,0:T(8,128)(2,1)S(1)} collective-permute-done((bf16[256,128]{1,0:T(8,128)(2,1)S(1)}, bf16[256,128]{1,0:T(8,128)(2,1)S(1)}, u32[]{:S(2)}, u32[]{:S(2)}) %collective-permute-start.4) | collective-permute-done | bytes 65568 | tf_op jit(solution)/shard_map/ppermute | solution.py:770
  15.0 0.0 collective-permute-done.5.message3
  15.0 3.1 %forward.1 = (f32[64,128]{1,0:T(8,128)S(1)}, f32[64,128]{1,0:T(8,128)S(1)}, f32[32,128]{1,0:T(8,128)S(1)}, f32[288,128]{1,0:T(8,128)S(1)}, f32[16,48,128]{2,1,0:...) custom-call(bf16[160,128,128]{2,1,0:T(8,128)(2,1)S(1)} %get-tuple-el, ...), custom_call_target="tpu_custom_call" | custom-call | tf_op jit(solution)/shard_map/forward/pallas_call | solution.py:801
  18.1 11.2 %all_to_all.5.arrived = f32[32,4,128]{2,1,0:T(4,128)S(1)} all-to-all(f32[32,4,128]{2,1,0:T(4,128)S(1)} %get-tuple-element.66), channel_id=1, replica_groups=mesh['comp'=2,'tile'=16] {'comp','tile'}, dimensions={0} | all-to-all | bytes 131072 | tf_op jit(solution)/shard_map/all_to_all | solution.py:834
  29.3 1.5 %backward.1 = f32[64,128]{1,0:T(8,128)} custom-call(f32[32,4,128]{2,1,0:T(4,128)S(1)} %all_to_all.5.arrived, f32[16,48,128]{2,1,0:T(8,128)S(1)} %get-tuple-element.67.weights, f32[32,128]{1,0:T(8,128)S(1)} %get-tuple-element.68.source, f32[288,128]{1,0:T(8,128)S(1)} %get-tuple-element.69.frame, f32[64,128]{1,0:T(8,128)S(1)} %get-tuple-element.70.force, ...), custom_call_target="tpu_custom_call" | custom-call | tf_op jit(solution)/shard_map/backward/pallas_call | solution.py:835
Async XLA Ops:
  0.6 1.9 %collective-permute-start = (bf16[4,8192]{1,0:T(4,128)(2,1)}, bf16[4,8192]{1,0:T(4,128)(2,1)S(1)}, u32[]{:S(2)}, u32[]{:S(2)}) collective-permute-start(bf16[4,8192]{1,0:T(4,128)(2,1)} %bitcast.36), channel_id=1, source_target_pairs={{0,16},{16,0},{1,17},{17,1},{2,18},{18,2},{3,19},{19,3},{4,20},{20... | collective-permute-start | bytes 196616 | tf_op jit(solution)/shard_map/ppermute | solution.py:725
  1.2 1.4 %collective-permute-start.1 = (s32[1,160]{1,0:T(1,128)}, s32[1,160]{1,0:T(1,128)S(1)}, u32[]{:S(2)}, u32[]{:S(2)}) collective-permute-start(s32[1,160]{1,0:T(1,128)} %bitcast.37), channel_id=1, source_target_pairs={{0,16},{16,0},{1,17},{17,1},{2,18},{18,2},{3,19},{19,3},{4,20},{20... | collective-permute-start | bytes 1928 | tf_op jit(solution)/shard_map/ppermute | solution.py:726
  2.8 11.8 %collective-permute-start.2 = (bf16[256,128]{1,0:T(8,128)(2,1)S(1)}, bf16[256,128]{1,0:T(8,128)(2,1)S(1)}, u32[]{:S(2)}, u32[]{:S(2)}) collective-permute-start(bf16[256,128]{1,0:T(8,128)(2,1)S(1)} %get-tuple-element.51), channel_id=1, source_target_pairs={{0,1},{1,2},{2,3},{3,4},{4,5},{5,7},{6,8},{7,6},{8,10},{9,11},{10,... | collective-permute-start | bytes 196616 | tf_op jit(solution)/shard_map/ppermute | solution.py:770
  5.6 8.9 %collective-permute-start.3 = (bf16[256,128]{1,0:T(8,128)(2,1)S(1)}, bf16[256,128]{1,0:T(8,128)(2,1)S(1)}, u32[]{:S(2)}, u32[]{:S(2)}) collective-permute-start(bf16[256,128]{1,0:T(8,128)(2,1)S(1)} %get-tuple-element.52), channel_id=1, source_target_pairs={{0,15},{1,3},{2,4},{3,1},{4,2},{5,6},{6,5},{7,9},{8,7},{9,10},{10,... | collective-permute-start | bytes 196616 | tf_op jit(solution)/shard_map/ppermute | solution.py:770
  9.7 5.3 %collective-permute-start.4 = (bf16[256,128]{1,0:T(8,128)(2,1)S(1)}, bf16[256,128]{1,0:T(8,128)(2,1)S(1)}, u32[]{:S(2)}, u32[]{:S(2)}) collective-permute-start(bf16[256,128]{1,0:T(8,128)(2,1)S(1)} %get-tuple-element.53), channel_id=1, source_target_pairs={{0,14},{1,15},{2,0},{3,2},{4,3},{5,4},{6,7},{7,5},{8,6},{9,8},{10,... | collective-permute-start | bytes 196616 | tf_op jit(solution)/shard_map/ppermute | solution.py:770
  10.4 4.6 %collective-permute-start.5 = (bf16[256,128]{1,0:T(8,128)(2,1)S(1)}, bf16[256,128]{1,0:T(8,128)(2,1)S(1)}, u32[]{:S(2)}, u32[]{:S(2)}) collective-permute-start(bf16[256,128]{1,0:T(8,128)(2,1)S(1)} %get-tuple-element.54), channel_id=1, source_target_pairs={{0,2},{1,0},{2,1},{3,5},{4,6},{5,3},{6,4},{7,8},{8,9},{9,7},{10,12... | collective-permute-start | bytes 196616 | tf_op jit(solution)/shard_map/ppermute | solution.py:770
